TPU v7x, 32 devices: a whole 2x2x4 slice. The times are simulated.
32 devices in a mesh: group: 16 (over z, y, core), inner: 2 (over x).
Axes of the slice: x: 2, y: 2, z: 4, core: 2. Of those that a mesh axis runs over, the one named last changes fastest.
Arguments:
- features: bfloat16 [49152, 768], P(('group', 'inner')), may hold values from -6 to 6
- projection: bfloat16 [768, 256], replicated, may hold values from -0.21875 to 0.21875
- adjacency: bfloat16 [49152, 512], P(('group', 'inner'))
- degree: int32 [49152], P(('group', 'inner')), may hold values from 2 to 9
- tile_src: int32 [384, 4], P(('group', 'inner')), may hold values from 0 to 31, as said below
- send_ids: int32 [32, 2, 2], P(('group', 'inner')), may hold values from 0 to 11, as said below
- send_count: int32 [32, 2], P(('group', 'inner')), may hold values from 1 to 2
- edge_ids: int32 [32, 2, 8], P(('group', 'inner')), may hold values from 0 to 11, as said below
- edge_count: int32 [32, 2], P(('group', 'inner')), may hold values from 1 to 8
- train_ids: int32 [32, 2, 64], P(('group', 'inner')), may hold values from 0 to 1535
Outputs:
- train_rows: bfloat16 [4096, 512], P(('group', 'inner'))
Inputs may be any that keep to these rules, and one draw needn't show every extreme that they name: `tile_src`: codes name only live sources: an own block, a live slot of another partition of the same group (never the own inner index), or a live slot of a neighbouring group's partition. `send_ids`: the 2 ids of one list are distinct. `edge_ids`: the 8 ids of one list are distinct.
All inputs are finite; a program needn't handle non-finite values.
Results may differ from a plain program's by a relative error of at most 0.0054.
Values may be sent and summed in bfloat16 or wider, within the bound.
No kernel may reach another device: no remote copies, remote signals or barrier semaphores. Data moves between devices by JAX's collectives and lax.ppermute only.
A program may use at most 64 MiB of HBM per device.

v0:
```python
import jax
import jax.numpy as jnp
from jax import lax
from jax.sharding import PartitionSpec as P

TILE = 128
TPB = 4
CAP = 2
CAPG = 8


def extended(block, sides, width):
    for axis, dim in sides:
        count = lax.axis_size(axis)
        forward = [(i, i + 1) for i in range(count - 1)]
        forward.append((count - 1, 0))
        backward = [(target, source) for source, target in forward]
        low = lax.ppermute(
            lax.slice_in_dim(block, block.shape[dim] - width, None, axis=dim), axis, forward
        )
        high = lax.ppermute(lax.slice_in_dim(block, 0, width, axis=dim), axis, backward)
        block = jnp.concatenate([low, block, high], axis=dim)
    return block


def on_device(
    features,
    projection,
    adjacency,
    degree,
    tile_src,
    send_ids,
    send_count,
    edge_ids,
    edge_count,
    train_ids,
):
    row_count = features.shape[0]
    block_count = row_count // TILE
    out_width = projection.shape[1]
    inv_root = lax.rsqrt(degree.astype(jnp.float32))[:, None]
    product = jnp.dot(features, projection, preferred_element_type=jnp.float32)
    first = (inv_root * product).astype(jnp.bfloat16)
    adj_blocks = adjacency.reshape(block_count, TILE, TPB * TILE)
    sent_ids = send_ids[0]
    sent_live = jnp.arange(CAP)[None, :] < send_count[0][:, None]
    rim_ids = edge_ids[0]
    rim_live = jnp.arange(CAPG)[None, :] < edge_count[0][:, None]
    nothing = jnp.zeros((), jnp.bfloat16)

    def spread(state):
        own_blocks = state.reshape(block_count, TILE, out_width)
        outgoing = jnp.where(sent_live[:, :, None, None], own_blocks[sent_ids], nothing)
        everyone = lax.all_gather(outgoing[None], "inner", axis=0, tiled=True)
        incoming = lax.dynamic_index_in_dim(everyone, lax.axis_index("inner"), 1, keepdims=False)
        rim_rows = jnp.where(rim_live[:, :, None, None], own_blocks[rim_ids], nothing)
        rim_rows = rim_rows.reshape(2 * CAPG, TILE, out_width)
        widened = extended(rim_rows, (("group", 0),), CAPG)
        table = jnp.concatenate(
            [
                own_blocks,
                incoming.reshape(-1, TILE, out_width),
                widened[:CAPG],
                widened[3 * CAPG :],
            ],
            axis=0,
        )
        fetched = table[tile_src].reshape(block_count, TPB * TILE, out_width)
        summed = jnp.einsum("bij,bjk->bik", adj_blocks, fetched, preferred_element_type=jnp.float32)
        return summed.reshape(row_count, out_width)

    hop_one = inv_root * spread(first)
    second = (inv_root * hop_one).astype(jnp.bfloat16)
    hop_two = inv_root * spread(second)
    chosen = train_ids[0]
    leaving = jnp.concatenate([hop_one[chosen], hop_two[chosen]], axis=-1).astype(jnp.bfloat16)
    arrived = lax.all_to_all(leaving, "inner", split_axis=0, concat_axis=0, tiled=True)
    return arrived.reshape(-1, 2 * out_width)


def solution(mesh):
    placed = (
        P(("group", "inner"), None),
        P(),
        P(("group", "inner"), None),
        P(("group", "inner")),
        P(("group", "inner"), None),
        P(("group", "inner"), None, None),
        P(("group", "inner"), None),
        P(("group", "inner"), None, None),
        P(("group", "inner"), None),
        P(("group", "inner"), None, None),
    )
    return jax.shard_map(
        on_device,
        mesh=mesh,
        in_specs=placed,
        out_specs=P(("group", "inner"), None),
        check_vma=False,
    )
```

profile of v0, /device:TPU:0, one launch (start us, length us, event | category | flops | bytes accessed | tf_op | source)
XLA Modules:
  0.0 74.8 jit_solution(14924737370847336479)
XLA Ops:
  0.0 0.0 copy-start
  0.0 0.9 %fusion.3 = (f32[12,128]{1,0:T(8,128)S(1)}, f32[1536]{0:T(1024)S(1)}) fusion(s32[1536]{0:T(1024)} %param.13), kind=kLoop, calls=%fused_computation.39 | loop fusion | flops 1536 | bytes 18432 | tf_op jit(solution)/shard_map/mul | solution.py:72
  0.9 0.7 compare_select_fusion.2
  1.5 0.1 reshape.210
  1.6 0.7 iota_compare_fusion
  2.4 0.0 copy-done
  2.4 1.8 %fusion = bf16[1536,256]{1,0:T(8,128)(2,1)S(1)} fusion(bf16[1536,768]{1,0:T(8,128)(2,1)S(1)} %copy-done, bf16[768,256]{1,0:T(8,128)(2,1)} %param.11, f32[1536]{0:T(1024)S(1)} %get-tuple-element.12), kind=kOutput, calls=%fused_computation.9 | convolution fusion | flops 604766208 | bytes 3545088 | tf_op jit(solution)/shard_map/dot_general | solution.py:42
  4.1 1.6 %gather_fusion.1 = bf16[16,128,256]{2,1,0:T(8,128)(2,1)} fusion(bf16[12,128,256]{2,1,0:T(8,128)(2,1)S(1)} %bitcast.64, s32[1024]{0:T(1024)S(1)} %pad_clamp_fusion.2), kind=kCustom, calls=%fused_computation.1 | custom fusion | bytes 2097216 | tf_op jit(solution)/shard_map/gather | solution.py:56
  5.7 0.0 copy-start.3
  5.7 0.0 copy-start.5
  5.7 0.0 copy-start.2
  5.7 0.0 copy-start.4
  5.8 1.4 %broadcast_select_fusion.1 = bf16[2,8,128,256]{3,2,1,0:T(8,128)(2,1)S(1)} fusion(bf16[2,8,128,256]{3,2,1,0:T(8,128)(2,1)} %bitcast.68, pred[2,8]{1,0:T(4,128)(4,1)S(1)} %iota_compare_fusion), kind=kLoop, calls=%fused_computation.18 | loop fusion | flops 524288 | bytes 2097168 | tf_op jit(solution)/shard_map/jit(_where)/select_n | solution.py:56
  7.2 1.1 %slice_bitcast_fusion.3 = (bf16[8,128,256]{2,1,0:T(8,128)(2,1)}, bf16[8,128,256]{2,1,0:T(8,128)(2,1)}) fusion(bf16[2,8,128,256]{3,2,1,0:T(8,128)(2,1)S(1)} %broadcast_select_fusion.1), kind=kLoop, calls=%fused_computation.22 | loop fusion | bytes 2097152 | tf_op jit(solution)/shard_map/slice | solution.py:19
  8.3 5.4 %collective-permute-start.1 = (bf16[8,128,256]{2,1,0:T(8,128)(2,1)}, bf16[8,128,256]{2,1,0:T(8,128)(2,1)}, u32[]{:S(2)}, u32[]{:S(2)}) collective-permute-start(bf16[8,128,256]{2,1,0:T(8,128)(2,1)} %get-tuple-element.8), channel_id=1, source_target_pairs={{2,0},{4,2},{6,4},{8,6},{10,8},{12,10},{14,12},{16,14},{18,16},{20... | collective-permute-start | bytes 1572872 | tf_op jit(solution)/shard_map/ppermute | solution.py:21
  13.7 0.0 collective-permute-start
  13.7 0.0 copy-done.3
  13.7 0.1 reshape.202
  13.8 0.0 copy-done.5
  13.8 0.1 iota_compare_fusion.1
  13.9 0.0 copy-done.2
  13.9 0.1 copy.15
  14.0 0.1 reshape.218
  14.1 0.0 copy-done.4
  14.1 0.6 gather_fusion
  14.7 0.1 reshape.226
  14.8 0.1 broadcast_select_fusion.3
  14.9 7.0 %all_gather.6 = bf16[2,2,2,128,256]{4,3,2,0,1:T(8,128)(2,1)S(1)} all-gather(bf16[1,2,2,128,256]{4,3,2,0,1:T(8,128)(2,1)S(1)} %broadcast_select_fusion.3), channel_id=1, replica_groups=mesh['group'=16,'inner'=2] {'inner'}, dimensions={0}, use_global_device_ids=true | all-gather | bytes 786432 | tf_op jit(solution)/shard_map/all_gather | solution.py:54
  21.9 0.0 collective-permute-done.1
  21.9 3.4 %collective-permute-done = bf16[8,128,256]{2,1,0:T(8,128)(2,1)} collective-permute-done((bf16[8,128,256]{2,1,0:T(8,128)(2,1)}, bf16[8,128,256]{2,1,0:T(8,128)(2,1)}, u32[]{:S(2)}, u32[]{:S(2)}) %collective-permute-start) | collective-permute-done | bytes 524320 | tf_op jit(solution)/shard_map/ppermute | solution.py:18
  25.3 2.8 %pad_maximum_fusion = bf16[32,128,256]{2,1,0:T(8,128)(2,1)} fusion(bf16[8,128,256]{2,1,0:T(8,128)(2,1)} %collective-permute-done.1, bf16[8,128,256]{2,1,0:T(8,128)(2,1)} %collective-permute-done, bf16[4,128,256]{2,1,0:T(8,128)(2,1)S(1)} %bitcast.70, bf16[12,128,256]{2,1,0:T(8,128)(2,1)S(1)} %bitcast.66), kind=kLoop, calls=%fused_computation.10 | loop fusion | flops 3145728 | bytes 4194304 | tf_op jit(solution)/shard_map/concatenate | solution.py:59
  28.2 4.1 %gather_fusion.2 = bf16[48,128,256]{2,1,0:T(8,128)(2,1)} fusion(bf16[32,128,256]{2,1,0:T(8,128)(2,1)} %pad_maximum_fusion, s32[1024]{0:T(1024)S(1)} %pad_clamp_fusion.1), kind=kCustom, calls=%fused_computation.2 | custom fusion | bytes 6291648 | tf_op jit(solution)/shard_map/gather | solution.py:68
  32.2 4.2 %fusion.2 = (bf16[12,128,256]{2,1,0:T(8,128)(2,1)S(1)}, f32[12,256,128]{1,2,0:T(8,128)}) fusion(f32[12,128]{1,0:T(8,128)S(1)} %get-tuple-element.11, bf16[12,128,512]{2,1,0:T(8,128)(2,1)} %bitcast.62, bf16[12,512,256]{2,1,0:T(8,128)(2,1)} %bitcast.60), kind=kOutput, calls=%fused_computation.16 | convolution fusion | flops 403832832 | bytes 7084032 | tf_op jit(solution)/shard_map/bij,bjk->bik/dot_general | solution.py:69
  36.5 1.6 %gather_fusion.5 = bf16[16,128,256]{2,1,0:T(8,128)(2,1)} fusion(bf16[12,128,256]{2,1,0:T(8,128)(2,1)S(1)} %get-tuple-element.13, s32[1024]{0:T(1024)S(1)} %pad_clamp_fusion.2), kind=kCustom, calls=%fused_computation.5 | custom fusion | bytes 2097216 | tf_op jit(solution)/shard_map/gather | solution.py:56
  38.0 1.4 %broadcast_select_fusion = bf16[2,8,128,256]{3,2,1,0:T(8,128)(2,1)S(1)} fusion(bf16[2,8,128,256]{3,2,1,0:T(8,128)(2,1)} %bitcast.67, pred[2,8]{1,0:T(4,128)(4,1)S(1)} %iota_compare_fusion), kind=kLoop, calls=%fused_computation.17 | loop fusion | flops 524288 | bytes 2097168 | tf_op jit(solution)/shard_map/jit(_where)/select_n | solution.py:56
  39.4 1.1 %slice_bitcast_fusion.1 = (bf16[8,128,256]{2,1,0:T(8,128)(2,1)}, bf16[8,128,256]{2,1,0:T(8,128)(2,1)}) fusion(bf16[2,8,128,256]{3,2,1,0:T(8,128)(2,1)S(1)} %broadcast_select_fusion), kind=kLoop, calls=%fused_computation.20 | loop fusion | bytes 2097152 | tf_op jit(solution)/shard_map/slice | solution.py:19
  40.5 0.3 collective-permute-start.3
  40.8 0.2 collective-permute-start.2
  41.0 0.6 gather_fusion.4
  41.6 0.1 broadcast_select_fusion.2
  41.7 8.9 %all_gather.7 = bf16[2,2,2,128,256]{4,3,2,0,1:T(8,128)(2,1)S(1)} all-gather(bf16[1,2,2,128,256]{4,3,2,0,1:T(8,128)(2,1)S(1)} %broadcast_select_fusion.2), channel_id=1, replica_groups=mesh['group'=16,'inner'=2] {'inner'}, dimensions={0}, use_global_device_ids=true | all-gather | bytes 786432 | tf_op jit(solution)/shard_map/all_gather | solution.py:54
  50.7 0.0 collective-permute-done.3
  50.7 1.9 %collective-permute-done.2 = bf16[8,128,256]{2,1,0:T(8,128)(2,1)} collective-permute-done((bf16[8,128,256]{2,1,0:T(8,128)(2,1)}, bf16[8,128,256]{2,1,0:T(8,128)(2,1)}, u32[]{:S(2)}, u32[]{:S(2)}) %collective-permute-start.2) | collective-permute-done | bytes 524320 | tf_op jit(solution)/shard_map/ppermute | solution.py:18
  52.6 2.8 %pad_maximum_fusion.1 = bf16[32,128,256]{2,1,0:T(8,128)(2,1)} fusion(bf16[8,128,256]{2,1,0:T(8,128)(2,1)} %collective-permute-done.3, bf16[8,128,256]{2,1,0:T(8,128)(2,1)} %collective-permute-done.2, bf16[4,128,256]{2,1,0:T(8,128)(2,1)S(1)} %bitcast.69, bf16[12,128,256]{2,1,0:T(8,128)(2,1)S(1)} %get-tuple-element.13), kind=kLoop, calls=%fused_computation.11 | loop fusion | flops 3145728 | bytes 4194304 | tf_op jit(solution)/shard_map/concatenate | solution.py:59
  55.4 4.1 %gather_fusion.6 = bf16[48,128,256]{2,1,0:T(8,128)(2,1)} fusion(bf16[32,128,256]{2,1,0:T(8,128)(2,1)} %pad_maximum_fusion.1, s32[1024]{0:T(1024)S(1)} %pad_clamp_fusion.1), kind=kCustom, calls=%fused_computation.6 | custom fusion | bytes 6291648 | tf_op jit(solution)/shard_map/gather | solution.py:68
  59.5 0.0 copy-start.1
  59.5 3.1 %fusion.4 = f32[12,256,128]{1,2,0:T(8,128)S(1)} fusion(bf16[12,128,512]{2,1,0:T(8,128)(2,1)} %bitcast.63, bf16[12,512,256]{2,1,0:T(8,128)(2,1)} %bitcast.61), kind=kOutput, calls=%fused_computation.40 | convolution fusion | flops 402653184 | bytes 6291456 | tf_op jit(solution)/shard_map/bij,bjk->bik/dot_general | solution.py:69
  62.5 0.0 copy-done.1
  62.6 1.2 %bitcast_multiply_fusion.1 = (bf16[1536,256]{1,0:T(8,128)(2,1)S(1)}, bf16[1536,256]{1,0:T(8,128)(2,1)}) fusion(f32[12,256,128]{1,2,0:T(8,128)S(1)} %copy-done.1, f32[1536]{0:T(1024)S(1)} %get-tuple-element.12, f32[12,256,128]{1,2,0:T(8,128)S(1)} %fusion.4), kind=kLoop, calls=%fused_computation.13 | loop fusion | flops 1572864 | bytes 4724736 | tf_op jit(solution)/shard_map/mul | solution.py:72
  63.7 2.0 %gather_fusion.7 = bf16[128,256]{1,0:T(8,128)(2,1)S(1)} fusion(bf16[1536,256]{1,0:T(8,128)(2,1)} %get-tuple-element.10, s32[1024]{0:T(1024)S(1)} %pad_clamp_fusion), kind=kCustom, calls=%fused_computation.7 | custom fusion | bytes 131584 | tf_op jit(solution)/shard_map/gather | solution.py:76
  65.7 0.8 %gather_fusion.3 = bf16[128,256]{1,0:T(8,128)(2,1)S(1)} fusion(bf16[1536,256]{1,0:T(8,128)(2,1)S(1)} %get-tuple-element.9, s32[1024]{0:T(1024)S(1)} %pad_clamp_fusion), kind=kCustom, calls=%fused_computation.3 | custom fusion | bytes 131584 | tf_op jit(solution)/shard_map/gather | solution.py:76
  66.6 7.6 %all_to_all.5 = bf16[2,64,512]{2,1,0:T(8,128)(2,1)S(1)} all-to-all(bf16[2,64,512]{2,1,0:T(8,128)(2,1)S(1)} %pad_maximum_fusion.2), channel_id=1, replica_groups=mesh['group'=16,'inner'=2] {'inner'}, dimensions={0} | all-to-all | bytes 262144 | tf_op jit(solution)/shard_map/all_to_all | solution.py:77
  74.2 0.7 copy.18
  (10 shorter events, 0.1 us)
Async XLA Ops:
  0.0 2.4 %copy-start = (bf16[1536,768]{1,0:T(8,128)(2,1)S(1)}, bf16[1536,768]{1,0:T(8,128)(2,1)}, u32[]{:S(2)}) copy-start(bf16[1536,768]{1,0:T(8,128)(2,1)} %param.10) | copy-start | bytes 7077892
  5.7 8.0 %copy-start.3 = (s32[1,2,2]{2,1,0:T(2,128)S(1)}, s32[1,2,2]{2,1,0:T(2,128)}, u32[]{:S(2)}) copy-start(s32[1,2,2]{2,1,0:T(2,128)} %param.15) | copy-start | bytes 52
  5.7 8.1 %copy-start.5 = (s32[1,2]{1,0:T(1,128)S(1)}, s32[1,2]{1,0:T(1,128)}, u32[]{:S(2)}) copy-start(s32[1,2]{1,0:T(1,128)} %param.16) | copy-start | bytes 28
  5.7 8.1 %copy-start.2 = (s32[12,4]{0,1:T(4,128)S(1)}, s32[12,4]{0,1:T(4,128)}, u32[]{:S(2)}) copy-start(s32[12,4]{0,1:T(4,128)} %param.14) | copy-start | bytes 580
  5.7 8.3 %copy-start.4 = (s32[1,2,64]{2,1,0:T(2,128)S(1)}, s32[1,2,64]{2,1,0:T(2,128)}, u32[]{:S(2)}) copy-start(s32[1,2,64]{2,1,0:T(2,128)} %param.19) | copy-start | bytes 1540
  8.3 13.7 %collective-permute-start.1 = (bf16[8,128,256]{2,1,0:T(8,128)(2,1)}, bf16[8,128,256]{2,1,0:T(8,128)(2,1)}, u32[]{:S(2)}, u32[]{:S(2)}) collective-permute-start(bf16[8,128,256]{2,1,0:T(8,128)(2,1)} %get-tuple-element.8), channel_id=1, source_target_pairs={{2,0},{4,2},{6,4},{8,6},{10,8},{12,10},{14,12},{16,14},{18,16},{20... | collective-permute-start | bytes 1572872 | tf_op jit(solution)/shard_map/ppermute | solution.py:21
  13.7 11.6 %collective-permute-start = (bf16[8,128,256]{2,1,0:T(8,128)(2,1)}, bf16[8,128,256]{2,1,0:T(8,128)(2,1)}, u32[]{:S(2)}, u32[]{:S(2)}) collective-permute-start(bf16[8,128,256]{2,1,0:T(8,128)(2,1)} %get-tuple-element.7), channel_id=1, source_target_pairs={{0,2},{2,4},{4,6},{6,8},{8,10},{10,12},{12,14},{14,16},{16,18},{18... | collective-permute-start | bytes 1572872 | tf_op jit(solution)/shard_map/ppermute | solution.py:18
  40.5 10.1 %collective-permute-start.3 = (bf16[8,128,256]{2,1,0:T(8,128)(2,1)}, bf16[8,128,256]{2,1,0:T(8,128)(2,1)}, u32[]{:S(2)}, u32[]{:S(2)}) collective-permute-start(bf16[8,128,256]{2,1,0:T(8,128)(2,1)} %get-tuple-element.6), channel_id=1, source_target_pairs={{2,0},{4,2},{6,4},{8,6},{10,8},{12,10},{14,12},{16,14},{18,16},{20... | collective-permute-start | bytes 1572872 | tf_op jit(solution)/shard_map/ppermute | solution.py:21
  40.8 11.7 %collective-permute-start.2 = (bf16[8,128,256]{2,1,0:T(8,128)(2,1)}, bf16[8,128,256]{2,1,0:T(8,128)(2,1)}, u32[]{:S(2)}, u32[]{:S(2)}) collective-permute-start(bf16[8,128,256]{2,1,0:T(8,128)(2,1)} %get-tuple-element.5), channel_id=1, source_target_pairs={{0,2},{2,4},{4,6},{6,8},{8,10},{10,12},{12,14},{14,16},{16,18},{18... | collective-permute-start | bytes 1572872 | tf_op jit(solution)/shard_map/ppermute | solution.py:18
  59.5 3.1 %copy-start.1 = (f32[12,256,128]{1,2,0:T(8,128)S(1)}, f32[12,256,128]{1,2,0:T(8,128)}, u32[]{:S(2)}) copy-start(f32[12,256,128]{1,2,0:T(8,128)} %get-tuple-element.14) | copy-start | bytes 4718596
where the time goes:
time: 75.3 us; the launch traced here: 74.8 us
  blocking collectives  23.6 us (31%)
  local copies, waits for them, and re-layouts  18.6 us (25%)
  other arithmetic  12.2 us (16%)
  matrix products  9.05 us (12%)
  starting transfers between devices  5.96 us (8%)
  waiting for transfers between devices  5.3 us (7%)
    all_gather x2, blocking collectives, spread(): everyone = lax.all_gather(outgoing[None], 'inner', axis=0, tiled=True)  16 us
    gather x2, local copies, waits for them, and re-layouts, spread(): fetched = table[tile_src].reshape(block_count, TPB * TILE, out_width)  8.15 us
    all_to_all x1, blocking collectives, on_device(): lax.all_to_all(leaving, 'inner', split_axis=0, concat_axis=0, tiled=True)  7.59 us
    dot_general x2, matrix products, spread(): jnp.einsum('bij,bjk->bik', adj_blocks, fetched, preferred_element_type=jn...  7.28 us
    ppermute x2, starting transfers between devices, extended(): lax.ppermute(lax.slice_in_dim(block, 0, width, axis=dim), axis, backward)  5.78 us
    concatenate x2, other arithmetic, spread(): jnp.concatenate([own_blocks, incoming.reshape(-1, TILE, out_width), widen...  5.66 us
    ppermute x2, waiting for transfers between devices, extended(): lax.ppermute(lax.slice_in_dim(block, block.shape[dim] - width, None, axis...  5.29 us
    gather x2, local copies, waits for them, and re-layouts, spread(): own_blocks[rim_ids]  3.19 us
  transfers between devices with their start and end apart: 4, of which 2 were waited for; matrix products, arithmetic and copies ran while one was open for 2% of the time, Pallas kernels for 0%

commit v1 on v0

v1 whole, which is shorter than its diff:
```python
import functools

import jax
import jax.numpy as jnp
from jax import lax
from jax.experimental import pallas as pl
from jax.experimental.pallas import tpu as pltpu
from jax.sharding import PartitionSpec as P

TILE = 128
TPB = 4
CAP = 2
CAPG = 8
BF = jnp.bfloat16
F32 = jnp.float32


META = 16


def ids_row(train_ref):
    owners = train_ref.shape[1]
    return jnp.concatenate([train_ref[0, j : j + 1, :] for j in range(owners)], axis=1)


def as_columns(rows):
    return jnp.transpose(rows)


def one_hot_rows(train_ref, row_count):
    row = ids_row(train_ref)
    count = row.shape[1]
    column = as_columns(jnp.broadcast_to(row.astype(F32), (8, count)))[:, 0:1]
    lanes = lax.broadcasted_iota(jnp.int32, (count, row_count), 1)
    return (lanes == column.astype(jnp.int32)).astype(F32).astype(BF)


def root_columns(degree_ref, scratch):
    count = degree_ref.shape[0]
    scratch[...] = jnp.ones_like(scratch)
    scratch[0:count, :] = degree_ref[...].astype(F32)
    return as_columns(lax.rsqrt(scratch[...]))


def project_kernel(
    tile_src, edge_ids, send_ids, train, degree, projection, features, adjacency,
    first, off, on, *rest,
):
    inner_out, (feat, adj, degs, feat_sems, adj_sem) = rest[:-5], rest[-5:]
    blocks = first.shape[0]
    owners = train.shape[1]
    width = first.shape[2]
    count = owners * train.shape[2]
    parity = lax.rem(lax.axis_index("group"), 2)
    mine = lax.axis_index("inner")
    copies = []
    for b in range(blocks):
        copies.append(
            pltpu.make_async_copy(
                features.at[pl.ds(b * TILE, TILE)], feat.at[pl.ds(b * TILE, TILE)], feat_sems.at[b]
            )
        )
        copies[-1].start()
    adj_copy = pltpu.make_async_copy(adjacency, adj, adj_sem)
    adj_copy.start()
    roots = root_columns(degree, degs)
    weights = projection[...]
    for b in range(blocks):
        copies[b].wait()
        product = jnp.dot(feat[pl.ds(b * TILE, TILE), :], weights, preferred_element_type=F32)
        first[b] = (roots[:, b : b + 1] * product).astype(BF)
    for s in range(CAPG):
        off[pl.ds(s * TILE, TILE), :] = first[edge_ids[0, parity, s]]
        on[pl.ds(s * TILE, TILE), :] = first[edge_ids[0, 1 - parity, s]]
    for k in range(1, owners):
        peer = lax.rem(mine + k, owners)
        for s in range(CAP):
            inner_out[k - 1][pl.ds(s * TILE, TILE), :] = first[send_ids[0, peer, s]]
    row = ids_row(train)
    block_of = lax.div(row, TILE)
    lane_of = lax.rem(row, TILE)
    lane_hot = lax.broadcasted_iota(jnp.int32, (TILE, count), 0) == lane_of
    by_block = jnp.dot(degs[...].astype(BF), lane_hot.astype(F32).astype(BF), preferred_element_type=F32)
    chosen = lax.broadcasted_iota(jnp.int32, by_block.shape, 0) == block_of
    meta = [jnp.sum(jnp.where(chosen, by_block, 0.0), axis=0, keepdims=True)]
    for t in range(TPB):
        codes = jnp.zeros((1, count), F32)
        for b in range(blocks):
            codes = jnp.where(block_of == b, tile_src[b, t].astype(F32), codes)
        meta.insert(t, codes)
    meta.append(jnp.ones((META - TPB - 1, count), F32))
    meta = jnp.concatenate(meta, axis=0)
    if count < width:
        meta = jnp.concatenate([meta, jnp.ones((META, width - count), F32)], axis=1)
    meta = meta.astype(BF)
    hot = one_hot_rows(train, blocks * TILE)
    adj_copy.wait()
    picked = jnp.dot(hot, adj[...], preferred_element_type=F32).astype(BF)
    strips = TPB * TILE // width
    for target, start in [(off, CAPG * TILE), (on, CAPG * TILE)] + [(m, CAP * TILE) for m in inner_out]:
        for h in range(strips):
            target[pl.ds(start + h * count, count), :] = picked[:, h * width : (h + 1) * width]
        target[pl.ds(start + strips * count, META), :] = meta


def expanded(message, start, count, width, base, slots):
    strips = TPB * TILE // width
    columns = as_columns(message[pl.ds(start + strips * count, META), 0:count].astype(F32))
    tiles = []
    for t in range(TPB):
        h, c = divmod(t * TILE, width)
        tiles.append(message[pl.ds(start + h * count, count), c : c + TILE].astype(F32))
    parts = []
    for s in range(slots):
        want = (base + s).astype(F32) if not isinstance(base, int) else float(base + s)
        part = jnp.zeros((count, TILE), F32)
        for t in range(TPB):
            part = part + jnp.where(columns[:, t : t + 1] == want, tiles[t], 0.0)
        parts.append(part.astype(BF))
    return parts, lax.rsqrt(columns[:, TPB : TPB + 1])


def spread_kernel(
    tile_src, edge_ids, send_ids, train, degree, adjacency, first, sent, off, on, *rest,
):
    owners = train.shape[1]
    slots = train.shape[2]
    inner_in = rest[: owners - 1]
    to_off, to_on = rest[owners - 1 : owners + 1]
    stays = rest[owners + 1]
    to_inner = rest[owners + 2 : 2 * owners + 1]
    table, second, hop, degs = rest[2 * owners + 1 :]
    blocks, _, width = first.shape
    count = owners * slots
    parity = lax.rem(lax.axis_index("group"), 2)
    mine = lax.axis_index("inner")
    inner_base = blocks
    group_base = blocks + owners * CAP
    for b in range(blocks):
        table[b] = first[b]
    for s in range(CAPG):
        table[group_base + parity * CAPG + s] = off[pl.ds(s * TILE, TILE), :]
        table[group_base + (1 - parity) * CAPG + s] = on[pl.ds(s * TILE, TILE), :]
    for k in range(1, owners):
        peer = lax.rem(mine - k + owners, owners)
        for s in range(CAP):
            table[inner_base + peer * CAP + s] = inner_in[k - 1][pl.ds(s * TILE, TILE), :]
    roots = root_columns(degree, degs)
    for b in range(blocks):
        fetched = jnp.concatenate([table[tile_src[b, t]] for t in range(TPB)], axis=0)
        total = jnp.dot(adjacency[pl.ds(b * TILE, TILE), :], fetched, preferred_element_type=F32)
        root = roots[:, b : b + 1]
        one = root * total
        hop[pl.ds(b * TILE, TILE), :] = one.astype(BF)
        second[b] = (root * one).astype(BF)

    def partial(message, start, base, ids):
        parts, scale = expanded(message, start, count, width, base, len(ids))
        total = jnp.dot(
            jnp.concatenate(parts, axis=1),
            jnp.concatenate([second[i] for i in ids], axis=0),
            preferred_element_type=F32,
        )
        return (scale * total).astype(BF)

    def spread_out(target, value):
        for j in range(owners):
            target[lax.rem(j - mine + owners, owners)] = value[j * slots : (j + 1) * slots]

    spread_out(
        to_off,
        partial(off, CAPG * TILE, group_base + (1 - parity) * CAPG, [edge_ids[0, parity, s] for s in range(CAPG)]),
    )
    spread_out(
        to_on,
        partial(on, CAPG * TILE, group_base + parity * CAPG, [edge_ids[0, 1 - parity, s] for s in range(CAPG)]),
    )
    own = partial(sent, CAPG * TILE, 0, list(range(blocks)))
    picked = jnp.dot(one_hot_rows(train, blocks * TILE), hop[...], preferred_element_type=F32).astype(BF)
    values = [(mine, own), (owners, picked)]
    for k in range(1, owners):
        peer = lax.rem(mine - k + owners, owners)
        values.append(
            (peer, partial(inner_in[k - 1], CAP * TILE, inner_base + mine * CAP, [send_ids[0, peer, s] for s in range(CAP)]))
        )
    for slot, value in values:
        for k in range(owners):
            target = stays if k == 0 else to_inner[k - 1]
            owner = lax.rem(mine + k, owners)
            piece = value[0:slots]
            for j in range(1, owners):
                piece = jnp.where(owner == j, value[j * slots : (j + 1) * slots].astype(F32), piece.astype(F32)).astype(BF)
            target[slot] = piece


def gather_kernel(owners, *refs):
    stays = refs[0]
    inner = refs[:owners]
    offs = refs[owners : 2 * owners]
    ons = refs[2 * owners : 3 * owners]
    out = refs[-1]
    slots, width = stays.shape[1:]
    mine = lax.axis_index("inner")
    for k in range(owners):
        part = lax.rem(mine - k + owners, owners)
        total = offs[k][...].astype(F32) + ons[k][...].astype(F32)
        for d in range(owners):
            total = total + inner[d][part].astype(F32)
        rows = pl.ds(pl.multiple_of(part * slots, slots), slots)
        out[rows, 0:width] = inner[k][owners]
        out[rows, width : 2 * width] = total.astype(BF)


SMEM = pl.BlockSpec(memory_space=pltpu.SMEM)
VMEM = pl.BlockSpec(memory_space=pltpu.VMEM)
ANY = pl.BlockSpec(memory_space=pl.ANY)


def on_device(groups, owners, features, projection, adjacency, degree, tile_src, send_ids, edge_ids, train_ids):
    row_count, depth = features.shape
    blocks = row_count // TILE
    width = projection.shape[1]
    slots = train_ids.shape[2]
    count = owners * slots
    request = TPB * TILE // width * count + META
    degree = degree.reshape(blocks, TILE)
    params = pltpu.CompilerParams(vmem_limit_bytes=30 * 1024 * 1024)

    across = [(g, (g + (1 if g % 2 else -1)) % groups) for g in range(groups)]
    beside = [(g, g ^ 1) for g in range(groups)]

    def to(pairs, k):
        return [
            (g * owners + i, h * owners + (i + k) % owners) for g, h in pairs for i in range(owners)
        ]

    def send(value, pairs, k=0):
        if k == 0:
            return lax.ppermute(value, "group", pairs)
        return lax.ppermute(value, ("group", "inner"), to(pairs, k))

    def around(value, k):
        return lax.ppermute(value, "inner", [(i, (i + k) % owners) for i in range(owners)])

    group_message = jax.ShapeDtypeStruct((CAPG * TILE + request, width), BF)
    inner_message = jax.ShapeDtypeStruct((CAP * TILE + request, width), BF)
    first, off, on, *inner_out = pl.pallas_call(
        project_kernel,
        out_shape=[jax.ShapeDtypeStruct((blocks, TILE, width), BF), group_message, group_message]
        + [inner_message] * (owners - 1),
        in_specs=[SMEM, SMEM, SMEM, VMEM, VMEM, VMEM, ANY, ANY],
        out_specs=[VMEM] * (3 + owners - 1),
        scratch_shapes=[
            pltpu.VMEM((row_count, depth), BF),
            pltpu.VMEM((row_count, TPB * TILE), BF),
            pltpu.VMEM((16, TILE), F32),
            pltpu.SemaphoreType.DMA((blocks,)),
            pltpu.SemaphoreType.DMA,
        ],
        compiler_params=params,
        name="project",
    )(tile_src, edge_ids, send_ids, train_ids, degree, projection, features, adjacency)

    off_in = send(off, across)
    inner_in = [around(inner_out[k - 1], k) for k in range(1, owners)]
    on_in = send(on, beside)

    piece = jax.ShapeDtypeStruct((owners, slots, width), BF)
    bundle = jax.ShapeDtypeStruct((owners + 1, slots, width), BF)
    to_off, to_on, stays, *to_inner = pl.pallas_call(
        spread_kernel,
        out_shape=[piece, piece] + [bundle] * owners,
        in_specs=[SMEM, SMEM, SMEM] + [VMEM] * (7 + owners - 1),
        out_specs=[VMEM] * (2 + owners),
        scratch_shapes=[
            pltpu.VMEM((blocks + owners * CAP + 2 * CAPG, TILE, width), BF),
            pltpu.VMEM((blocks, TILE, width), BF),
            pltpu.VMEM((row_count, width), BF),
            pltpu.VMEM((16, TILE), F32),
        ],
        compiler_params=params,
        name="spread",
    )(tile_src, edge_ids, send_ids, train_ids, degree, adjacency, first, on, off_in, on_in, *inner_in)

    offs = [send(to_off[k], across, k) for k in range(owners)]
    inner = [stays] + [around(to_inner[k - 1], k) for k in range(1, owners)]
    ons = [send(to_on[k], beside, k) for k in range(owners)]
    return pl.pallas_call(
        functools.partial(gather_kernel, owners),
        out_shape=jax.ShapeDtypeStruct((count, 2 * width), BF),
        in_specs=[VMEM] * (3 * owners),
        out_specs=VMEM,
        compiler_params=params,
        name="gather",
    )(*inner, *offs, *ons)


def solution(mesh):
    both = ("group", "inner")

    def run(
        features, projection, adjacency, degree, tile_src, send_ids, send_count, edge_ids, edge_count, train_ids
    ):
        return on_device(
            mesh.shape["group"], mesh.shape["inner"],
            features, projection, adjacency, degree, tile_src, send_ids, edge_ids, train_ids,
        )

    placed = (
        P(both, None),
        P(),
        P(both, None),
        P(both),
        P(both, None),
        P(both, None, None),
        P(both, None),
        P(both, None, None),
        P(both, None),
        P(both, None, None),
    )
    return jax.shard_map(run, mesh=mesh, in_specs=placed, out_specs=P(both, None), check_vma=False)
```

time: 75.3 us -> 46.9 us (0.62)
  blocking collectives: 23.6 us -> 0 us
  Pallas kernels: 0 us -> 12.7 us
  other arithmetic: 12.2 us -> 0 us
  local copies, waits for them, and re-layouts: 18.6 us -> 7.58 us
  starting transfers between devices: 5.96 us -> 15.3 us
  matrix products: 9.05 us -> 0 us
  waiting for transfers between devices: 5.3 us -> 10.9 us
    all_gather x2 -> x0, blocking collectives: 16 us -> none  [spread(): everyone = lax.all_gather(outgoing[None], 'inner', axis=0, tiled=True)]
    gather x8 -> x0, local copies, waits for them, and re-layouts: 15.3 us -> none  [the longest x2 8.15 us: spread(): fetched = table[tile_src].reshape(block_count, TPB * TILE, out_width)]
    pallas_call x0 -> x3, Pallas kernels: none -> 12.7 us  [the longest x1 7.66 us: on_device(): pl.pallas_call(project_kernel, out_shape=[jax.ShapeDtypeStruct((blocks, T...]
    ppermute x4 -> x8, starting transfers between devices: 5.96 us -> 15.3 us  [the longest x2 7.31 us: send(): return lax.ppermute(value, ('group', 'inner'), to(pairs, k))]
    dot_general x3 -> x0, matrix products: 9.05 us -> none  [the longest x2 7.28 us: spread(): jnp.einsum('bij,bjk->bik', adj_blocks, fetched, preferred_element_type=jn...]
    all_to_all x1 -> x0, blocking collectives: 7.59 us -> none  [on_device(): lax.all_to_all(leaving, 'inner', split_axis=0, concat_axis=0, tiled=True)]
    unnamed x13 -> x17, local copies, waits for them, and re-layouts: 0.68 us -> 7.57 us
    concatenate x3 -> x0, other arithmetic: 5.67 us -> none  [the longest x2 5.66 us: spread(): jnp.concatenate([own_blocks, incoming.reshape(-1, TILE, out_width), widen...]
  transfers between devices with their start and end apart: 4 -> 8, of which waited for: 2 -> 3; matrix products, arithmetic and copies ran while one was open for 2% -> 0% of each run, Pallas kernels for 0% -> 0%
where the time goes in v1:
time: 46.9 us; the launch traced here: 46.6 us
  starting transfers between devices  15.3 us (33%)
  Pallas kernels  12.7 us (27%)
  waiting for transfers between devices  10.9 us (23%)
  local copies, waits for them, and re-layouts  7.58 us (16%)
    pallas_call x1, Pallas kernels, on_device(): pl.pallas_call(project_kernel, out_shape=[jax.ShapeDtypeStruct((blocks, T...  7.66 us
    unnamed x17, local copies, waits for them, and re-layouts  7.57 us
    ppermute x2, waiting for transfers between devices, around(): lax.ppermute(value, 'inner', [(i, (i + k) % owners) for i in range(owners)])  7.41 us
    ppermute x2, starting transfers between devices, send(): return lax.ppermute(value, ('group', 'inner'), to(pairs, k))  7.31 us
    ppermute x4, starting transfers between devices, send(): return lax.ppermute(value, 'group', pairs)  5.97 us
    pallas_call x1, Pallas kernels, on_device(): pl.pallas_call(spread_kernel, out_shape=[piece, piece] + [bundle] * owner...  4.38 us
    ppermute x4, waiting for transfers between devices, send(): return lax.ppermute(value, 'group', pairs)  2.72 us
    ppermute x2, starting transfers between devices, around(): lax.ppermute(value, 'inner', [(i, (i + k) % owners) for i in range(owners)])  2.02 us
  transfers between devices with their start and end apart: 8, of which 3 were waited for; matrix products, arithmetic and copies ran while one was open for 0% of the time, Pallas kernels for 0%

profile of v1, /device:TPU:0, one launch (start us, length us, event | category | flops | bytes accessed | tf_op | source)
XLA Modules:
  0.0 46.6 jit_solution(110118148266097649)
XLA Ops:
  0.0 0.8 %copy.10.tile_src = s32[12,4]{1,0:T(8,128)S(1)} copy(s32[12,4]{0,1:T(4,128)} %param.14) | data formatting | bytes 384 | tf_op args[4]
  0.8 0.0 copy-start
  0.8 1.4 %copy-done = bf16[1536,512]{1,0:T(8,128)(2,1)S(1)} copy-done((bf16[1536,512]{1,0:T(8,128)(2,1)S(1)}, bf16[1536,512]{1,0:T(8,128)(2,1)}, u32[]{:S(2)}) %copy-start) | copy-done | bytes 1572888
  2.2 0.0 copy-start.2
  2.2 1.7 %copy-done.2 = bf16[1536,768]{1,0:T(8,128)(2,1)S(1)} copy-done((bf16[1536,768]{1,0:T(8,128)(2,1)S(1)}, bf16[1536,768]{1,0:T(8,128)(2,1)}, u32[]{:S(2)}) %copy-start.2) | copy-done | bytes 2359320
  3.8 0.0 copy-start.3
  3.8 1.0 %copy-done.3 = bf16[768,256]{1,0:T(8,128)(2,1)S(1)} copy-done((bf16[768,256]{1,0:T(8,128)(2,1)S(1)}, bf16[768,256]{1,0:T(8,128)(2,1)}, u32[]{:S(2)}) %copy-start.3) | copy-done | bytes 393240
  4.8 0.0 copy-start.4
  4.8 0.7 %copy-done.4 = s32[1536]{0:T(1024)S(1)} copy-done((s32[1536]{0:T(1024)S(1)}, s32[1536]{0:T(1024)}, u32[]{:S(2)}) %copy-start.4) | copy-done | bytes 6168
  5.5 0.0 copy-start.5
  5.5 0.7 %copy-done.5 = s32[1,2,8]{2,1,0:T(2,128)S(1)} copy-done((s32[1,2,8]{2,1,0:T(2,128)S(1)}, s32[1,2,8]{2,1,0:T(2,128)}, u32[]{:S(2)}) %copy-start.5) | copy-done | bytes 88
  6.2 0.0 copy-start.6
  6.2 0.7 %copy-done.6 = s32[1,2,2]{2,1,0:T(2,128)S(1)} copy-done((s32[1,2,2]{2,1,0:T(2,128)S(1)}, s32[1,2,2]{2,1,0:T(2,128)}, u32[]{:S(2)}) %copy-start.6) | copy-done | bytes 40
  6.9 0.0 copy-start.7
  6.9 0.7 %copy-done.7 = s32[1,2,64]{2,1,0:T(2,128)S(1)} copy-done((s32[1,2,64]{2,1,0:T(2,128)S(1)}, s32[1,2,64]{2,1,0:T(2,128)}, u32[]{:S(2)}) %copy-start.7) | copy-done | bytes 536
  7.6 0.0 copy-start.1
  7.6 7.7 %project.1 = (bf16[12,128,256]{2,1,0:T(8,128)(2,1)S(1)}, bf16[1296,256]{1,0:T(8,128)(2,1)S(1)}, bf16[1296,256]{1,0:T(8,128)(2,1)S(1)}, bf16[528,256]{1,0:T(8,128)(2,1)S(1)}) custom-call(s32[12,4]{1,0:T(8,128)S(1)} %copy.10.tile_src, s32[1,2,8]{2,1,0:T(2,128)S(1)} %copy-done.5, s32[1,2,2]{2,1,0:T(2,128)S(1)} %copy-done.6, s32[1,2,64]{2,1,0:T(2,128)S(1)} %copy-done.7, ...), custom_call_target="tpu_custom_call" | custom-call | tf_op jit(solution)/shard_map/project/pallas_call | solution.py:247
  15.2 5.5 %collective-permute-start = (bf16[1296,256]{1,0:T(8,128)(2,1)S(1)}, bf16[1296,256]{1,0:T(8,128)(2,1)S(1)}, u32[]{:S(2)}, u32[]{:S(2)}) collective-permute-start(bf16[1296,256]{1,0:T(8,128)(2,1)S(1)} %get-tuple-element.15), channel_id=1, source_target_pairs={{0,30},{2,4},{4,2},{6,8},{8,6},{10,12},{12,10},{14,16},{16,14},{18... | collective-permute-start | bytes 1990664 | tf_op jit(solution)/shard_map/ppermute | solution.py:239
  20.8 0.0 collective-permute-start.1
  20.8 1.5 %collective-permute-start.2 = (bf16[528,256]{1,0:T(8,128)(2,1)S(1)}, bf16[528,256]{1,0:T(8,128)(2,1)S(1)}, u32[]{:S(2)}, u32[]{:S(2)}) collective-permute-start(bf16[528,256]{1,0:T(8,128)(2,1)S(1)} %get-tuple-element.16), channel_id=1, source_target_pairs={{0,1},{1,0},{2,3},{3,2},{4,5},{5,4},{6,7},{7,6},{8,9},{9,8},{10,11... | collective-permute-start | bytes 811016 | tf_op jit(solution)/shard_map/ppermute | solution.py:243
  22.3 7.4 %collective-permute-done.2.rest_0_ = bf16[528,256]{1,0:T(8,128)(2,1)S(1)} collective-permute-done((bf16[528,256]{1,0:T(8,128)(2,1)S(1)}, bf16[528,256]{1,0:T(8,128)(2,1)S(1)}, u32[]{:S(2)}, u32[]{:S(2)}) %collective-permute-start.2) | collective-permute-done | bytes 270368 | tf_op jit(solution)/shard_map/ppermute | solution.py:243
  29.7 0.0 collective-permute-done.off
  29.7 0.0 collective-permute-done.1.on
  29.7 0.0 copy-done.1
  29.7 4.4 %spread.1 = (bf16[2,64,256]{2,1,0:T(8,128)(2,1)S(1)}, bf16[2,64,256]{2,1,0:T(8,128)(2,1)S(1)}, bf16[3,64,256]{2,1,0:T(8,128)(2,1)S(1)}, bf16[3,64,256]{2,1,0:T(8,128)(2,1)S(1)}) custom-call(s32[12,4]{1,0:T(8,128)S(1)} %copy.10.tile_src, s32[1,2,8]{2,1,0:T(2,128)S(1)} %copy-done.5, s32[1,2,2]{2,1,0:T(2,128)S(1)} %copy-done.6, s32[1,2,64]{2,1,0:T(2,128)S(1)} %copy-done.7, ...), custom_call_target="tpu_custom_call" | custom-call | tf_op jit(solution)/shard_map/spread/pallas_call | solution.py:270
  34.1 5.0 %collective-permute-start.5 = (bf16[64,256]{1,0:T(8,128)(2,1)S(1)}, bf16[64,256]{1,0:T(8,128)(2,1)S(1)}, u32[]{:S(2)}, u32[]{:S(2)}) collective-permute-start(bf16[64,256]{1,0:T(8,128)(2,1)S(1)} %get-tuple-element.23), channel_id=1, source_target_pairs={{0,31},{1,30},{2,5},{3,4},{4,3},{5,2},{6,9},{7,8},{8,7},{9,6},{10,... | collective-permute-start | bytes 98312 | tf_op jit(solution)/shard_map/ppermute | solution.py:240
  39.1 0.5 collective-permute-start.4
  39.5 0.5 %collective-permute-start.3 = (bf16[3,64,256]{2,1,0:T(8,128)(2,1)S(1)}, bf16[3,64,256]{2,1,0:T(8,128)(2,1)S(1)}, u32[]{:S(2)}, u32[]{:S(2)}) collective-permute-start(bf16[3,64,256]{2,1,0:T(8,128)(2,1)S(1)} %get-tuple-element.18), channel_id=1, source_target_pairs={{0,1},{1,0},{2,3},{3,2},{4,5},{5,4},{6,7},{7,6},{8,9},{9,8},{10,11... | collective-permute-start | bytes 294920 | tf_op jit(solution)/shard_map/ppermute | solution.py:243
  40.1 2.3 %collective-permute-start.7 = (bf16[64,256]{1,0:T(8,128)(2,1)S(1)}, bf16[64,256]{1,0:T(8,128)(2,1)S(1)}, u32[]{:S(2)}, u32[]{:S(2)}) collective-permute-start(bf16[64,256]{1,0:T(8,128)(2,1)S(1)} %get-tuple-element.21), channel_id=1, source_target_pairs={{0,3},{1,2},{2,1},{3,0},{4,7},{5,6},{6,5},{7,4},{8,11},{9,10},{10,... | collective-permute-start | bytes 98312 | tf_op jit(solution)/shard_map/ppermute | solution.py:240
  42.4 0.0 collective-permute-start.6
  42.4 0.0 collective-permute-done.5.refs_3_
  42.4 2.7 %collective-permute-done.4.refs_2_ = bf16[64,256]{1,0:T(8,128)(2,1)S(1)} collective-permute-done((bf16[64,256]{1,0:T(8,128)(2,1)S(1)}, bf16[64,256]{1,0:T(8,128)(2,1)S(1)}, u32[]{:S(2)}, u32[]{:S(2)}) %collective-permute-start.4) | collective-permute-done | bytes 32800 | tf_op jit(solution)/shard_map/ppermute | solution.py:239
  45.1 0.8 %collective-permute-done.7.refs_5_ = bf16[64,256]{1,0:T(8,128)(2,1)S(1)} collective-permute-done((bf16[64,256]{1,0:T(8,128)(2,1)S(1)}, bf16[64,256]{1,0:T(8,128)(2,1)S(1)}, u32[]{:S(2)}, u32[]{:S(2)}) %collective-permute-start.7) | collective-permute-done | bytes 32800 | tf_op jit(solution)/shard_map/ppermute | solution.py:240
  45.9 0.0 collective-permute-done.6.refs_4_
  45.9 0.0 collective-permute-done.3.refs_1_
  45.9 0.7 %gather.1 = bf16[128,512]{1,0:T(8,128)(2,1)} custom-call(bf16[3,64,256]{2,1,0:T(8,128)(2,1)S(1)} %get-tuple-element.17.refs_0_, bf16[3,64,256]{2,1,0:T(8,128)(2,1)S(1)} %collective-permute-done.3.refs_1_, bf16[64,256]{1,0:T(8,128)(2,1)S(1)} %collective-permute-done.4.refs_2_, bf16[64,256]{1,0:T(8,128)(2,1)S(1)} %collective-permute-done.5.refs_3_, ...), custom_call_target="tpu_custom_call" | custom-call | tf_op jit(solution)/shard_map/gather/pallas_call | solution.py:288
  (2 shorter events, 0.0 us)
Async XLA Ops:
  0.8 1.4 %copy-start = (bf16[1536,512]{1,0:T(8,128)(2,1)S(1)}, bf16[1536,512]{1,0:T(8,128)(2,1)}, u32[]{:S(2)}) copy-start(bf16[1536,512]{1,0:T(8,128)(2,1)} %adjacency.3) | copy-start | bytes 4718596
  2.2 1.7 %copy-start.2 = (bf16[1536,768]{1,0:T(8,128)(2,1)S(1)}, bf16[1536,768]{1,0:T(8,128)(2,1)}, u32[]{:S(2)}) copy-start(bf16[1536,768]{1,0:T(8,128)(2,1)} %features.1) | copy-start | bytes 7077892
  3.8 1.0 %copy-start.3 = (bf16[768,256]{1,0:T(8,128)(2,1)S(1)}, bf16[768,256]{1,0:T(8,128)(2,1)}, u32[]{:S(2)}) copy-start(bf16[768,256]{1,0:T(8,128)(2,1)} %projection.1) | copy-start | bytes 1179652
  4.8 0.7 %copy-start.4 = (s32[1536]{0:T(1024)S(1)}, s32[1536]{0:T(1024)}, u32[]{:S(2)}) copy-start(s32[1536]{0:T(1024)} %param.13) | copy-start | bytes 18436
  5.5 0.7 %copy-start.5 = (s32[1,2,8]{2,1,0:T(2,128)S(1)}, s32[1,2,8]{2,1,0:T(2,128)}, u32[]{:S(2)}) copy-start(s32[1,2,8]{2,1,0:T(2,128)} %edge_ids.3) | copy-start | bytes 196
  6.2 0.7 %copy-start.6 = (s32[1,2,2]{2,1,0:T(2,128)S(1)}, s32[1,2,2]{2,1,0:T(2,128)}, u32[]{:S(2)}) copy-start(s32[1,2,2]{2,1,0:T(2,128)} %send_ids.3) | copy-start | bytes 52
  6.9 0.7 %copy-start.7 = (s32[1,2,64]{2,1,0:T(2,128)S(1)}, s32[1,2,64]{2,1,0:T(2,128)}, u32[]{:S(2)}) copy-start(s32[1,2,64]{2,1,0:T(2,128)} %train.3) | copy-start | bytes 1540
  7.6 22.1 %copy-start.1 = (bf16[1536,512]{1,0:T(8,128)(2,1)S(1)}, bf16[1536,512]{1,0:T(8,128)(2,1)}, u32[]{:S(2)}) copy-start(bf16[1536,512]{1,0:T(8,128)(2,1)} %adjacency.3) | copy-start | bytes 4718596
  15.2 14.4 %collective-permute-start = (bf16[1296,256]{1,0:T(8,128)(2,1)S(1)}, bf16[1296,256]{1,0:T(8,128)(2,1)S(1)}, u32[]{:S(2)}, u32[]{:S(2)}) collective-permute-start(bf16[1296,256]{1,0:T(8,128)(2,1)S(1)} %get-tuple-element.15), channel_id=1, source_target_pairs={{0,30},{2,4},{4,2},{6,8},{8,6},{10,12},{12,10},{14,16},{16,14},{18... | collective-permute-start | bytes 1990664 | tf_op jit(solution)/shard_map/ppermute | solution.py:239
  20.8 8.9 %collective-permute-start.1 = (bf16[1296,256]{1,0:T(8,128)(2,1)S(1)}, bf16[1296,256]{1,0:T(8,128)(2,1)S(1)}, u32[]{:S(2)}, u32[]{:S(2)}) collective-permute-start(bf16[1296,256]{1,0:T(8,128)(2,1)S(1)} %get-tuple-element.14.sent), channel_id=1, source_target_pairs={{0,2},{2,0},{4,6},{6,4},{8,10},{10,8},{12,14},{14,12},{16,18},{18,... | collective-permute-start | bytes 1990664 | tf_op jit(solution)/shard_map/ppermute | solution.py:239
  20.8 8.9 %collective-permute-start.2 = (bf16[528,256]{1,0:T(8,128)(2,1)S(1)}, bf16[528,256]{1,0:T(8,128)(2,1)S(1)}, u32[]{:S(2)}, u32[]{:S(2)}) collective-permute-start(bf16[528,256]{1,0:T(8,128)(2,1)S(1)} %get-tuple-element.16), channel_id=1, source_target_pairs={{0,1},{1,0},{2,3},{3,2},{4,5},{5,4},{6,7},{7,6},{8,9},{9,8},{10,11... | collective-permute-start | bytes 811016 | tf_op jit(solution)/shard_map/ppermute | solution.py:243
  34.1 8.3 %collective-permute-start.5 = (bf16[64,256]{1,0:T(8,128)(2,1)S(1)}, bf16[64,256]{1,0:T(8,128)(2,1)S(1)}, u32[]{:S(2)}, u32[]{:S(2)}) collective-permute-start(bf16[64,256]{1,0:T(8,128)(2,1)S(1)} %get-tuple-element.23), channel_id=1, source_target_pairs={{0,31},{1,30},{2,5},{3,4},{4,3},{5,2},{6,9},{7,8},{8,7},{9,6},{10,... | collective-permute-start | bytes 98312 | tf_op jit(solution)/shard_map/ppermute | solution.py:240
  39.1 6.0 %collective-permute-start.4 = (bf16[64,256]{1,0:T(8,128)(2,1)S(1)}, bf16[64,256]{1,0:T(8,128)(2,1)S(1)}, u32[]{:S(2)}, u32[]{:S(2)}) collective-permute-start(bf16[64,256]{1,0:T(8,128)(2,1)S(1)} %get-tuple-element.24), channel_id=1, source_target_pairs={{0,30},{2,4},{4,2},{6,8},{8,6},{10,12},{12,10},{14,16},{16,14},{18... | collective-permute-start | bytes 98312 | tf_op jit(solution)/shard_map/ppermute | solution.py:239
  39.5 6.4 %collective-permute-start.3 = (bf16[3,64,256]{2,1,0:T(8,128)(2,1)S(1)}, bf16[3,64,256]{2,1,0:T(8,128)(2,1)S(1)}, u32[]{:S(2)}, u32[]{:S(2)}) collective-permute-start(bf16[3,64,256]{2,1,0:T(8,128)(2,1)S(1)} %get-tuple-element.18), channel_id=1, source_target_pairs={{0,1},{1,0},{2,3},{3,2},{4,5},{5,4},{6,7},{7,6},{8,9},{9,8},{10,11... | collective-permute-start | bytes 294920 | tf_op jit(solution)/shard_map/ppermute | solution.py:243
  40.1 5.8 %collective-permute-start.7 = (bf16[64,256]{1,0:T(8,128)(2,1)S(1)}, bf16[64,256]{1,0:T(8,128)(2,1)S(1)}, u32[]{:S(2)}, u32[]{:S(2)}) collective-permute-start(bf16[64,256]{1,0:T(8,128)(2,1)S(1)} %get-tuple-element.21), channel_id=1, source_target_pairs={{0,3},{1,2},{2,1},{3,0},{4,7},{5,6},{6,5},{7,4},{8,11},{9,10},{10,... | collective-permute-start | bytes 98312 | tf_op jit(solution)/shard_map/ppermute | solution.py:240
  42.4 3.5 %collective-permute-start.6 = (bf16[64,256]{1,0:T(8,128)(2,1)S(1)}, bf16[64,256]{1,0:T(8,128)(2,1)S(1)}, u32[]{:S(2)}, u32[]{:S(2)}) collective-permute-start(bf16[64,256]{1,0:T(8,128)(2,1)S(1)} %get-tuple-element.22), channel_id=1, source_target_pairs={{0,2},{2,0},{4,6},{6,4},{8,10},{10,8},{12,14},{14,12},{16,18},{18,... | collective-permute-start | bytes 98312 | tf_op jit(solution)/shard_map/ppermute | solution.py:239

commit v2 on v0

v2 whole, which is shorter than its diff:
```python
import functools

import jax
import jax.numpy as jnp
from jax import lax
from jax.experimental import pallas as pl
from jax.experimental.pallas import tpu as pltpu
from jax.sharding import PartitionSpec as P

TILE = 128
TPB = 4
CAP = 2
CAPG = 8
BF = jnp.bfloat16
F32 = jnp.float32
CHUNKS = 4


META = 16


def ids_row(train):
    owners = train.shape[1]
    return jnp.concatenate([train[0, j : j + 1, :] for j in range(owners)], axis=1)


def as_columns(rows):
    return jnp.transpose(rows)


def one_hot_rows(train, row_count):
    row = ids_row(train)
    count = row.shape[1]
    column = as_columns(jnp.broadcast_to(row.astype(F32), (8, count)))[:, 0:1]
    lanes = lax.broadcasted_iota(jnp.int32, (count, row_count), 1)
    return (lanes == column.astype(jnp.int32)).astype(F32).astype(BF)


def fetch(pairs, sems):
    copies = [pltpu.make_async_copy(source, target, sems.at[n]) for n, (source, target) in enumerate(pairs)]
    for copy in copies:
        copy.start()
    return copies


def project_kernel(
    tile_src, edge_ids, send_ids, train, degree, projection, features, adjacency,
    first, request, off, on, *rest,
):
    inner_out = rest[:-13]
    src_s, edge_s, send_s, train_v, deg_v, weights, feat, adj, blocks_v, request_v, sems, sent, block_sent = rest[-13:]
    blocks = first.shape[0]
    owners = train.shape[1]
    width = first.shape[2]
    count = owners * train.shape[2]
    parity = lax.rem(lax.axis_index("group"), 2)
    mine = lax.axis_index("inner")
    step = blocks // CHUNKS
    rows = [pl.ds(n * step * TILE, step * TILE) for n in range(CHUNKS)]
    small = fetch(
        [(train, train_v), (tile_src, src_s), (degree, deg_v.at[pl.ds(0, blocks)]), (edge_ids, edge_s), (send_ids, send_s)]
        + [(adjacency, adj), (projection, weights)]
        + [(features.at[r], feat.at[r]) for r in rows],
        sems,
    )
    deg_v[pl.ds(blocks, 16 - blocks), :] = jnp.ones((16 - blocks, TILE), jnp.int32)
    for copy in small[:5]:
        copy.wait()
    degrees = deg_v[...].astype(F32)
    roots = as_columns(lax.rsqrt(degrees))
    row = ids_row(train_v)
    block_of = lax.div(row, TILE)
    lane_of = lax.rem(row, TILE)
    lane_hot = lax.broadcasted_iota(jnp.int32, (TILE, count), 0) == lane_of
    by_block = jnp.dot(degrees.astype(BF), lane_hot.astype(F32).astype(BF), preferred_element_type=F32)
    chosen = lax.broadcasted_iota(jnp.int32, by_block.shape, 0) == block_of
    meta = []
    for t in range(TPB):
        codes = jnp.zeros((1, count), F32)
        for b in range(blocks):
            codes = jnp.where(block_of == b, src_s[t, b].astype(F32), codes)
        meta.append(codes)
    meta.append(jnp.sum(jnp.where(chosen, by_block, 0.0), axis=0, keepdims=True))
    meta.append(jnp.ones((META - TPB - 1, count), F32))
    meta = jnp.concatenate(meta, axis=0)
    if count < width:
        meta = jnp.concatenate([meta, jnp.ones((META, width - count), F32)], axis=1)
    strips = TPB * TILE // width
    request_v[pl.ds(strips * count, META), :] = meta.astype(BF)
    hot = one_hot_rows(train_v, blocks * TILE)
    small[5].wait()
    picked = jnp.dot(hot, adj[...], preferred_element_type=F32).astype(BF)
    for h in range(strips):
        request_v[pl.ds(h * count, count), :] = picked[:, h * width : (h + 1) * width]
    tail = request_v.shape[0]
    places = [off.at[pl.ds(CAPG * TILE, tail)]]
    places += [m.at[pl.ds(CAP * TILE, tail)] for m in inner_out]
    places += [on.at[pl.ds(CAPG * TILE, tail)], request]
    leaving = [pltpu.make_async_copy(request_v, place, sent.at[n]) for n, place in enumerate(places)]
    for copy in leaving:
        copy.start()
    offers = [(edge_s[0, parity, s], off, s) for s in range(CAPG)]
    for k in range(1, owners):
        peer = lax.rem(mine + k, owners)
        offers += [(send_s[0, peer, s], inner_out[k - 1], s) for s in range(CAP)]
    offers += [(edge_s[0, 1 - parity, s], on, s) for s in range(CAPG)]
    copies = [
        pltpu.make_async_copy(
            blocks_v.at[block], target.at[pl.ds(s * TILE, TILE)], sent.at[len(leaving) + n]
        )
        for n, (block, target, s) in enumerate(offers)
    ]
    small[6].wait()
    for n in range(CHUNKS):
        small[7 + n].wait()
        product = jnp.dot(feat[rows[n], :], weights[...], preferred_element_type=F32)
        for k in range(step):
            b = n * step + k
            blocks_v[b] = (roots[:, b : b + 1] * product[k * TILE : (k + 1) * TILE]).astype(BF)
        for copy, (block, _, _) in zip(copies, offers):
            pl.when(lax.div(block, step) == n)(copy.start)
        chunk = pl.ds(n * step, step)
        leaving.append(pltpu.make_async_copy(blocks_v.at[chunk], first.at[chunk], block_sent.at[n]))
        leaving[-1].start()
    for copy in copies + leaving:
        copy.wait()


def request_columns(message, start, count, width):
    strips = TPB * TILE // width
    return as_columns(message[pl.ds(start + strips * count, META), 0:count].astype(F32))


def expanded(message, start, count, width, wanted):
    columns = request_columns(message, start, count, width)
    tiles = []
    for t in range(TPB):
        h, c = divmod(t * TILE, width)
        tiles.append(message[pl.ds(start + h * count, count), c : c + TILE].astype(F32))
    parts = []
    for want in wanted:
        part = jnp.zeros((count, TILE), F32)
        for t in range(TPB):
            part = part + jnp.where(columns[:, t : t + 1] == want, tiles[t], 0.0)
        parts.append(part.astype(BF))
    return parts


def near_kernel(
    tile_src, edge_ids, send_ids, train, degree, first, adjacency, request, on, *rest,
):
    owners = train.shape[1]
    inner_in = rest[: owners - 1]
    sums, far, wide, hot, roots = rest[owners - 1 : owners + 4]
    src_s, edge_s, send_s, train_v, deg_v, table, sems = rest[owners + 4 :]
    blocks, _, width = first.shape
    count = owners * train.shape[2]
    parity = lax.rem(lax.axis_index("group"), 2)
    mine = lax.axis_index("inner")
    inner_base = blocks
    group_base = blocks + owners * CAP
    off_base = group_base + parity * CAPG
    on_base = group_base + (1 - parity) * CAPG
    small = fetch(
        [(train, train_v), (tile_src, src_s), (degree, deg_v.at[pl.ds(0, blocks)]), (edge_ids, edge_s), (send_ids, send_s)]
        + [(first, table.at[pl.ds(0, blocks)])],
        sems,
    )
    deg_v[pl.ds(blocks, 16 - blocks), :] = jnp.ones((16 - blocks, TILE), jnp.int32)
    far[...] = jnp.zeros_like(far)
    wide[...] = jnp.zeros_like(wide)
    for s in range(CAPG):
        table[off_base + s] = jnp.zeros((TILE, width), BF)
        table[on_base + s] = on[pl.ds(s * TILE, TILE), :]
    for s in range(CAP):
        table[inner_base + mine * CAP + s] = jnp.zeros((TILE, width), BF)
        for k in range(1, owners):
            peer = lax.rem(mine - k + owners, owners)
            table[inner_base + peer * CAP + s] = inner_in[k - 1][pl.ds(s * TILE, TILE), :]
    for copy in small:
        copy.wait()
    roots[...] = as_columns(lax.rsqrt(deg_v[...].astype(F32)))
    for b in range(blocks):
        fetched = jnp.concatenate([table[src_s[t, b]] for t in range(TPB)], axis=0)
        sums[pl.ds(b * TILE, TILE), :] = jnp.dot(
            adjacency[pl.ds(b * TILE, TILE), :], fetched, preferred_element_type=F32
        )
    for b in range(blocks):
        for t in range(TPB):
            slot = src_s[t, b] - off_base

            @pl.when(jnp.logical_and(slot >= 0, slot < CAPG))
            def _():
                place = (pl.ds(b * TILE, TILE), pl.ds(pl.multiple_of(slot * TILE, TILE), TILE))
                far[place] += adjacency[pl.ds(b * TILE, TILE), t * TILE : (t + 1) * TILE]

    parts = expanded(request, 0, count, width, [float(b) for b in range(blocks)])
    for b in range(blocks):
        wide[pl.ds(0, count), b * TILE : (b + 1) * TILE] = parts[b]
    asked = [(on, CAPG, off_base, lambda s: edge_s[0, 1 - parity, s])]
    for k in range(1, owners):
        peer = lax.rem(mine - k + owners, owners)
        asked.append((inner_in[k - 1], CAP, inner_base + mine * CAP, lambda s, peer=peer: send_s[0, peer, s]))
    for n, (message, slots, base, block) in enumerate(asked):
        parts = expanded(message, slots * TILE, count, width, [(base + s).astype(F32) for s in range(slots)])
        for s in range(slots):
            column = pl.multiple_of(block(s) * TILE, TILE)
            wide[pl.ds((n + 1) * count, count), pl.ds(column, TILE)] = parts[s]
    hot[...] = one_hot_rows(train_v, blocks * TILE)


def spread_kernel(edge_ids, off, request, on, *rest):
    owners = (len(rest) - 13) // 2 + 1
    inner_in = rest[: owners - 1]
    sums, far, wide, hot, roots = rest[owners - 1 : owners + 4]
    to_off, to_on, own, picked, *peers = rest[owners + 4 : -4]
    edge_s, second, hop, sem = rest[-4:]
    blocks = second.shape[0]
    width = second.shape[2]
    count = hot.shape[0]
    parity = lax.rem(lax.axis_index("group"), 2)
    group_base = blocks + owners * CAP
    copy = pltpu.make_async_copy(edge_ids, edge_s, sem)
    copy.start()
    step = blocks // CHUNKS
    for n in range(CHUNKS):
        rows = pl.ds(n * step * TILE, step * TILE)
        total = sums[rows, :] + jnp.dot(far[rows, :], off[pl.ds(0, CAPG * TILE), :], preferred_element_type=F32)
        for k in range(step):
            b = n * step + k
            root = roots[:, b : b + 1]
            one = root * total[k * TILE : (k + 1) * TILE]
            hop[pl.ds(b * TILE, TILE), :] = one.astype(BF)
            second[b] = (root * one).astype(BF)

    def scale(message, start):
        return lax.rsqrt(request_columns(message, start, count, width)[:, TPB : TPB + 1])

    wanted = [(group_base + (1 - parity) * CAPG + s).astype(F32) for s in range(CAPG)]
    asked = jnp.concatenate(expanded(off, CAPG * TILE, count, width, wanted), axis=1)
    copy.wait()
    offered = jnp.concatenate([second[edge_s[0, parity, s]] for s in range(CAPG)], axis=0)
    total = jnp.dot(asked, offered, preferred_element_type=F32)
    to_off[...] = (scale(off, CAPG * TILE) * total).astype(BF)
    mine = jnp.concatenate([second[b] for b in range(blocks)], axis=0)
    total = jnp.dot(wide[...], mine, preferred_element_type=F32)
    own[...] = scale(request, 0) * total[0:count]
    to_on[...] = (scale(on, CAPG * TILE) * total[count : 2 * count]).astype(BF)
    for k in range(1, owners):
        part = total[(k + 1) * count : (k + 2) * count]
        peers[k - 1][...] = (scale(inner_in[k - 1], CAP * TILE) * part).astype(BF)
    picked[...] = jnp.dot(hot[...], hop[...], preferred_element_type=F32).astype(BF)


def merge_kernel(owners, off, on, own, picked, *rest):
    peers = rest[: owners - 1]
    bundles = rest[owners - 1 :]
    slots = bundles[0].shape[1]
    mine = lax.axis_index("inner")
    for k in range(owners):
        rows = pl.ds(pl.multiple_of(lax.rem(mine + k, owners) * slots, slots), slots)
        total = own[rows, :] + off[rows, :].astype(F32) + on[rows, :].astype(F32)
        bundles[k][0] = total.astype(BF)
        bundles[k][1] = picked[rows, :]
        for r in range(1, owners):
            bundles[k][1 + r] = peers[r - 1][rows, :]


def gather_kernel(owners, *refs):
    bundles, out = refs[:owners], refs[owners]
    slots, width = bundles[0].shape[1:]
    mine = lax.axis_index("inner")
    for p in range(owners):
        total = bundles[p][0].astype(F32)
        for k in range(owners):
            if k != p:
                total = total + bundles[k][1 + (p - k) % owners].astype(F32)
        part = lax.rem(mine - p + owners, owners)
        rows = pl.ds(pl.multiple_of(part * slots, slots), slots)
        out[rows, 0:width] = bundles[p][1]
        out[rows, width : 2 * width] = total.astype(BF)


VMEM = pl.BlockSpec(memory_space=pltpu.VMEM)
HBM = pl.BlockSpec(memory_space=pltpu.HBM)


def call(kernel, name, inputs, specs, outputs, scratch=(), flops=0, limit=30, out_spec=VMEM):
    moved = sum(x.size * x.dtype.itemsize for x in list(inputs) + list(outputs))
    return pl.pallas_call(
        kernel,
        out_shape=outputs,
        in_specs=specs,
        out_specs=[out_spec] * len(outputs),
        scratch_shapes=list(scratch),
        compiler_params=pltpu.CompilerParams(vmem_limit_bytes=limit * 1024 * 1024),
        cost_estimate=pl.CostEstimate(flops=flops, bytes_accessed=moved, transcendentals=0),
        name=name,
    )(*inputs)


def on_device(groups, owners, features, projection, adjacency, degree, tile_src, send_ids, edge_ids, train_ids):
    row_count, depth = features.shape
    blocks = row_count // TILE
    width = projection.shape[1]
    slots = train_ids.shape[2]
    count = owners * slots
    request = TPB * TILE // width * count + META
    degree = degree.reshape(blocks, TILE)
    tile_src = tile_src.T
    across = [(g, (g + (1 if g % 2 else -1)) % groups) for g in range(groups)]
    beside = [(g, g ^ 1) for g in range(groups)]

    def around(value, k):
        return lax.ppermute(value, "inner", [(i, (i + k) % owners) for i in range(owners)])

    def array(*shape, kind=BF):
        return jax.ShapeDtypeStruct(shape, kind)

    integers = [
        pltpu.SMEM(tile_src.shape, jnp.int32),
        pltpu.SMEM(edge_ids.shape, jnp.int32),
        pltpu.SMEM(send_ids.shape, jnp.int32),
        pltpu.VMEM(train_ids.shape, jnp.int32),
        pltpu.VMEM((16, TILE), jnp.int32),
    ]
    indices = (tile_src, edge_ids, send_ids, train_ids, degree)
    group_message = array(CAPG * TILE + request, width)
    inner_message = array(CAP * TILE + request, width)
    first, own_request, off, on, *inner_out = call(
        project_kernel,
        "project",
        (*indices, projection, features, adjacency),
        [HBM] * 8,
        [array(blocks, TILE, width), array(request, width), group_message, group_message]
        + [inner_message] * (owners - 1),
        integers
        + [
            pltpu.VMEM(projection.shape, BF),
            pltpu.VMEM((row_count, depth), BF),
            pltpu.VMEM((row_count, TPB * TILE), BF),
            pltpu.VMEM((blocks, TILE, width), BF),
            pltpu.VMEM((request, width), BF),
            pltpu.SemaphoreType.DMA((7 + CHUNKS,)),
            pltpu.SemaphoreType.DMA((2 + owners + 2 * CAPG + (owners - 1) * CAP,)),
            pltpu.SemaphoreType.DMA((CHUNKS,)),
        ],
        2 * row_count * depth * width,
        60,
        HBM,
    )
    off_in = lax.ppermute(off, "group", across)
    inner_in = [around(inner_out[k - 1], k) for k in range(1, owners)]
    on_in = lax.ppermute(on, "group", beside)

    held = call(
        near_kernel,
        "near",
        (*indices, first, adjacency, own_request, on_in, *inner_in),
        [HBM] * 6 + [VMEM] * (2 + owners),
        [
            array(row_count, width, kind=F32),
            array(row_count, CAPG * TILE),
            array((owners + 1) * count, row_count),
            array(count, row_count),
            array(TILE, 16, kind=F32),
        ],
        integers
        + [
            pltpu.VMEM((blocks + owners * CAP + 2 * CAPG, TILE, width), BF),
            pltpu.SemaphoreType.DMA((6,)),
        ],
        2 * row_count * TPB * TILE * width,
    )
    to_off, to_on, own, picked, *peers = call(
        spread_kernel,
        "spread",
        (edge_ids, off_in, own_request, on_in, *inner_in, *held),
        [HBM] + [VMEM] * (7 + owners),
        [array(count, width), array(count, width), array(count, width, kind=F32), array(count, width)]
        + [array(count, width)] * (owners - 1),
        [
            pltpu.SMEM(edge_ids.shape, jnp.int32),
            pltpu.VMEM((blocks, TILE, width), BF),
            pltpu.VMEM((row_count, width), BF),
            pltpu.SemaphoreType.DMA,
        ],
        2 * row_count * CAPG * TILE * width,
    )
    off_part = lax.ppermute(to_off, "group", across)
    on_part = lax.ppermute(to_on, "group", beside)
    bundles = call(
        functools.partial(merge_kernel, owners),
        "merge",
        (off_part, on_part, own, picked, *peers),
        [VMEM] * (3 + owners),
        [array(1 + owners, slots, width)] * owners,
    )
    bundles = [bundles[0]] + [around(bundles[k], k) for k in range(1, owners)]
    return call(
        functools.partial(gather_kernel, owners), "gather", bundles, [VMEM] * owners, [array(count, 2 * width)]
    )[0]


def solution(mesh):
    both = ("group", "inner")

    def run(
        features, projection, adjacency, degree, tile_src, send_ids, send_count, edge_ids, edge_count, train_ids
    ):
        return on_device(
            mesh.shape["group"], mesh.shape["inner"],
            features, projection, adjacency, degree, tile_src, send_ids, edge_ids, train_ids,
        )

    placed = (
        P(both, None),
        P(),
        P(both, None),
        P(both),
        P(both, None),
        P(both, None, None),
        P(both, None),
        P(both, None, None),
        P(both, None),
        P(both, None, None),
    )
    return jax.shard_map(run, mesh=mesh, in_specs=placed, out_specs=P(both, None), check_vma=False)
```

time: 75.3 us -> 39 us (0.52)
  blocking collectives: 23.6 us -> 0 us
  local copies, waits for them, and re-layouts: 18.6 us -> 2.06 us
  Pallas kernels: 0 us -> 12.7 us
  other arithmetic: 12.2 us -> 0 us
  matrix products: 9.05 us -> 0 us
  waiting for transfers between devices: 5.3 us -> 13.5 us
  starting transfers between devices: 5.96 us -> 10.6 us
    all_gather x2 -> x0, blocking collectives: 16 us -> none  [spread(): everyone = lax.all_gather(outgoing[None], 'inner', axis=0, tiled=True)]
    gather x8 -> x0, local copies, waits for them, and re-layouts: 15.3 us -> none  [the longest x2 8.15 us: spread(): fetched = table[tile_src].reshape(block_count, TPB * TILE, out_width)]
    pallas_call x0 -> x5, Pallas kernels: none -> 12.7 us  [call(): pl.pallas_call(kernel, out_shape=outputs, in_specs=specs, out_specs=[out_...]
    dot_general x3 -> x0, matrix products: 9.05 us -> none  [the longest x2 7.28 us: spread(): jnp.einsum('bij,bjk->bik', adj_blocks, fetched, preferred_element_type=jn...]
    ppermute x4 -> x6, waiting for transfers between devices: 5.3 us -> 13.5 us  [the longest x2 8.27 us: around(): lax.ppermute(value, 'inner', [(i, (i + k) % owners) for i in range(owners)])]
    all_to_all x1 -> x0, blocking collectives: 7.59 us -> none  [on_device(): lax.all_to_all(leaving, 'inner', split_axis=0, concat_axis=0, tiled=True)]
    concatenate x3 -> x0, other arithmetic: 5.67 us -> none  [the longest x2 5.66 us: spread(): jnp.concatenate([own_blocks, incoming.reshape(-1, TILE, out_width), widen...]
    ppermute x4 -> x6, starting transfers between devices: 5.96 us -> 10.6 us  [the longest x1 5.65 us: on_device(): off_in = lax.ppermute(off, 'group', across)]
  transfers between devices with their start and end apart: 4 -> 6, of which waited for: 2 -> 3; matrix products, arithmetic and copies ran while one was open for 2% -> 0% of each run, Pallas kernels for 0% -> 11%
where the time goes in v2:
time: 39 us; the launch traced here: 38.9 us
  waiting for transfers between devices  13.5 us (35%)
  Pallas kernels  12.7 us (33%)
  starting transfers between devices  10.6 us (27%)
  local copies, waits for them, and re-layouts  2.06 us (5%)
    pallas_call x5, Pallas kernels, call(): pl.pallas_call(kernel, out_shape=outputs, in_specs=specs, out_specs=[out_...  12.7 us
    ppermute x2, waiting for transfers between devices, around(): lax.ppermute(value, 'inner', [(i, (i + k) % owners) for i in range(owners)])  8.27 us
    ppermute x1, starting transfers between devices, on_device(): off_in = lax.ppermute(off, 'group', across)  5.65 us
    ppermute x1, waiting for transfers between devices, on_device(): off_part = lax.ppermute(to_off, 'group', across)  5.18 us
    ppermute x2, starting transfers between devices, around(): lax.ppermute(value, 'inner', [(i, (i + k) % owners) for i in range(owners)])  3.08 us
    unnamed x16, local copies, waits for them, and re-layouts  2.06 us
    ppermute x1, starting transfers between devices, on_device(): off_part = lax.ppermute(to_off, 'group', across)  1 us
  transfers between devices with their start and end apart: 6, of which 3 were waited for; matrix products, arithmetic and copies ran while one was open for 0% of the time, Pallas kernels for 11%

profile of v2, /device:TPU:0, one launch (start us, length us, event | category | flops | bytes accessed | tf_op | source)
XLA Modules:
  0.0 38.9 jit_solution(12938379002958085092)
XLA Ops:
  0.0 0.0 copy-start
  0.0 0.0 copy-start.3
  0.0 0.0 copy-start.4
  0.0 0.0 copy-start.5
  0.0 0.0 copy-start.6
  0.0 0.0 copy-start.7
  0.0 5.0 %project.1 = (bf16[12,128,256]{2,1,0:T(8,128)(2,1)}, bf16[272,256]{1,0:T(8,128)(2,1)}, bf16[1296,256]{1,0:T(8,128)(2,1)}, bf16[1296,256]{1,0:T(8,128)(2,1)}, bf16[528,256]{1,0:T(8,128)(2,1)}) custom-call(s32[4,12]{1,0:T(4,128)} %bitcast.4, s32[1,2,8]{2,1,0:T(2,128)} %edge_ids.5, s32[1,2,2]{2,1,0:T(2,128)} %send_ids.3, s32[1,2,64]{2,1,0:T(2,128)} %train.3, ...), custom_call_target="tpu_custom_call" | custom-call | flops 603979776 | bytes 6855440 | tf_op jit(solution)/shard_map/project/pallas_call | solution.py:290
  5.0 0.6 %collective-permute-start.1 = (bf16[1296,256]{1,0:T(8,128)(2,1)}, bf16[1296,256]{1,0:T(8,128)(2,1)S(1)}, u32[]{:S(2)}, u32[]{:S(2)}) collective-permute-start(bf16[1296,256]{1,0:T(8,128)(2,1)} %get-tuple-element.24), channel_id=1, source_target_pairs={{0,2},{2,0},{4,6},{6,4},{8,10},{10,8},{12,14},{14,12},{16,18},{18,... | collective-permute-start | bytes 1990664 | tf_op jit(solution)/shard_map/ppermute | solution.py:354
  5.6 5.7 %collective-permute-start = (bf16[1296,256]{1,0:T(8,128)(2,1)}, bf16[1296,256]{1,0:T(8,128)(2,1)S(1)}, u32[]{:S(2)}, u32[]{:S(2)}) collective-permute-start(bf16[1296,256]{1,0:T(8,128)(2,1)} %get-tuple-element.22), channel_id=1, source_target_pairs={{0,30},{2,4},{4,2},{6,8},{8,6},{10,12},{12,10},{14,16},{16,14},{18... | collective-permute-start | bytes 1990664 | tf_op jit(solution)/shard_map/ppermute | solution.py:352
  11.2 1.5 %collective-permute-start.2 = (bf16[528,256]{1,0:T(8,128)(2,1)}, bf16[528,256]{1,0:T(8,128)(2,1)S(1)}, u32[]{:S(2)}, u32[]{:S(2)}) collective-permute-start(bf16[528,256]{1,0:T(8,128)(2,1)} %get-tuple-element.25), channel_id=1, source_target_pairs={{0,1},{1,0},{2,3},{3,2},{4,5},{5,4},{6,7},{7,6},{8,9},{9,8},{10,11... | collective-permute-start | bytes 811016 | tf_op jit(solution)/shard_map/ppermute | solution.py:315
  12.8 5.2 %collective-permute-done.2.rest_0_ = bf16[528,256]{1,0:T(8,128)(2,1)S(1)} collective-permute-done((bf16[528,256]{1,0:T(8,128)(2,1)}, bf16[528,256]{1,0:T(8,128)(2,1)S(1)}, u32[]{:S(2)}, u32[]{:S(2)}) %collective-permute-start.2) | collective-permute-done | bytes 270368 | tf_op jit(solution)/shard_map/ppermute | solution.py:315
  17.9 0.0 collective-permute-done.1.on
  17.9 0.0 copy-done
  17.9 0.0 copy-done.3
  17.9 0.0 copy-done.4
  17.9 0.0 copy-done.5
  18.0 0.0 copy-done.6
  18.0 0.0 copy-done.7
  18.0 0.0 copy-start.1
  18.0 1.1 %copy-done.1 = bf16[12,128,256]{2,1,0:T(8,128)(2,1)S(1)} copy-done((bf16[12,128,256]{2,1,0:T(8,128)(2,1)S(1)}, bf16[12,128,256]{2,1,0:T(8,128)(2,1)}, u32[]{:S(2)}) %copy-start.1) | copy-done | bytes 786456
  19.1 0.0 copy-start.2
  19.1 0.9 %copy-done.2 = bf16[272,256]{1,0:T(8,128)(2,1)S(1)} copy-done((bf16[272,256]{1,0:T(8,128)(2,1)S(1)}, bf16[272,256]{1,0:T(8,128)(2,1)}, u32[]{:S(2)}) %copy-start.2) | copy-done | bytes 139288
  20.0 4.5 %near.1 = (f32[1536,256]{1,0:T(8,128)S(1)}, bf16[1536,1024]{1,0:T(8,128)(2,1)S(1)}, bf16[384,1536]{1,0:T(8,128)(2,1)S(1)}, bf16[128,1536]{1,0:T(8,128)(2,1)S(1)}, f32[128,16]{1,0:T(8,128)S(1)}) custom-call(s32[4,12]{1,0:T(4,128)S(1)} %bitcast.5, s32[1,2,8]{2,1,0:T(2,128)S(1)} %copy-done.4, s32[1,2,2]{2,1,0:T(2,128)S(1)} %copy-done.6, ...), custom_call_target="tpu_custom_call" | custom-call | flops 402653184 | bytes 9739024 | tf_op jit(solution)/shard_map/near/pallas_call | solution.py:290
  24.5 0.0 collective-permute-done.off
  24.5 2.5 %spread.1 = (bf16[128,256]{1,0:T(8,128)(2,1)S(1)}, bf16[128,256]{1,0:T(8,128)(2,1)S(1)}, f32[128,256]{1,0:T(8,128)S(1)}, bf16[128,256]{1,0:T(8,128)(2,1)S(1)}, bf16[128,256]{1,0:T(8,128)(2,1)S(1)}) custom-call(s32[1,2,8]{2,1,0:T(2,128)S(1)} %copy-done.4, bf16[1296,256]{1,0:T(8,128)(2,1)S(1)} %collective-permute-done.off, bf16[272,256]{1,0:T(8,128)(2,1)S(1)} %copy-done.2, ...), custom_call_target="tpu_custom_call" | custom-call | flops 805306368 | bytes 8429632 | tf_op jit(solution)/shard_map/spread/pallas_call | solution.py:290
  27.0 1.0 %collective-permute-start.3 = (bf16[128,256]{1,0:T(8,128)(2,1)S(1)}, bf16[128,256]{1,0:T(8,128)(2,1)S(1)}, u32[]{:S(2)}, u32[]{:S(2)}) collective-permute-start(bf16[128,256]{1,0:T(8,128)(2,1)S(1)} %get-tuple-element.32), channel_id=1, source_target_pairs={{0,30},{2,4},{4,2},{6,8},{8,6},{10,12},{12,10},{14,16},{16,14},{18... | collective-permute-start | bytes 196616 | tf_op jit(solution)/shard_map/ppermute | solution.py:390
  28.0 0.3 collective-permute-start.4
  28.3 5.2 %collective-permute-done.3.off = bf16[128,256]{1,0:T(8,128)(2,1)S(1)} collective-permute-done((bf16[128,256]{1,0:T(8,128)(2,1)S(1)}, bf16[128,256]{1,0:T(8,128)(2,1)S(1)}, u32[]{:S(2)}, u32[]{:S(2)}) %collective-permute-start.3) | collective-permute-done | bytes 65568 | tf_op jit(solution)/shard_map/ppermute | solution.py:390
  33.5 0.0 collective-permute-done.4.on
  33.5 1.6 %collective-permute-start.5 = (bf16[3,64,256]{2,1,0:T(8,128)(2,1)S(1)}, bf16[3,64,256]{2,1,0:T(8,128)(2,1)S(1)}, u32[]{:S(2)}, u32[]{:S(2)}) collective-permute-start(bf16[3,64,256]{2,1,0:T(8,128)(2,1)S(1)} %get-tuple-element.38), channel_id=1, source_target_pairs={{0,1},{1,0},{2,3},{3,2},{4,5},{5,4},{6,7},{7,6},{8,9},{9,8},{10,11... | collective-permute-start | bytes 294920 | tf_op jit(solution)/shard_map/ppermute | solution.py:315
  35.1 3.1 %collective-permute-done.5.refs_1_ = bf16[3,64,256]{2,1,0:T(8,128)(2,1)S(1)} collective-permute-done((bf16[3,64,256]{2,1,0:T(8,128)(2,1)S(1)}, bf16[3,64,256]{2,1,0:T(8,128)(2,1)S(1)}, u32[]{:S(2)}, u32[]{:S(2)}) %collective-permute-start.5) | collective-permute-done | bytes 98336 | tf_op jit(solution)/shard_map/ppermute | solution.py:315
  38.2 0.7 %gather.1 = bf16[128,512]{1,0:T(8,128)(2,1)} custom-call(bf16[3,64,256]{2,1,0:T(8,128)(2,1)S(1)} %get-tuple-element.37.refs_0_, bf16[3,64,256]{2,1,0:T(8,128)(2,1)S(1)} %collective-permute-done.5.refs_1_), custom_call_target="tpu_custom_call" | custom-call | bytes 327680 | tf_op jit(solution)/shard_map/gather/pallas_call | solution.py:290
  (1 shorter events, 0.0 us)
Async XLA Ops:
  0.0 17.9 %copy-start = (bf16[1536,512]{1,0:T(8,128)(2,1)S(1)}, bf16[1536,512]{1,0:T(8,128)(2,1)}, u32[]{:S(2)}) copy-start(bf16[1536,512]{1,0:T(8,128)(2,1)} %adjacency.3) | copy-start | bytes 4718596
  0.0 17.9 %copy-start.3 = (s32[1536]{0:T(1024)S(1)}, s32[1536]{0:T(1024)}, u32[]{:S(2)}) copy-start(s32[1536]{0:T(1024)} %param.13) | copy-start | bytes 18436
  0.0 17.9 %copy-start.4 = (s32[1,2,8]{2,1,0:T(2,128)S(1)}, s32[1,2,8]{2,1,0:T(2,128)}, u32[]{:S(2)}) copy-start(s32[1,2,8]{2,1,0:T(2,128)} %edge_ids.5) | copy-start | bytes 196
  0.0 17.9 %copy-start.5 = (s32[12,4]{0,1:T(4,128)S(1)}, s32[12,4]{0,1:T(4,128)}, u32[]{:S(2)}) copy-start(s32[12,4]{0,1:T(4,128)} %param.14) | copy-start | bytes 580
  0.0 17.9 %copy-start.6 = (s32[1,2,2]{2,1,0:T(2,128)S(1)}, s32[1,2,2]{2,1,0:T(2,128)}, u32[]{:S(2)}) copy-start(s32[1,2,2]{2,1,0:T(2,128)} %send_ids.3) | copy-start | bytes 52
  0.0 17.9 %copy-start.7 = (s32[1,2,64]{2,1,0:T(2,128)S(1)}, s32[1,2,64]{2,1,0:T(2,128)}, u32[]{:S(2)}) copy-start(s32[1,2,64]{2,1,0:T(2,128)} %train.3) | copy-start | bytes 1540
  5.0 12.9 %collective-permute-start.1 = (bf16[1296,256]{1,0:T(8,128)(2,1)}, bf16[1296,256]{1,0:T(8,128)(2,1)S(1)}, u32[]{:S(2)}, u32[]{:S(2)}) collective-permute-start(bf16[1296,256]{1,0:T(8,128)(2,1)} %get-tuple-element.24), channel_id=1, source_target_pairs={{0,2},{2,0},{4,6},{6,4},{8,10},{10,8},{12,14},{14,12},{16,18},{18,... | collective-permute-start | bytes 1990664 | tf_op jit(solution)/shard_map/ppermute | solution.py:354
  5.6 18.9 %collective-permute-start = (bf16[1296,256]{1,0:T(8,128)(2,1)}, bf16[1296,256]{1,0:T(8,128)(2,1)S(1)}, u32[]{:S(2)}, u32[]{:S(2)}) collective-permute-start(bf16[1296,256]{1,0:T(8,128)(2,1)} %get-tuple-element.22), channel_id=1, source_target_pairs={{0,30},{2,4},{4,2},{6,8},{8,6},{10,12},{12,10},{14,16},{16,14},{18... | collective-permute-start | bytes 1990664 | tf_op jit(solution)/shard_map/ppermute | solution.py:352
  11.2 6.7 %collective-permute-start.2 = (bf16[528,256]{1,0:T(8,128)(2,1)}, bf16[528,256]{1,0:T(8,128)(2,1)S(1)}, u32[]{:S(2)}, u32[]{:S(2)}) collective-permute-start(bf16[528,256]{1,0:T(8,128)(2,1)} %get-tuple-element.25), channel_id=1, source_target_pairs={{0,1},{1,0},{2,3},{3,2},{4,5},{5,4},{6,7},{7,6},{8,9},{9,8},{10,11... | collective-permute-start | bytes 811016 | tf_op jit(solution)/shard_map/ppermute | solution.py:315
  18.0 1.1 %copy-start.1 = (bf16[12,128,256]{2,1,0:T(8,128)(2,1)S(1)}, bf16[12,128,256]{2,1,0:T(8,128)(2,1)}, u32[]{:S(2)}) copy-start(bf16[12,128,256]{2,1,0:T(8,128)(2,1)} %get-tuple-element.26.first) | copy-start | bytes 2359300
  19.1 0.9 %copy-start.2 = (bf16[272,256]{1,0:T(8,128)(2,1)S(1)}, bf16[272,256]{1,0:T(8,128)(2,1)}, u32[]{:S(2)}) copy-start(bf16[272,256]{1,0:T(8,128)(2,1)} %get-tuple-element.23.request) | copy-start | bytes 417796
  27.0 6.5 %collective-permute-start.3 = (bf16[128,256]{1,0:T(8,128)(2,1)S(1)}, bf16[128,256]{1,0:T(8,128)(2,1)S(1)}, u32[]{:S(2)}, u32[]{:S(2)}) collective-permute-start(bf16[128,256]{1,0:T(8,128)(2,1)S(1)} %get-tuple-element.32), channel_id=1, source_target_pairs={{0,30},{2,4},{4,2},{6,8},{8,6},{10,12},{12,10},{14,16},{16,14},{18... | collective-permute-start | bytes 196616 | tf_op jit(solution)/shard_map/ppermute | solution.py:390
  28.0 5.5 %collective-permute-start.4 = (bf16[128,256]{1,0:T(8,128)(2,1)S(1)}, bf16[128,256]{1,0:T(8,128)(2,1)S(1)}, u32[]{:S(2)}, u32[]{:S(2)}) collective-permute-start(bf16[128,256]{1,0:T(8,128)(2,1)S(1)} %get-tuple-element.33), channel_id=1, source_target_pairs={{0,2},{2,0},{4,6},{6,4},{8,10},{10,8},{12,14},{14,12},{16,18},{18,... | collective-permute-start | bytes 196616 | tf_op jit(solution)/shard_map/ppermute | solution.py:391
  33.5 4.7 %collective-permute-start.5 = (bf16[3,64,256]{2,1,0:T(8,128)(2,1)S(1)}, bf16[3,64,256]{2,1,0:T(8,128)(2,1)S(1)}, u32[]{:S(2)}, u32[]{:S(2)}) collective-permute-start(bf16[3,64,256]{2,1,0:T(8,128)(2,1)S(1)} %get-tuple-element.38), channel_id=1, source_target_pairs={{0,1},{1,0},{2,3},{3,2},{4,5},{5,4},{6,7},{7,6},{8,9},{9,8},{10,11... | collective-permute-start | bytes 294920 | tf_op jit(solution)/shard_map/ppermute | solution.py:315

commit v3 on v0

v3 whole, which is shorter than its diff:
```python
import functools

import jax
import jax.numpy as jnp
from jax import lax
from jax.experimental import pallas as pl
from jax.experimental.pallas import tpu as pltpu
from jax.sharding import PartitionSpec as P

TILE = 128
TPB = 4
CAP = 2
CAPG = 8
BF = jnp.bfloat16
F32 = jnp.float32
SPREAD_CHUNKS = 2


META = 16


def ids_row(train):
    owners = train.shape[1]
    return jnp.concatenate([train[0, j : j + 1, :] for j in range(owners)], axis=1)


def as_columns(rows):
    return jnp.transpose(rows)


def spread_lanes(column):
    return jnp.broadcast_to(column, (column.shape[0], TILE)).astype(BF)


def one_hot_parts(train, blocks):
    row = ids_row(train)
    count = row.shape[1]
    column = as_columns(jnp.broadcast_to(row.astype(F32), (8, count)))[:, 0:1].astype(jnp.int32)
    lane = lax.broadcasted_iota(jnp.int32, (count, TILE), 1) == lax.rem(column, TILE)
    lane = lane.astype(F32).astype(BF)
    block = spread_lanes(lax.div(column, TILE).astype(F32))
    nothing = jnp.zeros((), BF)
    return [jnp.where(block == jnp.array(b, BF), lane, nothing) for b in range(blocks)]


def fetch(pairs, sems):
    copies = [pltpu.make_async_copy(source, target, sems.at[n]) for n, (source, target) in enumerate(pairs)]
    for copy in copies:
        copy.start()
    return copies


def fill_degrees(degrees, blocks):
    degrees[pl.ds(blocks, 16 - blocks), :] = jnp.ones((16 - blocks, TILE), jnp.int32)


def first_kernel(edge_ids, send_ids, degree, product, first, off, on, *rest):
    inner_out = rest[:-4]
    edge_s, send_s, degrees, sems = rest[-4:]
    blocks = first.shape[0]
    owners = len(inner_out) + 1
    parity = lax.rem(lax.axis_index("group"), 2)
    mine = lax.axis_index("inner")
    arriving = fetch([(degree, degrees.at[pl.ds(0, blocks)]), (edge_ids, edge_s), (send_ids, send_s)], sems)
    fill_degrees(degrees, blocks)
    arriving[0].wait()
    roots = as_columns(lax.rsqrt(degrees[...].astype(F32)))
    for b in range(blocks):
        first[b] = (roots[:, b : b + 1] * product[pl.ds(b * TILE, TILE), :]).astype(BF)
    arriving[1].wait()
    arriving[2].wait()
    for s in range(CAPG):
        off[pl.ds(s * TILE, TILE), :] = first[edge_s[0, parity, s]]
        on[pl.ds(s * TILE, TILE), :] = first[edge_s[0, 1 - parity, s]]
    for k in range(1, owners):
        peer = lax.rem(mine + k, owners)
        for s in range(CAP):
            inner_out[k - 1][pl.ds(s * TILE, TILE), :] = first[send_s[0, peer, s]]


def request_columns(request, count, width):
    strips = TPB * TILE // width
    return as_columns(request[pl.ds(strips * count, META), 0:count].astype(F32))


def request_scale(request, count, width):
    return lax.rsqrt(request_columns(request, count, width)[:, TPB : TPB + 1])


def expanded(request, count, width, wanted):
    columns = request_columns(request, count, width)
    codes = [spread_lanes(columns[:, t : t + 1]) for t in range(TPB)]
    tiles = []
    for t in range(TPB):
        h, c = divmod(t * TILE, width)
        tiles.append(request[pl.ds(h * count, count), c : c + TILE])
    nothing = jnp.zeros((), BF)
    parts = []
    for want in wanted:
        want = jnp.asarray(want, F32).astype(BF)
        parts.append(sum(jnp.where(codes[t] == want, tiles[t], nothing) for t in range(TPB)))
    return parts


def ask_kernel(
    tile_src, train, degree, after, adjacency, request, far, hot, roots, src_s, train_v, degrees, sems
):
    blocks = degree.shape[0]
    owners = train.shape[1]
    count = owners * train.shape[2]
    width = request.shape[1]
    parity = lax.rem(lax.axis_index("group"), 2)
    off_base = blocks + owners * CAP + parity * CAPG
    arriving = fetch([(train, train_v), (tile_src, src_s), (degree, degrees.at[pl.ds(0, blocks)])], sems)
    fill_degrees(degrees, blocks)
    far[...] = jnp.zeros_like(far)
    for copy in arriving:
        copy.wait()
    roots[...] = as_columns(lax.rsqrt(degrees[...].astype(F32)))
    row = ids_row(train_v)
    block_of = lax.div(row, TILE)
    lane_hot = lax.broadcasted_iota(jnp.int32, (TILE, count), 0) == lax.rem(row, TILE)
    by_block = jnp.dot(
        degrees[...].astype(F32).astype(BF), lane_hot.astype(F32).astype(BF), preferred_element_type=F32
    )
    chosen = lax.broadcasted_iota(jnp.int32, by_block.shape, 0) == block_of
    meta = []
    for t in range(TPB):
        codes = jnp.zeros((1, count), F32)
        for b in range(blocks):
            codes = jnp.where(block_of == b, src_s[t, b].astype(F32), codes)
        meta.append(codes)
    meta.append(jnp.sum(jnp.where(chosen, by_block, 0.0), axis=0, keepdims=True))
    meta.append(jnp.ones((META - TPB - 1, count), F32))
    meta = jnp.concatenate(meta, axis=0)
    if count < width:
        meta = jnp.concatenate([meta, jnp.ones((META, width - count), F32)], axis=1)
    strips = TPB * TILE // width
    request[pl.ds(strips * count, META), :] = meta.astype(BF)
    for b, part in enumerate(one_hot_parts(train_v, blocks)):
        hot[:, b * TILE : (b + 1) * TILE] = part
    picked = jnp.dot(hot[...], adjacency[...], preferred_element_type=F32).astype(BF)
    for h in range(strips):
        request[pl.ds(h * count, count), :] = picked[:, h * width : (h + 1) * width]
    for b in range(blocks):
        for t in range(TPB):
            slot = src_s[t, b] - off_base

            @pl.when(jnp.logical_and(slot >= 0, slot < CAPG))
            def _():
                place = (pl.ds(b * TILE, TILE), pl.ds(pl.multiple_of(slot * TILE, TILE), TILE))
                far[place] += adjacency[pl.ds(b * TILE, TILE), t * TILE : (t + 1) * TILE]


def near_kernel(tile_src, first, adjacency, request, on, *rest):
    owners = len(rest) - 4
    inner_in = rest[: owners - 1]
    sums, ask, src_s, table, sems = rest[owners - 1 :]
    blocks, _, width = first.shape
    parity = lax.rem(lax.axis_index("group"), 2)
    mine = lax.axis_index("inner")
    group_base = blocks + owners * CAP
    arriving = fetch([(tile_src, src_s), (first, table.at[pl.ds(0, blocks)])], sems)
    ask[...] = request[...]
    for s in range(CAPG):
        table[group_base + parity * CAPG + s] = jnp.zeros((TILE, width), BF)
        table[group_base + (1 - parity) * CAPG + s] = on[pl.ds(s * TILE, TILE), :]
    for s in range(CAP):
        table[blocks + mine * CAP + s] = jnp.zeros((TILE, width), BF)
        for k in range(1, owners):
            peer = lax.rem(mine - k + owners, owners)
            table[blocks + peer * CAP + s] = inner_in[k - 1][pl.ds(s * TILE, TILE), :]
    for copy in arriving:
        copy.wait()
    for b in range(blocks):
        fetched = jnp.concatenate([table[src_s[t, b]] for t in range(TPB)], axis=0)
        sums[pl.ds(b * TILE, TILE), :] = jnp.dot(
            adjacency[pl.ds(b * TILE, TILE), :], fetched, preferred_element_type=F32
        )


def spread_kernel(edge_ids, off, sums, far, roots, second, hop, offered, edge_s, sem):
    row_count = second.shape[0]
    parity = lax.rem(lax.axis_index("group"), 2)
    copy = pltpu.make_async_copy(edge_ids, edge_s, sem)
    copy.start()
    chunk = row_count // SPREAD_CHUNKS
    for n in range(SPREAD_CHUNKS):
        rows = pl.ds(n * chunk, chunk)
        total = sums[rows, :] + jnp.dot(far[rows, :], off[...], preferred_element_type=F32)
        for k in range(chunk // TILE):
            b = n * (chunk // TILE) + k
            root = roots[:, b : b + 1]
            one = root * total[k * TILE : (k + 1) * TILE]
            hop[pl.ds(b * TILE, TILE), :] = one.astype(BF)
            second[pl.ds(b * TILE, TILE), :] = (root * one).astype(BF)
    copy.wait()
    for s in range(CAPG):
        block = pl.ds(pl.multiple_of(edge_s[0, parity, s] * TILE, TILE), TILE)
        offered[pl.ds(s * TILE, TILE), :] = second[block, :]


def rest_kernel(edge_ids, send_ids, second, hop, hot, request, on, *rest):
    owners = send_ids.shape[1]
    inner_in = rest[: owners - 1]
    to_on, own, picked, *peers = rest[owners - 1 : -4]
    wide, edge_s, send_s, sems = rest[-4:]
    count = hot.shape[0]
    row_count, width = second.shape
    blocks = row_count // TILE
    parity = lax.rem(lax.axis_index("group"), 2)
    mine = lax.axis_index("inner")
    arriving = fetch([(edge_ids, edge_s), (send_ids, send_s)], sems)
    wide[...] = jnp.zeros_like(wide)
    parts = expanded(request, count, width, [float(b) for b in range(blocks)])
    for b in range(blocks):
        wide[pl.ds(0, count), b * TILE : (b + 1) * TILE] = parts[b]
    picked[...] = jnp.dot(hot[...], hop[...], preferred_element_type=F32).astype(BF)
    for copy in arriving:
        copy.wait()
    asked = [(on, CAPG, blocks + owners * CAP + parity * CAPG, lambda s: edge_s[0, 1 - parity, s])]
    for k in range(1, owners):
        peer = lax.rem(mine - k + owners, owners)
        asked.append((inner_in[k - 1], CAP, blocks + mine * CAP, lambda s, peer=peer: send_s[0, peer, s]))
    for n, (message, slots, base, block) in enumerate(asked):
        parts = expanded(message, count, width, [base + s for s in range(slots)])
        for s in range(slots):
            column = pl.multiple_of(block(s) * TILE, TILE)
            wide[pl.ds((n + 1) * count, count), pl.ds(column, TILE)] = parts[s]
    total = jnp.dot(wide[...], second[...], preferred_element_type=F32)
    own[...] = request_scale(request, count, width) * total[0:count]
    to_on[...] = (request_scale(on, count, width) * total[count : 2 * count]).astype(BF)
    for k in range(1, owners):
        part = total[(k + 1) * count : (k + 2) * count]
        peers[k - 1][...] = (request_scale(inner_in[k - 1], count, width) * part).astype(BF)


def answer_kernel(group_base, request, offered, to_off):
    count, width = to_off.shape
    parity = lax.rem(lax.axis_index("group"), 2)
    base = group_base + (1 - parity) * CAPG
    asked = jnp.concatenate(expanded(request, count, width, [base + s for s in range(CAPG)]), axis=1)
    total = jnp.dot(asked, offered[...], preferred_element_type=F32)
    to_off[...] = (request_scale(request, count, width) * total).astype(BF)


def merge_kernel(owners, off, on, own, picked, *rest):
    peers = rest[: owners - 1]
    bundles = rest[owners - 1 :]
    slots = bundles[0].shape[1]
    mine = lax.axis_index("inner")
    for k in range(owners):
        rows = pl.ds(pl.multiple_of(lax.rem(mine + k, owners) * slots, slots), slots)
        total = own[rows, :] + off[rows, :].astype(F32) + on[rows, :].astype(F32)
        bundles[k][0] = total.astype(BF)
        bundles[k][1] = picked[rows, :]
        for r in range(1, owners):
            bundles[k][1 + r] = peers[r - 1][rows, :]


def gather_kernel(owners, *refs):
    bundles, out = refs[:owners], refs[owners]
    slots, width = bundles[0].shape[1:]
    mine = lax.axis_index("inner")
    for p in range(owners):
        total = bundles[p][0].astype(F32)
        for k in range(owners):
            if k != p:
                total = total + bundles[k][1 + (p - k) % owners].astype(F32)
        part = lax.rem(mine - p + owners, owners)
        rows = pl.ds(pl.multiple_of(part * slots, slots), slots)
        out[rows, 0:width] = bundles[p][1]
        out[rows, width : 2 * width] = total.astype(BF)


VMEM = pl.BlockSpec(memory_space=pltpu.VMEM)
HBM = pl.BlockSpec(memory_space=pltpu.HBM)
ANY = pl.BlockSpec(memory_space=pl.ANY)


def call(kernel, name, inputs, specs, outputs, scratch=()):
    return pl.pallas_call(
        kernel,
        out_shape=outputs,
        in_specs=specs,
        out_specs=[VMEM] * len(outputs),
        scratch_shapes=list(scratch),
        compiler_params=pltpu.CompilerParams(vmem_limit_bytes=30 * 1024 * 1024),
        name=name,
    )(*inputs)


def on_device(groups, owners, features, projection, adjacency, degree, tile_src, send_ids, edge_ids, train_ids):
    row_count, depth = features.shape
    blocks = row_count // TILE
    width = projection.shape[1]
    slots = train_ids.shape[2]
    count = owners * slots
    tail = TPB * TILE // width * count + META
    degree = degree.reshape(blocks, TILE)
    tile_src = tile_src.T
    across = [(g, (g + (1 if g % 2 else -1)) % groups) for g in range(groups)]
    beside = [(g, g ^ 1) for g in range(groups)]

    def around(value, k):
        return lax.ppermute(value, "inner", [(i, (i + k) % owners) for i in range(owners)])

    def array(*shape, kind=BF):
        return jax.ShapeDtypeStruct(shape, kind)

    def smem(like):
        return pltpu.SMEM(like.shape, jnp.int32)

    train_scratch = pltpu.VMEM(train_ids.shape, jnp.int32)
    degree_scratch = pltpu.VMEM((16, TILE), jnp.int32)
    dma = pltpu.SemaphoreType.DMA

    product = jnp.dot(features, projection, preferred_element_type=F32)
    first, off, on, *inner_out = call(
        first_kernel,
        "first",
        (edge_ids, send_ids, degree, product),
        [HBM] * 3 + [VMEM],
        [array(blocks, TILE, width), array(CAPG * TILE, width), array(CAPG * TILE, width)]
        + [array(CAP * TILE, width)] * (owners - 1),
        [smem(edge_ids), smem(send_ids), degree_scratch, dma((3,))],
    )
    off_in = lax.ppermute(off, "group", across)
    inner_in = [around(inner_out[k - 1], k) for k in range(1, owners)]
    on_in = lax.ppermute(on, "group", beside)
    request, far, hot, roots = call(
        ask_kernel,
        "ask",
        (tile_src, train_ids, degree, on_in, adjacency),
        [HBM] * 3 + [ANY, VMEM],
        [
            array(tail, width),
            array(row_count, CAPG * TILE),
            array(count, row_count),
            array(TILE, 16, kind=F32),
        ],
        [smem(tile_src), train_scratch, degree_scratch, dma((3,))],
    )
    asked_inner = [around(request, k) for k in range(1, owners)]
    asked_on = lax.ppermute(request, "group", beside)
    sums, ask = call(
        near_kernel,
        "near",
        (tile_src, first, adjacency, request, on_in, *inner_in),
        [HBM] * 2 + [VMEM] * (2 + owners),
        [array(row_count, width, kind=F32), array(tail, width)],
        [smem(tile_src), pltpu.VMEM((blocks + owners * CAP + 2 * CAPG, TILE, width), BF), dma((2,))],
    )
    asked_off = lax.ppermute(ask, "group", across)
    second, hop, offered = call(
        spread_kernel,
        "spread",
        (edge_ids, off_in, sums, far, roots),
        [HBM] + [VMEM] * 4,
        [array(row_count, width), array(row_count, width), array(CAPG * TILE, width)],
        [smem(edge_ids), dma],
    )
    (to_off,) = call(
        functools.partial(answer_kernel, blocks + owners * CAP),
        "answer",
        (asked_off, offered),
        [VMEM] * 2,
        [array(count, width)],
    )
    to_on, own, picked, *peers = call(
        rest_kernel,
        "rest",
        (edge_ids, send_ids, second, hop, hot, request, asked_on, *asked_inner),
        [HBM] * 2 + [VMEM] * (4 + owners),
        [array(count, width), array(count, width, kind=F32), array(count, width)]
        + [array(count, width)] * (owners - 1),
        [pltpu.VMEM(((owners + 1) * count, row_count), BF), smem(edge_ids), smem(send_ids), dma((2,))],
    )
    off_part = lax.ppermute(to_off, "group", across)
    on_part = lax.ppermute(to_on, "group", beside)
    bundles = call(
        functools.partial(merge_kernel, owners),
        "merge",
        (off_part, on_part, own, picked, *peers),
        [VMEM] * (3 + owners),
        [array(1 + owners, slots, width)] * owners,
    )
    bundles = [bundles[0]] + [around(bundles[k], k) for k in range(1, owners)]
    return call(
        functools.partial(gather_kernel, owners), "gather", bundles, [VMEM] * owners, [array(count, 2 * width)]
    )[0]


def solution(mesh):
    both = ("group", "inner")

    def run(
        features, projection, adjacency, degree, tile_src, send_ids, send_count, edge_ids, edge_count, train_ids
    ):
        return on_device(
            mesh.shape["group"], mesh.shape["inner"],
            features, projection, adjacency, degree, tile_src, send_ids, edge_ids, train_ids,
        )

    placed = (
        P(both, None),
        P(),
        P(both, None),
        P(both),
        P(both, None),
        P(both, None, None),
        P(both, None),
        P(both, None, None),
        P(both, None),
        P(both, None, None),
    )
    return jax.shard_map(run, mesh=mesh, in_specs=placed, out_specs=P(both, None), check_vma=False)
```

time: 75.3 us -> 36.2 us (0.48)
  blocking collectives: 23.6 us -> 0 us
  local copies, waits for them, and re-layouts: 18.6 us -> 1.66 us
  other arithmetic: 12.2 us -> 0 us
  Pallas kernels: 0 us -> 7.62 us
  waiting for transfers between devices: 5.3 us -> 12.8 us
  matrix products: 9.05 us -> 1.77 us
  starting transfers between devices: 5.96 us -> 12 us
    all_gather x2 -> x0, blocking collectives: 16 us -> none  [spread(): everyone = lax.all_gather(outgoing[None], 'inner', axis=0, tiled=True)]
    gather x8 -> x0, local copies, waits for them, and re-layouts: 15.3 us -> none  [the longest x2 8.15 us: spread(): fetched = table[tile_src].reshape(block_count, TPB * TILE, out_width)]
    pallas_call x0 -> x8, Pallas kernels: none -> 7.62 us  [call(): pl.pallas_call(kernel, out_shape=outputs, in_specs=specs, out_specs=[VMEM...]
    all_to_all x1 -> x0, blocking collectives: 7.59 us -> none  [on_device(): lax.all_to_all(leaving, 'inner', split_axis=0, concat_axis=0, tiled=True)]
    ppermute x4 -> x9, waiting for transfers between devices: 5.3 us -> 12.8 us  [the longest x3 4.86 us: around(): lax.ppermute(value, 'inner', [(i, (i + k) % owners) for i in range(owners)])]
    dot_general x3 -> x1, matrix products: 9.05 us -> 1.77 us  [on_device(): product = jnp.dot(features, projection, preferred_element_type=F32)]
    ppermute x4 -> x9, starting transfers between devices: 5.96 us -> 12 us  [the longest x1 5.67 us: on_device(): off_in = lax.ppermute(off, 'group', across)]
    concatenate x3 -> x0, other arithmetic: 5.67 us -> none  [the longest x2 5.66 us: spread(): jnp.concatenate([own_blocks, incoming.reshape(-1, TILE, out_width), widen...]
  transfers between devices with their start and end apart: 4 -> 9, of which waited for: 2 -> 4; matrix products, arithmetic and copies ran while one was open for 2% -> 0% of each run, Pallas kernels for 0% -> 17%
where the time goes in v3:
time: 36.2 us; the launch traced here: 36 us
  waiting for transfers between devices  12.8 us (35%)
  starting transfers between devices  12 us (33%)
  Pallas kernels  7.62 us (21%)
  matrix products  1.77 us (5%)
  local copies, waits for them, and re-layouts  1.66 us (5%)
    pallas_call x8, Pallas kernels, call(): pl.pallas_call(kernel, out_shape=outputs, in_specs=specs, out_specs=[VMEM...  7.62 us
    ppermute x1, starting transfers between devices, on_device(): off_in = lax.ppermute(off, 'group', across)  5.67 us
    ppermute x3, waiting for transfers between devices, around(): lax.ppermute(value, 'inner', [(i, (i + k) % owners) for i in range(owners)])  4.86 us
    ppermute x3, starting transfers between devices, around(): lax.ppermute(value, 'inner', [(i, (i + k) % owners) for i in range(owners)])  4.61 us
    ppermute x1, waiting for transfers between devices, on_device(): asked_off = lax.ppermute(ask, 'group', across)  4.01 us
    ppermute x1, waiting for transfers between devices, on_device(): off_part = lax.ppermute(to_off, 'group', across)  3.94 us
    dot_general x1, matrix products, on_device(): product = jnp.dot(features, projection, preferred_element_type=F32)  1.77 us
    unnamed x14, local copies, waits for them, and re-layouts  1.66 us
  transfers between devices with their start and end apart: 9, of which 4 were waited for; matrix products, arithmetic and copies ran while one was open for 0% of the time, Pallas kernels for 17%

profile of v3, /device:TPU:0, one launch (start us, length us, event | category | flops | bytes accessed | tf_op | source)
XLA Modules:
  0.0 36.0 jit_solution(10880650715543945288)
XLA Ops:
  0.0 0.0 copy-start
  0.0 0.0 copy-start.3
  0.0 0.0 copy-start.5
  0.0 0.0 copy-start.2
  0.0 0.0 copy-start.4
  0.0 0.0 copy-start.6
  0.0 1.6 %copy-done = bf16[1536,768]{1,0:T(8,128)(2,1)S(1)} copy-done((bf16[1536,768]{1,0:T(8,128)(2,1)S(1)}, bf16[1536,768]{1,0:T(8,128)(2,1)}, u32[]{:S(2)}) %copy-start) | copy-done | bytes 2359320
  1.7 1.8 %fusion.product = f32[1536,256]{1,0:T(8,128)S(1)} fusion(bf16[1536,768]{1,0:T(8,128)(2,1)S(1)} %copy-done, bf16[768,256]{1,0:T(8,128)(2,1)} %param.11), kind=kOutput, calls=%fused_computation | convolution fusion | flops 603979776 | bytes 4325376 | tf_op jit(solution)/shard_map/dot_general | solution.py:318
  3.4 0.0 copy-start.1
  3.5 0.0 copy-done.3
  3.5 0.0 copy-done.5
  3.5 0.0 copy-done.2
  3.5 0.7 %first.1 = (bf16[12,128,256]{2,1,0:T(8,128)(2,1)S(1)}, bf16[1024,256]{1,0:T(8,128)(2,1)S(1)}, bf16[1024,256]{1,0:T(8,128)(2,1)S(1)}, bf16[256,256]{1,0:T(8,128)(2,1)S(1)}) custom-call(s32[1,2,8]{2,1,0:T(2,128)S(1)} %copy-done.3, s32[1,2,2]{2,1,0:T(2,128)S(1)} %copy-done.5, s32[12,128]{1,0:T(8,128)S(1)} %bitcast.4, f32[1536,256]{1,0:T(8,128)S(1)} %fusion.product), custom_call_target="tpu_custom_call" | custom-call | tf_op jit(solution)/shard_map/first/pallas_call | solution.py:282
  4.2 0.5 %collective-permute-start = (bf16[1024,256]{1,0:T(8,128)(2,1)S(1)}, bf16[1024,256]{1,0:T(8,128)(2,1)S(1)}, u32[]{:S(2)}, u32[]{:S(2)}) collective-permute-start(bf16[1024,256]{1,0:T(8,128)(2,1)S(1)} %get-tuple-element.25), channel_id=1, source_target_pairs={{0,2},{2,0},{4,6},{6,4},{8,10},{10,8},{12,14},{14,12},{16,18},{18,... | collective-permute-start | bytes 1572872 | tf_op jit(solution)/shard_map/ppermute | solution.py:330
  4.7 5.7 %collective-permute-start.3 = (bf16[1024,256]{1,0:T(8,128)(2,1)S(1)}, bf16[1024,256]{1,0:T(8,128)(2,1)S(1)}, u32[]{:S(2)}, u32[]{:S(2)}) collective-permute-start(bf16[1024,256]{1,0:T(8,128)(2,1)S(1)} %get-tuple-element.29), channel_id=1, source_target_pairs={{0,30},{2,4},{4,2},{6,8},{8,6},{10,12},{12,10},{14,16},{16,14},{18... | collective-permute-start | bytes 1572872 | tf_op jit(solution)/shard_map/ppermute | solution.py:328
  10.4 1.5 %collective-permute-start.1 = (bf16[256,256]{1,0:T(8,128)(2,1)S(1)}, bf16[256,256]{1,0:T(8,128)(2,1)S(1)}, u32[]{:S(2)}, u32[]{:S(2)}) collective-permute-start(bf16[256,256]{1,0:T(8,128)(2,1)S(1)} %get-tuple-element.27), channel_id=1, source_target_pairs={{0,1},{1,0},{2,3},{3,2},{4,5},{5,4},{6,7},{7,6},{8,9},{9,8},{10,11... | collective-permute-start | bytes 393224 | tf_op jit(solution)/shard_map/ppermute | solution.py:306
  11.9 0.0 collective-permute-done.after.on
  11.9 0.0 copy-done.4
  11.9 0.0 copy-done.6
  11.9 0.0 copy-done.1
  11.9 1.7 %ask.1 = (bf16[272,256]{1,0:T(8,128)(2,1)S(1)}, bf16[1536,1024]{1,0:T(8,128)(2,1)S(1)}, bf16[128,1536]{1,0:T(8,128)(2,1)S(1)}, f32[128,16]{1,0:T(8,128)S(1)}) custom-call(s32[4,12]{1,0:T(4,128)S(1)} %bitcast.6, s32[1,2,64]{2,1,0:T(2,128)S(1)} %copy-done.6, s32[12,128]{1,0:T(8,128)S(1)} %bitcast.5, bf16[1024,256]{1,0:T(8,128)(2,1)S(1)} %collective-permute-done.after.on, ...), custom_call_target="tpu_custom_call" | custom-call | tf_op jit(solution)/shard_map/ask/pallas_call | solution.py:282
  13.6 1.7 %collective-permute-done.1.rest_0_ = bf16[256,256]{1,0:T(8,128)(2,1)S(1)} collective-permute-done((bf16[256,256]{1,0:T(8,128)(2,1)S(1)}, bf16[256,256]{1,0:T(8,128)(2,1)S(1)}, u32[]{:S(2)}, u32[]{:S(2)}) %collective-permute-start.1) | collective-permute-done | bytes 131104 | tf_op jit(solution)/shard_map/ppermute | solution.py:306
  15.3 1.2 %near.1 = (f32[1536,256]{1,0:T(8,128)S(1)}, bf16[272,256]{1,0:T(8,128)(2,1)S(1)}) custom-call(s32[4,12]{1,0:T(4,128)S(1)} %bitcast.7, bf16[12,128,256]{2,1,0:T(8,128)(2,1)S(1)} %get-tuple-element.24.first, bf16[1536,512]{1,0:T(8,128)(2,1)S(1)} %copy-done.1, bf16[272,256]{1,0:T(8,128)(2,1)S(1)} %get-tuple-element.26.request, ...), custom_call_target="tpu_custom_call" | custom-call | tf_op jit(solution)/shard_map/near/pallas_call | solution.py:282
  16.5 0.1 collective-permute-start.2
  16.6 0.1 collective-permute-start.5
  16.7 1.6 %collective-permute-start.6 = (bf16[272,256]{1,0:T(8,128)(2,1)S(1)}, bf16[272,256]{1,0:T(8,128)(2,1)S(1)}, u32[]{:S(2)}, u32[]{:S(2)}) collective-permute-start(bf16[272,256]{1,0:T(8,128)(2,1)S(1)} %get-tuple-element.26.request), channel_id=1, source_target_pairs={{0,1},{1,0},{2,3},{3,2},{4,5},{5,4},{6,7},{7,6},{8,9},{9,8},{10,11... | collective-permute-start | bytes 417800 | tf_op jit(solution)/shard_map/ppermute | solution.py:306
  18.2 0.0 collective-permute-done.3.off
  18.2 1.5 %spread.1 = (bf16[1536,256]{1,0:T(8,128)(2,1)S(1)}, bf16[1536,256]{1,0:T(8,128)(2,1)S(1)}, bf16[1024,256]{1,0:T(8,128)(2,1)S(1)}) custom-call(s32[1,2,8]{2,1,0:T(2,128)S(1)} %copy-done.3, bf16[1024,256]{1,0:T(8,128)(2,1)S(1)} %collective-permute-done.3.off, f32[1536,256]{1,0:T(8,128)S(1)} %get-tuple-element.30.sums, ...), custom_call_target="tpu_custom_call" | custom-call | tf_op jit(solution)/shard_map/spread/pallas_call | solution.py:282
  19.7 4.0 %collective-permute-done.2.request = bf16[272,256]{1,0:T(8,128)(2,1)S(1)} collective-permute-done((bf16[272,256]{1,0:T(8,128)(2,1)S(1)}, bf16[272,256]{1,0:T(8,128)(2,1)S(1)}, u32[]{:S(2)}, u32[]{:S(2)}) %collective-permute-start.2) | collective-permute-done | bytes 139296 | tf_op jit(solution)/shard_map/ppermute | solution.py:354
  23.8 0.4 %answer.1 = bf16[128,256]{1,0:T(8,128)(2,1)S(1)} custom-call(bf16[272,256]{1,0:T(8,128)(2,1)S(1)} %collective-permute-done.2.request, bf16[1024,256]{1,0:T(8,128)(2,1)S(1)} %get-tuple-element.33.offered), custom_call_target="tpu_custom_call" | custom-call | tf_op jit(solution)/shard_map/answer/pallas_call | solution.py:282
  24.1 0.2 collective-permute-start.4
  24.3 0.0 collective-permute-done.5.on
  24.3 0.0 collective-permute-done.6.rest_0_
  24.3 1.5 %rest.1 = (bf16[128,256]{1,0:T(8,128)(2,1)S(1)}, f32[128,256]{1,0:T(8,128)S(1)}, bf16[128,256]{1,0:T(8,128)(2,1)S(1)}, bf16[128,256]{1,0:T(8,128)(2,1)S(1)}) custom-call(s32[1,2,8]{2,1,0:T(2,128)S(1)} %copy-done.3, s32[1,2,2]{2,1,0:T(2,128)S(1)} %copy-done.5, bf16[1536,256]{1,0:T(8,128)(2,1)S(1)} %get-tuple-element.34.second, ...), custom_call_target="tpu_custom_call" | custom-call | tf_op jit(solution)/shard_map/rest/pallas_call | solution.py:282
  25.8 0.8 %collective-permute-start.7 = (bf16[128,256]{1,0:T(8,128)(2,1)S(1)}, bf16[128,256]{1,0:T(8,128)(2,1)S(1)}, u32[]{:S(2)}, u32[]{:S(2)}) collective-permute-start(bf16[128,256]{1,0:T(8,128)(2,1)S(1)} %get-tuple-element.37), channel_id=1, source_target_pairs={{0,2},{2,0},{4,6},{6,4},{8,10},{10,8},{12,14},{14,12},{16,18},{18,... | collective-permute-start | bytes 196616 | tf_op jit(solution)/shard_map/ppermute | solution.py:380
  26.7 3.9 %collective-permute-done.4.off = bf16[128,256]{1,0:T(8,128)(2,1)S(1)} collective-permute-done((bf16[128,256]{1,0:T(8,128)(2,1)S(1)}, bf16[128,256]{1,0:T(8,128)(2,1)S(1)}, u32[]{:S(2)}, u32[]{:S(2)}) %collective-permute-start.4) | collective-permute-done | bytes 65568 | tf_op jit(solution)/shard_map/ppermute | solution.py:379
  30.6 0.0 collective-permute-done.7.on
  30.6 1.6 %collective-permute-start.8 = (bf16[3,64,256]{2,1,0:T(8,128)(2,1)S(1)}, bf16[3,64,256]{2,1,0:T(8,128)(2,1)S(1)}, u32[]{:S(2)}, u32[]{:S(2)}) collective-permute-start(bf16[3,64,256]{2,1,0:T(8,128)(2,1)S(1)} %get-tuple-element.42), channel_id=1, source_target_pairs={{0,1},{1,0},{2,3},{3,2},{4,5},{5,4},{6,7},{7,6},{8,9},{9,8},{10,11... | collective-permute-start | bytes 294920 | tf_op jit(solution)/shard_map/ppermute | solution.py:306
  32.2 3.1 %collective-permute-done.8.refs_1_ = bf16[3,64,256]{2,1,0:T(8,128)(2,1)S(1)} collective-permute-done((bf16[3,64,256]{2,1,0:T(8,128)(2,1)S(1)}, bf16[3,64,256]{2,1,0:T(8,128)(2,1)S(1)}, u32[]{:S(2)}, u32[]{:S(2)}) %collective-permute-start.8) | collective-permute-done | bytes 98336 | tf_op jit(solution)/shard_map/ppermute | solution.py:306
  35.3 0.7 %gather.1 = bf16[128,512]{1,0:T(8,128)(2,1)} custom-call(bf16[3,64,256]{2,1,0:T(8,128)(2,1)S(1)} %get-tuple-element.41.refs_0_, bf16[3,64,256]{2,1,0:T(8,128)(2,1)S(1)} %collective-permute-done.8.refs_1_), custom_call_target="tpu_custom_call" | custom-call | tf_op jit(solution)/shard_map/gather/pallas_call | solution.py:282
  (1 shorter events, 0.0 us)
Async XLA Ops:
  0.0 1.7 %copy-start = (bf16[1536,768]{1,0:T(8,128)(2,1)S(1)}, bf16[1536,768]{1,0:T(8,128)(2,1)}, u32[]{:S(2)}) copy-start(bf16[1536,768]{1,0:T(8,128)(2,1)} %param.10) | copy-start | bytes 7077892
  0.0 3.5 %copy-start.3 = (s32[1,2,8]{2,1,0:T(2,128)S(1)}, s32[1,2,8]{2,1,0:T(2,128)}, u32[]{:S(2)}) copy-start(s32[1,2,8]{2,1,0:T(2,128)} %edge_ids.5) | copy-start | bytes 196
  0.0 3.5 %copy-start.5 = (s32[1,2,2]{2,1,0:T(2,128)S(1)}, s32[1,2,2]{2,1,0:T(2,128)}, u32[]{:S(2)}) copy-start(s32[1,2,2]{2,1,0:T(2,128)} %send_ids.3) | copy-start | bytes 52
  0.0 3.5 %copy-start.2 = (s32[1536]{0:T(1024)S(1)}, s32[1536]{0:T(1024)}, u32[]{:S(2)}) copy-start(s32[1536]{0:T(1024)} %param.13) | copy-start | bytes 18436
  0.0 11.9 %copy-start.4 = (s32[12,4]{0,1:T(4,128)S(1)}, s32[12,4]{0,1:T(4,128)}, u32[]{:S(2)}) copy-start(s32[12,4]{0,1:T(4,128)} %param.14) | copy-start | bytes 580
  0.0 11.8 %copy-start.6 = (s32[1,2,64]{2,1,0:T(2,128)S(1)}, s32[1,2,64]{2,1,0:T(2,128)}, u32[]{:S(2)}) copy-start(s32[1,2,64]{2,1,0:T(2,128)} %train.1) | copy-start | bytes 1540
  3.4 8.4 %copy-start.1 = (bf16[1536,512]{1,0:T(8,128)(2,1)S(1)}, bf16[1536,512]{1,0:T(8,128)(2,1)}, u32[]{:S(2)}) copy-start(bf16[1536,512]{1,0:T(8,128)(2,1)} %adjacency.3) | copy-start | bytes 4718596
  4.2 7.7 %collective-permute-start = (bf16[1024,256]{1,0:T(8,128)(2,1)S(1)}, bf16[1024,256]{1,0:T(8,128)(2,1)S(1)}, u32[]{:S(2)}, u32[]{:S(2)}) collective-permute-start(bf16[1024,256]{1,0:T(8,128)(2,1)S(1)} %get-tuple-element.25), channel_id=1, source_target_pairs={{0,2},{2,0},{4,6},{6,4},{8,10},{10,8},{12,14},{14,12},{16,18},{18,... | collective-permute-start | bytes 1572872 | tf_op jit(solution)/shard_map/ppermute | solution.py:330
  4.7 13.5 %collective-permute-start.3 = (bf16[1024,256]{1,0:T(8,128)(2,1)S(1)}, bf16[1024,256]{1,0:T(8,128)(2,1)S(1)}, u32[]{:S(2)}, u32[]{:S(2)}) collective-permute-start(bf16[1024,256]{1,0:T(8,128)(2,1)S(1)} %get-tuple-element.29), channel_id=1, source_target_pairs={{0,30},{2,4},{4,2},{6,8},{8,6},{10,12},{12,10},{14,16},{16,14},{18... | collective-permute-start | bytes 1572872 | tf_op jit(solution)/shard_map/ppermute | solution.py:328
  10.4 5.0 %collective-permute-start.1 = (bf16[256,256]{1,0:T(8,128)(2,1)S(1)}, bf16[256,256]{1,0:T(8,128)(2,1)S(1)}, u32[]{:S(2)}, u32[]{:S(2)}) collective-permute-start(bf16[256,256]{1,0:T(8,128)(2,1)S(1)} %get-tuple-element.27), channel_id=1, source_target_pairs={{0,1},{1,0},{2,3},{3,2},{4,5},{5,4},{6,7},{7,6},{8,9},{9,8},{10,11... | collective-permute-start | bytes 393224 | tf_op jit(solution)/shard_map/ppermute | solution.py:306
  16.5 7.2 %collective-permute-start.2 = (bf16[272,256]{1,0:T(8,128)(2,1)S(1)}, bf16[272,256]{1,0:T(8,128)(2,1)S(1)}, u32[]{:S(2)}, u32[]{:S(2)}) collective-permute-start(bf16[272,256]{1,0:T(8,128)(2,1)S(1)} %get-tuple-element.28), channel_id=1, source_target_pairs={{0,30},{2,4},{4,2},{6,8},{8,6},{10,12},{12,10},{14,16},{16,14},{18... | collective-permute-start | bytes 417800 | tf_op jit(solution)/shard_map/ppermute | solution.py:354
  16.6 7.7 %collective-permute-start.5 = (bf16[272,256]{1,0:T(8,128)(2,1)S(1)}, bf16[272,256]{1,0:T(8,128)(2,1)S(1)}, u32[]{:S(2)}, u32[]{:S(2)}) collective-permute-start(bf16[272,256]{1,0:T(8,128)(2,1)S(1)} %get-tuple-element.26.request), channel_id=1, source_target_pairs={{0,2},{2,0},{4,6},{6,4},{8,10},{10,8},{12,14},{14,12},{16,18},{18,... | collective-permute-start | bytes 417800 | tf_op jit(solution)/shard_map/ppermute | solution.py:345
  16.7 7.7 %collective-permute-start.6 = (bf16[272,256]{1,0:T(8,128)(2,1)S(1)}, bf16[272,256]{1,0:T(8,128)(2,1)S(1)}, u32[]{:S(2)}, u32[]{:S(2)}) collective-permute-start(bf16[272,256]{1,0:T(8,128)(2,1)S(1)} %get-tuple-element.26.request), channel_id=1, source_target_pairs={{0,1},{1,0},{2,3},{3,2},{4,5},{5,4},{6,7},{7,6},{8,9},{9,8},{10,11... | collective-permute-start | bytes 417800 | tf_op jit(solution)/shard_map/ppermute | solution.py:306
  24.1 6.5 %collective-permute-start.4 = (bf16[128,256]{1,0:T(8,128)(2,1)S(1)}, bf16[128,256]{1,0:T(8,128)(2,1)S(1)}, u32[]{:S(2)}, u32[]{:S(2)}) collective-permute-start(bf16[128,256]{1,0:T(8,128)(2,1)S(1)} %answer.1), channel_id=1, source_target_pairs={{0,30},{2,4},{4,2},{6,8},{8,6},{10,12},{12,10},{14,16},{16,14},{18... | collective-permute-start | bytes 196616 | tf_op jit(solution)/shard_map/ppermute | solution.py:379
  25.8 4.8 %collective-permute-start.7 = (bf16[128,256]{1,0:T(8,128)(2,1)S(1)}, bf16[128,256]{1,0:T(8,128)(2,1)S(1)}, u32[]{:S(2)}, u32[]{:S(2)}) collective-permute-start(bf16[128,256]{1,0:T(8,128)(2,1)S(1)} %get-tuple-element.37), channel_id=1, source_target_pairs={{0,2},{2,0},{4,6},{6,4},{8,10},{10,8},{12,14},{14,12},{16,18},{18,... | collective-permute-start | bytes 196616 | tf_op jit(solution)/shard_map/ppermute | solution.py:380
  30.6 4.7 %collective-permute-start.8 = (bf16[3,64,256]{2,1,0:T(8,128)(2,1)S(1)}, bf16[3,64,256]{2,1,0:T(8,128)(2,1)S(1)}, u32[]{:S(2)}, u32[]{:S(2)}) collective-permute-start(bf16[3,64,256]{2,1,0:T(8,128)(2,1)S(1)} %get-tuple-element.42), channel_id=1, source_target_pairs={{0,1},{1,0},{2,3},{3,2},{4,5},{5,4},{6,7},{7,6},{8,9},{9,8},{10,11... | collective-permute-start | bytes 294920 | tf_op jit(solution)/shard_map/ppermute | solution.py:306

commit v4 on v3

--- a/solution.py
+++ b/solution.py
@@ -13,7 +13,7 @@
 CAPG = 8
 BF = jnp.bfloat16
 F32 = jnp.float32
-SPREAD_CHUNKS = 2
+SPREAD_CHUNKS = 3
 
 
 META = 16
@@ -54,21 +54,23 @@
     degrees[pl.ds(blocks, 16 - blocks), :] = jnp.ones((16 - blocks, TILE), jnp.int32)
 
 
-def first_kernel(edge_ids, send_ids, degree, product, first, off, on, *rest):
+def first_kernel(edge_ids, send_ids, degree, low, high, first, off, on, *rest):
     inner_out = rest[:-4]
     edge_s, send_s, degrees, sems = rest[-4:]
     blocks = first.shape[0]
     owners = len(inner_out) + 1
     parity = lax.rem(lax.axis_index("group"), 2)
     mine = lax.axis_index("inner")
-    arriving = fetch([(degree, degrees.at[pl.ds(0, blocks)]), (edge_ids, edge_s), (send_ids, send_s)], sems)
+    arriving = fetch([(edge_ids, edge_s), (send_ids, send_s), (degree, degrees.at[pl.ds(0, blocks)])], sems)
     fill_degrees(degrees, blocks)
+    arriving[2].wait()
+    roots = as_columns(lax.rsqrt(degrees[...].astype(F32)))
+    for part, rows in ((low, 0), (high, low.shape[0] // TILE)):
+        for b in range(part.shape[0] // TILE):
+            root = roots[:, rows + b : rows + b + 1]
+            first[rows + b] = (root * part[pl.ds(b * TILE, TILE), :]).astype(BF)
     arriving[0].wait()
-    roots = as_columns(lax.rsqrt(degrees[...].astype(F32)))
-    for b in range(blocks):
-        first[b] = (roots[:, b : b + 1] * product[pl.ds(b * TILE, TILE), :]).astype(BF)
     arriving[1].wait()
-    arriving[2].wait()
     for s in range(CAPG):
         off[pl.ds(s * TILE, TILE), :] = first[edge_s[0, parity, s]]
         on[pl.ds(s * TILE, TILE), :] = first[edge_s[0, 1 - parity, s]]
@@ -102,21 +104,21 @@
     return parts
 
 
-def ask_kernel(
-    tile_src, train, degree, after, adjacency, request, far, hot, roots, src_s, train_v, degrees, sems
-):
+def ask_kernel(tile_src, train, degree, after, adjacency, request, src_s, train_v, degrees, sems):
     blocks = degree.shape[0]
     owners = train.shape[1]
     count = owners * train.shape[2]
     width = request.shape[1]
-    parity = lax.rem(lax.axis_index("group"), 2)
-    off_base = blocks + owners * CAP + parity * CAPG
     arriving = fetch([(train, train_v), (tile_src, src_s), (degree, degrees.at[pl.ds(0, blocks)])], sems)
     fill_degrees(degrees, blocks)
-    far[...] = jnp.zeros_like(far)
-    for copy in arriving:
-        copy.wait()
-    roots[...] = as_columns(lax.rsqrt(degrees[...].astype(F32)))
+    arriving[0].wait()
+    hot = jnp.concatenate(one_hot_parts(train_v, blocks), axis=1)
+    picked = jnp.dot(hot, adjacency[...], preferred_element_type=F32).astype(BF)
+    strips = TPB * TILE // width
+    for h in range(strips):
+        request[pl.ds(h * count, count), :] = picked[:, h * width : (h + 1) * width]
+    arriving[1].wait()
+    arriving[2].wait()
     row = ids_row(train_v)
     block_of = lax.div(row, TILE)
     lane_hot = lax.broadcasted_iota(jnp.int32, (TILE, count), 0) == lax.rem(row, TILE)
@@ -135,13 +137,27 @@
     meta = jnp.concatenate(meta, axis=0)
     if count < width:
         meta = jnp.concatenate([meta, jnp.ones((META, width - count), F32)], axis=1)
-    strips = TPB * TILE // width
     request[pl.ds(strips * count, META), :] = meta.astype(BF)
+
+
+def far_kernel(
+    tile_src, train, degree, adjacency, request, far, hot, roots, wide, src_s, train_v, degrees, sems
+):
+    blocks = degree.shape[0]
+    owners = train.shape[1]
+    parity = lax.rem(lax.axis_index("group"), 2)
+    off_base = blocks + owners * CAP + parity * CAPG
+    arriving = fetch([(train, train_v), (tile_src, src_s), (degree, degrees.at[pl.ds(0, blocks)])], sems)
+    fill_degrees(degrees, blocks)
+    far[...] = jnp.zeros_like(far)
+    count, width = hot.shape[0], request.shape[1]
+    for b, part in enumerate(expanded(request, count, width, [float(b) for b in range(blocks)])):
+        wide[:, b * TILE : (b + 1) * TILE] = part
+    for copy in arriving:
+        copy.wait()
+    roots[...] = as_columns(lax.rsqrt(degrees[...].astype(F32)))
     for b, part in enumerate(one_hot_parts(train_v, blocks)):
         hot[:, b * TILE : (b + 1) * TILE] = part
-    picked = jnp.dot(hot[...], adjacency[...], preferred_element_type=F32).astype(BF)
-    for h in range(strips):
-        request[pl.ds(h * count, count), :] = picked[:, h * width : (h + 1) * width]
     for b in range(blocks):
         for t in range(TPB):
             slot = src_s[t, b] - off_base
@@ -179,7 +195,7 @@
         )
 
 
-def spread_kernel(edge_ids, off, sums, far, roots, second, hop, offered, edge_s, sem):
+def spread_kernel(edge_ids, off, sums, far, roots, second, hop, offered, offered_on, edge_s, sem):
     row_count = second.shape[0]
     parity = lax.rem(lax.axis_index("group"), 2)
     copy = pltpu.make_async_copy(edge_ids, edge_s, sem)
@@ -198,50 +214,47 @@
     for s in range(CAPG):
         block = pl.ds(pl.multiple_of(edge_s[0, parity, s] * TILE, TILE), TILE)
         offered[pl.ds(s * TILE, TILE), :] = second[block, :]
-
-
-def rest_kernel(edge_ids, send_ids, second, hop, hot, request, on, *rest):
+        block = pl.ds(pl.multiple_of(edge_s[0, 1 - parity, s] * TILE, TILE), TILE)
+        offered_on[pl.ds(s * TILE, TILE), :] = second[block, :]
+
+
+def rest_kernel(send_ids, second, hop, hot, wide, request, *rest):
     owners = send_ids.shape[1]
     inner_in = rest[: owners - 1]
-    to_on, own, picked, *peers = rest[owners - 1 : -4]
-    wide, edge_s, send_s, sems = rest[-4:]
+    own, picked, *peers = rest[owners - 1 : -2]
+    send_s, sem = rest[-2:]
     count = hot.shape[0]
     row_count, width = second.shape
     blocks = row_count // TILE
-    parity = lax.rem(lax.axis_index("group"), 2)
     mine = lax.axis_index("inner")
-    arriving = fetch([(edge_ids, edge_s), (send_ids, send_s)], sems)
-    wide[...] = jnp.zeros_like(wide)
-    parts = expanded(request, count, width, [float(b) for b in range(blocks)])
-    for b in range(blocks):
-        wide[pl.ds(0, count), b * TILE : (b + 1) * TILE] = parts[b]
+    copy = pltpu.make_async_copy(send_ids, send_s, sem)
+    copy.start()
+    total = jnp.dot(wide[...], second[...], preferred_element_type=F32)
+    own[...] = request_scale(request, count, width) * total
     picked[...] = jnp.dot(hot[...], hop[...], preferred_element_type=F32).astype(BF)
-    for copy in arriving:
-        copy.wait()
-    asked = [(on, CAPG, blocks + owners * CAP + parity * CAPG, lambda s: edge_s[0, 1 - parity, s])]
+    copy.wait()
     for k in range(1, owners):
         peer = lax.rem(mine - k + owners, owners)
-        asked.append((inner_in[k - 1], CAP, blocks + mine * CAP, lambda s, peer=peer: send_s[0, peer, s]))
-    for n, (message, slots, base, block) in enumerate(asked):
-        parts = expanded(message, count, width, [base + s for s in range(slots)])
-        for s in range(slots):
-            column = pl.multiple_of(block(s) * TILE, TILE)
-            wide[pl.ds((n + 1) * count, count), pl.ds(column, TILE)] = parts[s]
-    total = jnp.dot(wide[...], second[...], preferred_element_type=F32)
-    own[...] = request_scale(request, count, width) * total[0:count]
-    to_on[...] = (request_scale(on, count, width) * total[count : 2 * count]).astype(BF)
-    for k in range(1, owners):
-        part = total[(k + 1) * count : (k + 2) * count]
-        peers[k - 1][...] = (request_scale(inner_in[k - 1], count, width) * part).astype(BF)
-
-
-def answer_kernel(group_base, request, offered, to_off):
+        message = inner_in[k - 1]
+        base = blocks + mine * CAP
+        asked = jnp.concatenate(expanded(message, count, width, [base + s for s in range(CAP)]), axis=1)
+        offered = [
+            second[pl.ds(pl.multiple_of(send_s[0, peer, s] * TILE, TILE), TILE), :] for s in range(CAP)
+        ]
+        total = jnp.dot(asked, jnp.concatenate(offered, axis=0), preferred_element_type=F32)
+        peers[k - 1][...] = (request_scale(message, count, width) * total).astype(BF)
+
+
+def answer_kernel(group_base, off, offered, on, offered_on, to_off, to_on):
     count, width = to_off.shape
     parity = lax.rem(lax.axis_index("group"), 2)
-    base = group_base + (1 - parity) * CAPG
-    asked = jnp.concatenate(expanded(request, count, width, [base + s for s in range(CAPG)]), axis=1)
-    total = jnp.dot(asked, offered[...], preferred_element_type=F32)
-    to_off[...] = (request_scale(request, count, width) * total).astype(BF)
+    for request, rows, base, answer in (
+        (off, offered, group_base + (1 - parity) * CAPG, to_off),
+        (on, offered_on, group_base + parity * CAPG, to_on),
+    ):
+        asked = jnp.concatenate(expanded(request, count, width, [base + s for s in range(CAPG)]), axis=1)
+        total = jnp.dot(asked, rows[...], preferred_element_type=F32)
+        answer[...] = (request_scale(request, count, width) * total).astype(BF)
 
 
 def merge_kernel(owners, off, on, own, picked, *rest):
@@ -315,12 +328,15 @@
     degree_scratch = pltpu.VMEM((16, TILE), jnp.int32)
     dma = pltpu.SemaphoreType.DMA
 
-    product = jnp.dot(features, projection, preferred_element_type=F32)
+    cut = row_count // 2
+    low, high = [
+        jnp.dot(features[r], projection, preferred_element_type=F32) for r in (slice(0, cut), slice(cut, row_count))
+    ]
     first, off, on, *inner_out = call(
         first_kernel,
         "first",
-        (edge_ids, send_ids, degree, product),
-        [HBM] * 3 + [VMEM],
+        (edge_ids, send_ids, degree, low, high),
+        [HBM] * 3 + [VMEM] * 2,
         [array(blocks, TILE, width), array(CAPG * TILE, width), array(CAPG * TILE, width)]
         + [array(CAP * TILE, width)] * (owners - 1),
         [smem(edge_ids), smem(send_ids), degree_scratch, dma((3,))],
@@ -328,21 +344,28 @@
     off_in = lax.ppermute(off, "group", across)
     inner_in = [around(inner_out[k - 1], k) for k in range(1, owners)]
     on_in = lax.ppermute(on, "group", beside)
-    request, far, hot, roots = call(
+    (request,) = call(
         ask_kernel,
         "ask",
-        (tile_src, train_ids, degree, on_in, adjacency),
+        (tile_src, train_ids, degree, first, adjacency),
         [HBM] * 3 + [ANY, VMEM],
+        [array(tail, width)],
+        [smem(tile_src), train_scratch, degree_scratch, dma((3,))],
+    )
+    asked_off = lax.ppermute(request, "group", across)
+    far, hot, roots, wide = call(
+        far_kernel,
+        "far",
+        (tile_src, train_ids, degree, adjacency, request),
+        [HBM] * 3 + [VMEM] * 2,
         [
-            array(tail, width),
             array(row_count, CAPG * TILE),
             array(count, row_count),
             array(TILE, 16, kind=F32),
+            array(count, row_count),
         ],
         [smem(tile_src), train_scratch, degree_scratch, dma((3,))],
     )
-    asked_inner = [around(request, k) for k in range(1, owners)]
-    asked_on = lax.ppermute(request, "group", beside)
     sums, ask = call(
         near_kernel,
         "near",
@@ -351,30 +374,30 @@
         [array(row_count, width, kind=F32), array(tail, width)],
         [smem(tile_src), pltpu.VMEM((blocks + owners * CAP + 2 * CAPG, TILE, width), BF), dma((2,))],
     )
-    asked_off = lax.ppermute(ask, "group", across)
-    second, hop, offered = call(
+    asked_on = lax.ppermute(ask, "group", beside)
+    asked_inner = [around(ask, k) for k in range(1, owners)]
+    second, hop, offered, offered_on = call(
         spread_kernel,
         "spread",
         (edge_ids, off_in, sums, far, roots),
         [HBM] + [VMEM] * 4,
-        [array(row_count, width), array(row_count, width), array(CAPG * TILE, width)],
+        [array(row_count, width)] * 2 + [array(CAPG * TILE, width)] * 2,
         [smem(edge_ids), dma],
     )
-    (to_off,) = call(
+    to_off, to_on = call(
         functools.partial(answer_kernel, blocks + owners * CAP),
         "answer",
-        (asked_off, offered),
-        [VMEM] * 2,
-        [array(count, width)],
-    )
-    to_on, own, picked, *peers = call(
+        (asked_off, offered, asked_on, offered_on),
+        [VMEM] * 4,
+        [array(count, width)] * 2,
+    )
+    own, picked, *peers = call(
         rest_kernel,
         "rest",
-        (edge_ids, send_ids, second, hop, hot, request, asked_on, *asked_inner),
-        [HBM] * 2 + [VMEM] * (4 + owners),
-        [array(count, width), array(count, width, kind=F32), array(count, width)]
-        + [array(count, width)] * (owners - 1),
-        [pltpu.VMEM(((owners + 1) * count, row_count), BF), smem(edge_ids), smem(send_ids), dma((2,))],
+        (send_ids, second, hop, hot, wide, request, *asked_inner),
+        [HBM] + [VMEM] * (4 + owners),
+        [array(count, width, kind=F32)] + [array(count, width)] * owners,
+        [smem(send_ids), dma],
     )
     off_part = lax.ppermute(to_off, "group", across)
     on_part = lax.ppermute(to_on, "group", beside)

time: 36.2 us -> 33.6 us (0.928)
  waiting for transfers between devices: 12.8 us -> 7.68 us
  starting transfers between devices: 12 us -> 14.9 us
  local copies, waits for them, and re-layouts: 1.66 us -> 1.01 us
  matrix products: 1.77 us -> 2.21 us
    ppermute x2, waiting for transfers between devices: 4.02 us -> 0.01 us  [the longest x1 0.01 us: on_device(): asked_off = lax.ppermute(request, 'group', across)]
    ppermute x1, waiting for transfers between devices: 3.94 us -> 0.73 us  [on_device(): off_part = lax.ppermute(to_off, 'group', across)]
    ppermute x1, starting transfers between devices: 0.18 us -> 2.66 us  [on_device(): off_part = lax.ppermute(to_off, 'group', across)]
    ppermute x3, waiting for transfers between devices: 4.86 us -> 6.94 us  [around(): lax.ppermute(value, 'inner', [(i, (i + k) % owners) for i in range(owners)])]
    ppermute x1, starting transfers between devices: 0.85 us -> 2.05 us  [on_device(): on_part = lax.ppermute(to_on, 'group', beside)]
    ppermute x3, starting transfers between devices: 4.61 us -> 3.9 us  [around(): lax.ppermute(value, 'inner', [(i, (i + k) % owners) for i in range(owners)])]
    unnamed x14 -> x16, local copies, waits for them, and re-layouts: 1.66 us -> 1.01 us
    dot_general x1 -> x2, matrix products: 1.77 us -> 2.21 us  [on_device(): jnp.dot(features[r], projection, preferred_element_type=F32)]
  transfers between devices with their start and end apart: 9 -> 9, of which waited for: 4 -> 3; matrix products, arithmetic and copies ran while one was open for 0% -> 0% of each run, Pallas kernels for 17% -> 18%
where the time goes in v4:
time: 33.6 us; the launch traced here: 33.5 us
  starting transfers between devices  14.9 us (44%)
  waiting for transfers between devices  7.68 us (23%)
  Pallas kernels  7.44 us (22%)
  matrix products  2.21 us (7%)
  local copies, waits for them, and re-layouts  1.01 us (3%)
    pallas_call x9, Pallas kernels, call(): pl.pallas_call(kernel, out_shape=outputs, in_specs=specs, out_specs=[VMEM...  7.44 us
    ppermute x3, waiting for transfers between devices, around(): lax.ppermute(value, 'inner', [(i, (i + k) % owners) for i in range(owners)])  6.94 us
    ppermute x1, starting transfers between devices, on_device(): off_in = lax.ppermute(off, 'group', across)  5.67 us
    ppermute x3, starting transfers between devices, around(): lax.ppermute(value, 'inner', [(i, (i + k) % owners) for i in range(owners)])  3.9 us
    ppermute x1, starting transfers between devices, on_device(): off_part = lax.ppermute(to_off, 'group', across)  2.66 us
    dot_general x2, matrix products, on_device(): jnp.dot(features[r], projection, preferred_element_type=F32)  2.21 us
    ppermute x1, starting transfers between devices, on_device(): on_part = lax.ppermute(to_on, 'group', beside)  2.05 us
    unnamed x16, local copies, waits for them, and re-layouts  1.01 us
  transfers between devices with their start and end apart: 9, of which 3 were waited for; matrix products, arithmetic and copies ran while one was open for 0% of the time, Pallas kernels for 18%

profile of v4, /device:TPU:0, one launch (start us, length us, event | category | flops | bytes accessed | tf_op | source)
XLA Modules:
  0.0 33.5 jit_solution(9678949199837087029)
XLA Ops:
  0.0 0.0 copy-start
  0.0 0.0 copy-start.7
  0.0 0.0 copy-start.2
  0.0 0.0 copy-start.6
  0.0 0.0 copy-start.5
  0.0 1.0 %copy-done = bf16[768,256]{1,0:T(8,128)(2,1)S(1)} copy-done((bf16[768,256]{1,0:T(8,128)(2,1)S(1)}, bf16[768,256]{1,0:T(8,128)(2,1)}, u32[]{:S(2)}) %copy-start) | copy-done | bytes 393240
  1.0 1.7 %fusion.high = f32[768,256]{1,0:T(8,128)S(1)} fusion(bf16[768,256]{1,0:T(8,128)(2,1)S(1)} %copy-done, bf16[1536,768]{1,0:T(8,128)(2,1)} %param.10), kind=kOutput, calls=%fused_computation | convolution fusion | flops 301989888 | bytes 2359296 | tf_op jit(solution)/shard_map/dot_general | solution.py:333
  2.7 0.0 copy-done.7
  2.8 0.0 copy-start.1
  2.8 0.0 copy-start.3
  2.8 0.0 copy-start.4
  2.8 0.5 %fusion.2.low = f32[768,256]{1,0:T(8,128)S(1)} fusion(bf16[768,256]{1,0:T(8,128)(2,1)S(1)} %copy-done, bf16[1536,768]{1,0:T(8,128)(2,1)S(1)} %copy-done.7), kind=kOutput, calls=%fused_computation.2 | convolution fusion | flops 301989888 | bytes 2359296 | tf_op jit(solution)/shard_map/dot_general | solution.py:333
  3.3 0.0 copy-done.2
  3.3 0.0 copy-done.6
  3.3 0.0 copy-done.5
  3.3 0.7 %first.1 = (bf16[12,128,256]{2,1,0:T(8,128)(2,1)S(1)}, bf16[1024,256]{1,0:T(8,128)(2,1)S(1)}, bf16[1024,256]{1,0:T(8,128)(2,1)S(1)}, bf16[256,256]{1,0:T(8,128)(2,1)S(1)}) custom-call(s32[1,2,8]{2,1,0:T(2,128)S(1)} %copy-done.5, s32[1,2,2]{2,1,0:T(2,128)S(1)} %copy-done.6, s32[12,128]{1,0:T(8,128)S(1)} %bitcast.4, f32[768,256]{1,0:T(8,128)S(1)} %fusion.2.low, ...), custom_call_target="tpu_custom_call" | custom-call | tf_op jit(solution)/shard_map/first/pallas_call | solution.py:295
  4.0 0.5 %collective-permute-start.2 = (bf16[1024,256]{1,0:T(8,128)(2,1)S(1)}, bf16[1024,256]{1,0:T(8,128)(2,1)S(1)}, u32[]{:S(2)}, u32[]{:S(2)}) collective-permute-start(bf16[1024,256]{1,0:T(8,128)(2,1)S(1)} %get-tuple-element.28), channel_id=1, source_target_pairs={{0,2},{2,0},{4,6},{6,4},{8,10},{10,8},{12,14},{14,12},{16,18},{18,... | collective-permute-start | bytes 1572872 | tf_op jit(solution)/shard_map/ppermute | solution.py:346
  4.5 5.7 %collective-permute-start.1 = (bf16[1024,256]{1,0:T(8,128)(2,1)S(1)}, bf16[1024,256]{1,0:T(8,128)(2,1)S(1)}, u32[]{:S(2)}, u32[]{:S(2)}) collective-permute-start(bf16[1024,256]{1,0:T(8,128)(2,1)S(1)} %get-tuple-element.27), channel_id=1, source_target_pairs={{0,30},{2,4},{4,2},{6,8},{8,6},{10,12},{12,10},{14,16},{16,14},{18... | collective-permute-start | bytes 1572872 | tf_op jit(solution)/shard_map/ppermute | solution.py:344
  10.2 1.5 %collective-permute-start.3 = (bf16[256,256]{1,0:T(8,128)(2,1)S(1)}, bf16[256,256]{1,0:T(8,128)(2,1)S(1)}, u32[]{:S(2)}, u32[]{:S(2)}) collective-permute-start(bf16[256,256]{1,0:T(8,128)(2,1)S(1)} %get-tuple-element.29), channel_id=1, source_target_pairs={{0,1},{1,0},{2,3},{3,2},{4,5},{5,4},{6,7},{7,6},{8,9},{9,8},{10,11... | collective-permute-start | bytes 393224 | tf_op jit(solution)/shard_map/ppermute | solution.py:319
  11.7 0.0 copy-done.1
  11.7 0.0 copy-done.3
  11.7 0.0 copy-done.4
  11.7 0.8 %ask.1.request = bf16[272,256]{1,0:T(8,128)(2,1)S(1)} custom-call(s32[4,12]{1,0:T(4,128)S(1)} %bitcast.7, s32[1,2,64]{2,1,0:T(2,128)S(1)} %copy-done.4, s32[12,128]{1,0:T(8,128)S(1)} %bitcast.5, bf16[12,128,256]{2,1,0:T(8,128)(2,1)S(1)} %get-tuple-element.26.after.first, bf16[1536,512]{1,0:T(8,128)(2,1)S(1)} %copy-done.1), custom_call_target="tpu_custom_call" | custom-call | tf_op jit(solution)/shard_map/ask/pallas_call | solution.py:295
  12.5 0.1 collective-permute-start
  12.6 2.5 %collective-permute-done.3.rest_0_ = bf16[256,256]{1,0:T(8,128)(2,1)S(1)} collective-permute-done((bf16[256,256]{1,0:T(8,128)(2,1)S(1)}, bf16[256,256]{1,0:T(8,128)(2,1)S(1)}, u32[]{:S(2)}, u32[]{:S(2)}) %collective-permute-start.3) | collective-permute-done | bytes 131104 | tf_op jit(solution)/shard_map/ppermute | solution.py:319
  15.1 0.0 collective-permute-done.2.on
  15.1 1.2 %near.1 = (f32[1536,256]{1,0:T(8,128)S(1)}, bf16[272,256]{1,0:T(8,128)(2,1)S(1)}) custom-call(s32[4,12]{1,0:T(4,128)S(1)} %bitcast.8, bf16[12,128,256]{2,1,0:T(8,128)(2,1)S(1)} %get-tuple-element.26.after.first, bf16[1536,512]{1,0:T(8,128)(2,1)S(1)} %copy-done.1, bf16[272,256]{1,0:T(8,128)(2,1)S(1)} %ask.1.request, ...), custom_call_target="tpu_custom_call" | custom-call | tf_op jit(solution)/shard_map/near/pallas_call | solution.py:295
  16.3 0.1 collective-permute-start.4
  16.4 1.6 %collective-permute-start.7 = (bf16[272,256]{1,0:T(8,128)(2,1)S(1)}, bf16[272,256]{1,0:T(8,128)(2,1)S(1)}, u32[]{:S(2)}, u32[]{:S(2)}) collective-permute-start(bf16[272,256]{1,0:T(8,128)(2,1)S(1)} %get-tuple-element.34), channel_id=1, source_target_pairs={{0,1},{1,0},{2,3},{3,2},{4,5},{5,4},{6,7},{7,6},{8,9},{9,8},{10,11... | collective-permute-start | bytes 417800 | tf_op jit(solution)/shard_map/ppermute | solution.py:319
  18.0 1.4 %far.1 = (bf16[1536,1024]{1,0:T(8,128)(2,1)S(1)}, bf16[128,1536]{1,0:T(8,128)(2,1)S(1)}, f32[128,16]{1,0:T(8,128)S(1)}, bf16[128,1536]{1,0:T(8,128)(2,1)S(1)}) custom-call(s32[4,12]{1,0:T(4,128)S(1)} %bitcast.9, s32[1,2,64]{2,1,0:T(2,128)S(1)} %copy-done.4, s32[12,128]{1,0:T(8,128)S(1)} %bitcast.6, bf16[1536,512]{1,0:T(8,128)(2,1)S(1)} %copy-done.1, ...), custom_call_target="tpu_custom_call" | custom-call | tf_op jit(solution)/shard_map/far/pallas_call | solution.py:295
  19.3 0.0 collective-permute-done.1.off
  19.3 1.1 %spread.1 = (bf16[1536,256]{1,0:T(8,128)(2,1)S(1)}, bf16[1536,256]{1,0:T(8,128)(2,1)S(1)}, bf16[1024,256]{1,0:T(8,128)(2,1)S(1)}, bf16[1024,256]{1,0:T(8,128)(2,1)S(1)}) custom-call(s32[1,2,8]{2,1,0:T(2,128)S(1)} %copy-done.5, bf16[1024,256]{1,0:T(8,128)(2,1)S(1)} %collective-permute-done.1.off, f32[1536,256]{1,0:T(8,128)S(1)} %get-tuple-element.30.sums, ...), custom_call_target="tpu_custom_call" | custom-call | tf_op jit(solution)/shard_map/spread/pallas_call | solution.py:295
  20.5 0.0 collective-permute-done.off
  20.5 0.0 collective-permute-done.4.on
  20.5 0.5 %answer.1 = (bf16[128,256]{1,0:T(8,128)(2,1)S(1)}, bf16[128,256]{1,0:T(8,128)(2,1)S(1)}) custom-call(bf16[272,256]{1,0:T(8,128)(2,1)S(1)} %collective-permute-done.off, bf16[1024,256]{1,0:T(8,128)(2,1)S(1)} %get-tuple-element.33.offered, bf16[272,256]{1,0:T(8,128)(2,1)S(1)} %collective-permute-done.4.on, bf16[1024,256]{1,0:T(8,128)(2,1)S(1)} %get-tuple-element.35.offered_on), custom_call_target="tpu_custom_call" | custom-call | tf_op jit(solution)/shard_map/answer/pallas_call | solution.py:295
  21.0 2.7 %collective-permute-start.5 = (bf16[128,256]{1,0:T(8,128)(2,1)S(1)}, bf16[128,256]{1,0:T(8,128)(2,1)S(1)}, u32[]{:S(2)}, u32[]{:S(2)}) collective-permute-start(bf16[128,256]{1,0:T(8,128)(2,1)S(1)} %get-tuple-element.36), channel_id=1, source_target_pairs={{0,30},{2,4},{4,2},{6,8},{8,6},{10,12},{12,10},{14,16},{16,14},{18... | collective-permute-start | bytes 196616 | tf_op jit(solution)/shard_map/ppermute | solution.py:402
  23.7 2.1 %collective-permute-start.6 = (bf16[128,256]{1,0:T(8,128)(2,1)S(1)}, bf16[128,256]{1,0:T(8,128)(2,1)S(1)}, u32[]{:S(2)}, u32[]{:S(2)}) collective-permute-start(bf16[128,256]{1,0:T(8,128)(2,1)S(1)} %get-tuple-element.37), channel_id=1, source_target_pairs={{0,2},{2,0},{4,6},{6,4},{8,10},{10,8},{12,14},{14,12},{16,18},{18,... | collective-permute-start | bytes 196616 | tf_op jit(solution)/shard_map/ppermute | solution.py:403
  25.7 0.0 collective-permute-done.7.rest_0_
  25.7 1.0 %rest.1 = (f32[128,256]{1,0:T(8,128)S(1)}, bf16[128,256]{1,0:T(8,128)(2,1)S(1)}, bf16[128,256]{1,0:T(8,128)(2,1)S(1)}) custom-call(s32[1,2,2]{2,1,0:T(2,128)S(1)} %copy-done.6, bf16[1536,256]{1,0:T(8,128)(2,1)S(1)} %get-tuple-element.38.second, bf16[1536,256]{1,0:T(8,128)(2,1)S(1)} %get-tuple-element.39.hop, bf16[128,1536]{1,0:T(8,128)(2,1)S(1)} %get-tuple-element.40.hot, ...), custom_call_target="tpu_custom_call" | custom-call | tf_op jit(solution)/shard_map/rest/pallas_call | solution.py:295
  26.8 0.7 %collective-permute-done.5.off = bf16[128,256]{1,0:T(8,128)(2,1)S(1)} collective-permute-done((bf16[128,256]{1,0:T(8,128)(2,1)S(1)}, bf16[128,256]{1,0:T(8,128)(2,1)S(1)}, u32[]{:S(2)}, u32[]{:S(2)}) %collective-permute-start.5) | collective-permute-done | bytes 65568 | tf_op jit(solution)/shard_map/ppermute | solution.py:402
  27.5 0.0 collective-permute-done.6.on
  27.5 0.9 %collective-permute-start.8 = (bf16[3,64,256]{2,1,0:T(8,128)(2,1)S(1)}, bf16[3,64,256]{2,1,0:T(8,128)(2,1)S(1)}, u32[]{:S(2)}, u32[]{:S(2)}) collective-permute-start(bf16[3,64,256]{2,1,0:T(8,128)(2,1)S(1)} %get-tuple-element.46), channel_id=1, source_target_pairs={{0,1},{1,0},{2,3},{3,2},{4,5},{5,4},{6,7},{7,6},{8,9},{9,8},{10,11... | collective-permute-start | bytes 294920 | tf_op jit(solution)/shard_map/ppermute | solution.py:319
  28.4 4.4 %collective-permute-done.8.refs_1_ = bf16[3,64,256]{2,1,0:T(8,128)(2,1)S(1)} collective-permute-done((bf16[3,64,256]{2,1,0:T(8,128)(2,1)S(1)}, bf16[3,64,256]{2,1,0:T(8,128)(2,1)S(1)}, u32[]{:S(2)}, u32[]{:S(2)}) %collective-permute-start.8) | collective-permute-done | bytes 98336 | tf_op jit(solution)/shard_map/ppermute | solution.py:319
  32.8 0.7 %gather.1 = bf16[128,512]{1,0:T(8,128)(2,1)} custom-call(bf16[3,64,256]{2,1,0:T(8,128)(2,1)S(1)} %get-tuple-element.45.refs_0_, bf16[3,64,256]{2,1,0:T(8,128)(2,1)S(1)} %collective-permute-done.8.refs_1_), custom_call_target="tpu_custom_call" | custom-call | tf_op jit(solution)/shard_map/gather/pallas_call | solution.py:295
  (1 shorter events, 0.0 us)
Async XLA Ops:
  0.0 1.0 %copy-start = (bf16[768,256]{1,0:T(8,128)(2,1)S(1)}, bf16[768,256]{1,0:T(8,128)(2,1)}, u32[]{:S(2)}) copy-start(bf16[768,256]{1,0:T(8,128)(2,1)} %param.11) | copy-start | bytes 1179652
  0.0 2.7 %copy-start.7 = (bf16[1536,768]{1,0:T(8,128)(2,1)S(1)}, bf16[1536,768]{1,0:T(8,128)(2,1)}, u32[]{:S(2)}) copy-start(bf16[1536,768]{1,0:T(8,128)(2,1)} %param.10) | copy-start | bytes 7077892
  0.0 3.3 %copy-start.2 = (s32[1536]{0:T(1024)S(1)}, s32[1536]{0:T(1024)}, u32[]{:S(2)}) copy-start(s32[1536]{0:T(1024)} %param.13) | copy-start | bytes 18436
  0.0 3.3 %copy-start.6 = (s32[1,2,2]{2,1,0:T(2,128)S(1)}, s32[1,2,2]{2,1,0:T(2,128)}, u32[]{:S(2)}) copy-start(s32[1,2,2]{2,1,0:T(2,128)} %send_ids.3) | copy-start | bytes 52
  0.0 3.3 %copy-start.5 = (s32[1,2,8]{2,1,0:T(2,128)S(1)}, s32[1,2,8]{2,1,0:T(2,128)}, u32[]{:S(2)}) copy-start(s32[1,2,8]{2,1,0:T(2,128)} %edge_ids.3) | copy-start | bytes 196
  2.8 8.9 %copy-start.1 = (bf16[1536,512]{1,0:T(8,128)(2,1)S(1)}, bf16[1536,512]{1,0:T(8,128)(2,1)}, u32[]{:S(2)}) copy-start(bf16[1536,512]{1,0:T(8,128)(2,1)} %adjacency.5) | copy-start | bytes 4718596
  2.8 8.9 %copy-start.3 = (s32[12,4]{0,1:T(4,128)S(1)}, s32[12,4]{0,1:T(4,128)}, u32[]{:S(2)}) copy-start(s32[12,4]{0,1:T(4,128)} %param.14) | copy-start | bytes 580
  2.8 8.9 %copy-start.4 = (s32[1,2,64]{2,1,0:T(2,128)S(1)}, s32[1,2,64]{2,1,0:T(2,128)}, u32[]{:S(2)}) copy-start(s32[1,2,64]{2,1,0:T(2,128)} %train.3) | copy-start | bytes 1540
  4.0 11.2 %collective-permute-start.2 = (bf16[1024,256]{1,0:T(8,128)(2,1)S(1)}, bf16[1024,256]{1,0:T(8,128)(2,1)S(1)}, u32[]{:S(2)}, u32[]{:S(2)}) collective-permute-start(bf16[1024,256]{1,0:T(8,128)(2,1)S(1)} %get-tuple-element.28), channel_id=1, source_target_pairs={{0,2},{2,0},{4,6},{6,4},{8,10},{10,8},{12,14},{14,12},{16,18},{18,... | collective-permute-start | bytes 1572872 | tf_op jit(solution)/shard_map/ppermute | solution.py:346
  4.5 14.8 %collective-permute-start.1 = (bf16[1024,256]{1,0:T(8,128)(2,1)S(1)}, bf16[1024,256]{1,0:T(8,128)(2,1)S(1)}, u32[]{:S(2)}, u32[]{:S(2)}) collective-permute-start(bf16[1024,256]{1,0:T(8,128)(2,1)S(1)} %get-tuple-element.27), channel_id=1, source_target_pairs={{0,30},{2,4},{4,2},{6,8},{8,6},{10,12},{12,10},{14,16},{16,14},{18... | collective-permute-start | bytes 1572872 | tf_op jit(solution)/shard_map/ppermute | solution.py:344
  10.2 5.0 %collective-permute-start.3 = (bf16[256,256]{1,0:T(8,128)(2,1)S(1)}, bf16[256,256]{1,0:T(8,128)(2,1)S(1)}, u32[]{:S(2)}, u32[]{:S(2)}) collective-permute-start(bf16[256,256]{1,0:T(8,128)(2,1)S(1)} %get-tuple-element.29), channel_id=1, source_target_pairs={{0,1},{1,0},{2,3},{3,2},{4,5},{5,4},{6,7},{7,6},{8,9},{9,8},{10,11... | collective-permute-start | bytes 393224 | tf_op jit(solution)/shard_map/ppermute | solution.py:319
  12.5 7.9 %collective-permute-start = (bf16[272,256]{1,0:T(8,128)(2,1)S(1)}, bf16[272,256]{1,0:T(8,128)(2,1)S(1)}, u32[]{:S(2)}, u32[]{:S(2)}) collective-permute-start(bf16[272,256]{1,0:T(8,128)(2,1)S(1)} %ask.1.request), channel_id=1, source_target_pairs={{0,30},{2,4},{4,2},{6,8},{8,6},{10,12},{12,10},{14,16},{16,14},{18... | collective-permute-start | bytes 417800 | tf_op jit(solution)/shard_map/ppermute | solution.py:355
  16.3 4.2 %collective-permute-start.4 = (bf16[272,256]{1,0:T(8,128)(2,1)S(1)}, bf16[272,256]{1,0:T(8,128)(2,1)S(1)}, u32[]{:S(2)}, u32[]{:S(2)}) collective-permute-start(bf16[272,256]{1,0:T(8,128)(2,1)S(1)} %get-tuple-element.34), channel_id=1, source_target_pairs={{0,2},{2,0},{4,6},{6,4},{8,10},{10,8},{12,14},{14,12},{16,18},{18,... | collective-permute-start | bytes 417800 | tf_op jit(solution)/shard_map/ppermute | solution.py:377
  16.4 9.3 %collective-permute-start.7 = (bf16[272,256]{1,0:T(8,128)(2,1)S(1)}, bf16[272,256]{1,0:T(8,128)(2,1)S(1)}, u32[]{:S(2)}, u32[]{:S(2)}) collective-permute-start(bf16[272,256]{1,0:T(8,128)(2,1)S(1)} %get-tuple-element.34), channel_id=1, source_target_pairs={{0,1},{1,0},{2,3},{3,2},{4,5},{5,4},{6,7},{7,6},{8,9},{9,8},{10,11... | collective-permute-start | bytes 417800 | tf_op jit(solution)/shard_map/ppermute | solution.py:319
  21.0 6.5 %collective-permute-start.5 = (bf16[128,256]{1,0:T(8,128)(2,1)S(1)}, bf16[128,256]{1,0:T(8,128)(2,1)S(1)}, u32[]{:S(2)}, u32[]{:S(2)}) collective-permute-start(bf16[128,256]{1,0:T(8,128)(2,1)S(1)} %get-tuple-element.36), channel_id=1, source_target_pairs={{0,30},{2,4},{4,2},{6,8},{8,6},{10,12},{12,10},{14,16},{16,14},{18... | collective-permute-start | bytes 196616 | tf_op jit(solution)/shard_map/ppermute | solution.py:402
  23.7 3.8 %collective-permute-start.6 = (bf16[128,256]{1,0:T(8,128)(2,1)S(1)}, bf16[128,256]{1,0:T(8,128)(2,1)S(1)}, u32[]{:S(2)}, u32[]{:S(2)}) collective-permute-start(bf16[128,256]{1,0:T(8,128)(2,1)S(1)} %get-tuple-element.37), channel_id=1, source_target_pairs={{0,2},{2,0},{4,6},{6,4},{8,10},{10,8},{12,14},{14,12},{16,18},{18,... | collective-permute-start | bytes 196616 | tf_op jit(solution)/shard_map/ppermute | solution.py:403
  27.5 5.3 %collective-permute-start.8 = (bf16[3,64,256]{2,1,0:T(8,128)(2,1)S(1)}, bf16[3,64,256]{2,1,0:T(8,128)(2,1)S(1)}, u32[]{:S(2)}, u32[]{:S(2)}) collective-permute-start(bf16[3,64,256]{2,1,0:T(8,128)(2,1)S(1)} %get-tuple-element.46), channel_id=1, source_target_pairs={{0,1},{1,0},{2,3},{3,2},{4,5},{5,4},{6,7},{7,6},{8,9},{9,8},{10,11... | collective-permute-start | bytes 294920 | tf_op jit(solution)/shard_map/ppermute | solution.py:319

commit v5 on v4

--- a/solution.py
+++ b/solution.py
@@ -54,7 +54,7 @@
     degrees[pl.ds(blocks, 16 - blocks), :] = jnp.ones((16 - blocks, TILE), jnp.int32)
 
 
-def first_kernel(edge_ids, send_ids, degree, low, high, first, off, on, *rest):
+def first_kernel(edge_ids, send_ids, degree, projection, features, head, first, off, on, *rest):
     inner_out = rest[:-4]
     edge_s, send_s, degrees, sems = rest[-4:]
     blocks = first.shape[0]
@@ -65,10 +65,14 @@
     fill_degrees(degrees, blocks)
     arriving[2].wait()
     roots = as_columns(lax.rsqrt(degrees[...].astype(F32)))
-    for part, rows in ((low, 0), (high, low.shape[0] // TILE)):
-        for b in range(part.shape[0] // TILE):
-            root = roots[:, rows + b : rows + b + 1]
-            first[rows + b] = (root * part[pl.ds(b * TILE, TILE), :]).astype(BF)
+    done = head.shape[0] // TILE
+    for b in range(done):
+        first[b] = (roots[:, b : b + 1] * head[pl.ds(b * TILE, TILE), :]).astype(BF)
+    product = jnp.dot(
+        features[pl.ds(done * TILE, (blocks - done) * TILE), :], projection[...], preferred_element_type=F32
+    )
+    for b in range(done, blocks):
+        first[b] = (roots[:, b : b + 1] * product[(b - done) * TILE : (b - done + 1) * TILE]).astype(BF)
     arriving[0].wait()
     arriving[1].wait()
     for s in range(CAPG):
@@ -141,7 +145,7 @@
 
 
 def far_kernel(
-    tile_src, train, degree, adjacency, request, far, hot, roots, wide, src_s, train_v, degrees, sems
+    tile_src, train, degree, adjacency, request, far, hot, roots, wide, ask, src_s, train_v, degrees, sems
 ):
     blocks = degree.shape[0]
     owners = train.shape[1]
@@ -151,6 +155,7 @@
     fill_degrees(degrees, blocks)
     far[...] = jnp.zeros_like(far)
     count, width = hot.shape[0], request.shape[1]
+    ask[...] = request[...]
     for b, part in enumerate(expanded(request, count, width, [float(b) for b in range(blocks)])):
         wide[:, b * TILE : (b + 1) * TILE] = part
     for copy in arriving:
@@ -328,15 +333,12 @@
     degree_scratch = pltpu.VMEM((16, TILE), jnp.int32)
     dma = pltpu.SemaphoreType.DMA
 
-    cut = row_count // 2
-    low, high = [
-        jnp.dot(features[r], projection, preferred_element_type=F32) for r in (slice(0, cut), slice(cut, row_count))
-    ]
+    head = jnp.dot(features[: blocks * 7 // 12 * TILE], projection, preferred_element_type=F32)
     first, off, on, *inner_out = call(
         first_kernel,
         "first",
-        (edge_ids, send_ids, degree, low, high),
-        [HBM] * 3 + [VMEM] * 2,
+        (edge_ids, send_ids, degree, projection, features, head),
+        [HBM] * 3 + [VMEM] * 3,
         [array(blocks, TILE, width), array(CAPG * TILE, width), array(CAPG * TILE, width)]
         + [array(CAP * TILE, width)] * (owners - 1),
         [smem(edge_ids), smem(send_ids), degree_scratch, dma((3,))],
@@ -353,7 +355,7 @@
         [smem(tile_src), train_scratch, degree_scratch, dma((3,))],
     )
     asked_off = lax.ppermute(request, "group", across)
-    far, hot, roots, wide = call(
+    far, hot, roots, wide, ask = call(
         far_kernel,
         "far",
         (tile_src, train_ids, degree, adjacency, request),
@@ -363,13 +365,14 @@
             array(count, row_count),
             array(TILE, 16, kind=F32),
             array(count, row_count),
+            array(tail, width),
         ],
         [smem(tile_src), train_scratch, degree_scratch, dma((3,))],
     )
     sums, ask = call(
         near_kernel,
         "near",
-        (tile_src, first, adjacency, request, on_in, *inner_in),
+        (tile_src, first, adjacency, ask, on_in, *inner_in),
         [HBM] * 2 + [VMEM] * (2 + owners),
         [array(row_count, width, kind=F32), array(tail, width)],
         [smem(tile_src), pltpu.VMEM((blocks + owners * CAP + 2 * CAPG, TILE, width), BF), dma((2,))],

time: 33.6 us -> 32.2 us (0.958)
  waiting for transfers between devices: 7.68 us -> 6.14 us
  starting transfers between devices: 14.9 us -> 16.2 us
  local copies, waits for them, and re-layouts: 1.01 us -> 0.13 us
    ppermute x3, waiting for transfers between devices: 6.94 us -> 5.22 us  [around(): lax.ppermute(value, 'inner', [(i, (i + k) % owners) for i in range(owners)])]
    unnamed x16, local copies, waits for them, and re-layouts: 1.01 us -> 0.13 us
    ppermute x1, waiting for transfers between devices: 0.01 us -> 0.81 us  [on_device(): asked_off = lax.ppermute(request, 'group', across)]
    ppermute x1, waiting for transfers between devices: 0.73 us -> 0.1 us  [on_device(): off_part = lax.ppermute(to_off, 'group', across)]
    ppermute x3, starting transfers between devices: 3.9 us -> 4.53 us  [around(): lax.ppermute(value, 'inner', [(i, (i + k) % owners) for i in range(owners)])]
    ppermute x1, starting transfers between devices: 2.66 us -> 3.26 us  [on_device(): off_part = lax.ppermute(to_off, 'group', across)]
    dot_general x2 -> x1, matrix products: 2.21 us -> 2.08 us  [on_device(): jnp.dot(features[:blocks * 7 // 12 * TILE], projection, preferred_element...]
  transfers between devices with their start and end apart: 9 -> 9, of which waited for: 3 -> 4; matrix products, arithmetic and copies ran while one was open for 0% -> 0% of each run, Pallas kernels for 18% -> 19%
where the time goes in v5:
time: 32.2 us; the launch traced here: 32.1 us
  starting transfers between devices  16.2 us (50%)
  Pallas kernels  7.46 us (23%)
  waiting for transfers between devices  6.14 us (19%)
  matrix products  2.08 us (6%)
    pallas_call x9, Pallas kernels, call(): pl.pallas_call(kernel, out_shape=outputs, in_specs=specs, out_specs=[VMEM...  7.46 us
    ppermute x1, starting transfers between devices, on_device(): off_in = lax.ppermute(off, 'group', across)  5.67 us
    ppermute x3, waiting for transfers between devices, around(): lax.ppermute(value, 'inner', [(i, (i + k) % owners) for i in range(owners)])  5.22 us
    ppermute x3, starting transfers between devices, around(): lax.ppermute(value, 'inner', [(i, (i + k) % owners) for i in range(owners)])  4.53 us
    ppermute x1, starting transfers between devices, on_device(): off_part = lax.ppermute(to_off, 'group', across)  3.26 us
    dot_general x1, matrix products, on_device(): jnp.dot(features[:blocks * 7 // 12 * TILE], projection, preferred_element...  2.08 us
    ppermute x1, starting transfers between devices, on_device(): on_part = lax.ppermute(to_on, 'group', beside)  2.05 us
    ppermute x1, waiting for transfers between devices, on_device(): asked_off = lax.ppermute(request, 'group', across)  0.81 us
  transfers between devices with their start and end apart: 9, of which 4 were waited for; matrix products, arithmetic and copies ran while one was open for 0% of the time, Pallas kernels for 19%

profile of v5, /device:TPU:0, one launch (start us, length us, event | category | flops | bytes accessed | tf_op | source)
XLA Modules:
  0.0 32.1 jit_solution(9494264837944689598)
XLA Ops:
  0.0 0.0 copy-start.1
  0.0 0.0 copy-start.2
  0.0 0.0 copy-start.3
  0.0 0.0 copy-start.7
  0.0 0.0 copy-start.6
  0.0 2.1 %fusion.head = f32[896,256]{1,0:T(8,128)S(1)} fusion(bf16[768,256]{1,0:T(8,128)(2,1)} %projection.1, bf16[1536,768]{1,0:T(8,128)(2,1)} %features.1), kind=kOutput, calls=%fused_computation | convolution fusion | flops 352321536 | bytes 2686976 | tf_op jit(solution)/shard_map/dot_general | solution.py:336
  2.1 0.0 copy-start
  2.1 0.0 copy-start.4
  2.1 0.0 copy-start.5
  2.1 0.1 copy-done.1
  2.2 0.0 copy-done.2
  2.2 0.0 copy-done.3
  2.2 0.0 copy-done.7
  2.2 0.0 copy-done.6
  2.2 0.7 %first.1 = (bf16[12,128,256]{2,1,0:T(8,128)(2,1)S(1)}, bf16[1024,256]{1,0:T(8,128)(2,1)S(1)}, bf16[1024,256]{1,0:T(8,128)(2,1)S(1)}, bf16[256,256]{1,0:T(8,128)(2,1)S(1)}) custom-call(s32[1,2,8]{2,1,0:T(2,128)S(1)} %copy-done.6, s32[1,2,2]{2,1,0:T(2,128)S(1)} %copy-done.7, s32[12,128]{1,0:T(8,128)S(1)} %bitcast.3, bf16[768,256]{1,0:T(8,128)(2,1)S(1)} %copy-done.2, ...), custom_call_target="tpu_custom_call" | custom-call | tf_op jit(solution)/shard_map/first/pallas_call | solution.py:300
  2.9 0.5 %collective-permute-start.2 = (bf16[1024,256]{1,0:T(8,128)(2,1)S(1)}, bf16[1024,256]{1,0:T(8,128)(2,1)S(1)}, u32[]{:S(2)}, u32[]{:S(2)}) collective-permute-start(bf16[1024,256]{1,0:T(8,128)(2,1)S(1)} %get-tuple-element.30), channel_id=1, source_target_pairs={{0,2},{2,0},{4,6},{6,4},{8,10},{10,8},{12,14},{14,12},{16,18},{18,... | collective-permute-start | bytes 1572872 | tf_op jit(solution)/shard_map/ppermute | solution.py:348
  3.4 5.7 %collective-permute-start.1 = (bf16[1024,256]{1,0:T(8,128)(2,1)S(1)}, bf16[1024,256]{1,0:T(8,128)(2,1)S(1)}, u32[]{:S(2)}, u32[]{:S(2)}) collective-permute-start(bf16[1024,256]{1,0:T(8,128)(2,1)S(1)} %get-tuple-element.28), channel_id=1, source_target_pairs={{0,30},{2,4},{4,2},{6,8},{8,6},{10,12},{12,10},{14,16},{16,14},{18... | collective-permute-start | bytes 1572872 | tf_op jit(solution)/shard_map/ppermute | solution.py:346
  9.1 1.5 %collective-permute-start.3 = (bf16[256,256]{1,0:T(8,128)(2,1)S(1)}, bf16[256,256]{1,0:T(8,128)(2,1)S(1)}, u32[]{:S(2)}, u32[]{:S(2)}) collective-permute-start(bf16[256,256]{1,0:T(8,128)(2,1)S(1)} %get-tuple-element.31), channel_id=1, source_target_pairs={{0,1},{1,0},{2,3},{3,2},{4,5},{5,4},{6,7},{7,6},{8,9},{9,8},{10,11... | collective-permute-start | bytes 393224 | tf_op jit(solution)/shard_map/ppermute | solution.py:324
  10.6 0.0 copy-done
  10.6 0.0 copy-done.4
  10.6 0.0 copy-done.5
  10.6 0.8 %ask.1.request = bf16[272,256]{1,0:T(8,128)(2,1)S(1)} custom-call(s32[4,12]{1,0:T(4,128)S(1)} %bitcast.6, s32[1,2,64]{2,1,0:T(2,128)S(1)} %copy-done.5, s32[12,128]{1,0:T(8,128)S(1)} %bitcast.4, bf16[12,128,256]{2,1,0:T(8,128)(2,1)S(1)} %get-tuple-element.27.after.first, bf16[1536,512]{1,0:T(8,128)(2,1)S(1)} %copy-done), custom_call_target="tpu_custom_call" | custom-call | tf_op jit(solution)/shard_map/ask/pallas_call | solution.py:300
  11.5 0.1 collective-permute-start
  11.5 1.4 %far.1 = (bf16[1536,1024]{1,0:T(8,128)(2,1)S(1)}, bf16[128,1536]{1,0:T(8,128)(2,1)S(1)}, f32[128,16]{1,0:T(8,128)S(1)}, bf16[128,1536]{1,0:T(8,128)(2,1)S(1)}, bf16[272,256]{1,0:T(8,128)(2,1)S(1)}) custom-call(s32[4,12]{1,0:T(4,128)S(1)} %bitcast.7, s32[1,2,64]{2,1,0:T(2,128)S(1)} %copy-done.5, s32[12,128]{1,0:T(8,128)S(1)} %bitcast.5, ...), custom_call_target="tpu_custom_call" | custom-call | tf_op jit(solution)/shard_map/far/pallas_call | solution.py:300
  12.9 1.1 %collective-permute-done.3.rest_0_ = bf16[256,256]{1,0:T(8,128)(2,1)S(1)} collective-permute-done((bf16[256,256]{1,0:T(8,128)(2,1)S(1)}, bf16[256,256]{1,0:T(8,128)(2,1)S(1)}, u32[]{:S(2)}, u32[]{:S(2)}) %collective-permute-start.3) | collective-permute-done | bytes 131104 | tf_op jit(solution)/shard_map/ppermute | solution.py:324
  14.1 0.0 collective-permute-done.2.on
  14.1 1.2 %near.1 = (f32[1536,256]{1,0:T(8,128)S(1)}, bf16[272,256]{1,0:T(8,128)(2,1)S(1)}) custom-call(s32[4,12]{1,0:T(4,128)S(1)} %bitcast.8, bf16[12,128,256]{2,1,0:T(8,128)(2,1)S(1)} %get-tuple-element.27.after.first, bf16[1536,512]{1,0:T(8,128)(2,1)S(1)} %copy-done, bf16[272,256]{1,0:T(8,128)(2,1)S(1)} %get-tuple-element.29.request, ...), custom_call_target="tpu_custom_call" | custom-call | tf_op jit(solution)/shard_map/near/pallas_call | solution.py:300
  15.3 0.1 collective-permute-start.4
  15.3 1.6 %collective-permute-start.7 = (bf16[272,256]{1,0:T(8,128)(2,1)S(1)}, bf16[272,256]{1,0:T(8,128)(2,1)S(1)}, u32[]{:S(2)}, u32[]{:S(2)}) collective-permute-start(bf16[272,256]{1,0:T(8,128)(2,1)S(1)} %get-tuple-element.36), channel_id=1, source_target_pairs={{0,1},{1,0},{2,3},{3,2},{4,5},{5,4},{6,7},{7,6},{8,9},{9,8},{10,11... | collective-permute-start | bytes 417800 | tf_op jit(solution)/shard_map/ppermute | solution.py:324
  16.9 0.0 collective-permute-done.1.off
  16.9 1.1 %spread.1 = (bf16[1536,256]{1,0:T(8,128)(2,1)S(1)}, bf16[1536,256]{1,0:T(8,128)(2,1)S(1)}, bf16[1024,256]{1,0:T(8,128)(2,1)S(1)}, bf16[1024,256]{1,0:T(8,128)(2,1)S(1)}) custom-call(s32[1,2,8]{2,1,0:T(2,128)S(1)} %copy-done.6, bf16[1024,256]{1,0:T(8,128)(2,1)S(1)} %collective-permute-done.1.off, f32[1536,256]{1,0:T(8,128)S(1)} %get-tuple-element.32.sums, ...), custom_call_target="tpu_custom_call" | custom-call | tf_op jit(solution)/shard_map/spread/pallas_call | solution.py:300
  18.0 0.8 %collective-permute-done.off = bf16[272,256]{1,0:T(8,128)(2,1)S(1)} collective-permute-done((bf16[272,256]{1,0:T(8,128)(2,1)S(1)}, bf16[272,256]{1,0:T(8,128)(2,1)S(1)}, u32[]{:S(2)}, u32[]{:S(2)}) %collective-permute-start) | collective-permute-done | bytes 139296 | tf_op jit(solution)/shard_map/ppermute | solution.py:357
  18.8 0.0 collective-permute-done.4.on
  18.8 0.5 %answer.1 = (bf16[128,256]{1,0:T(8,128)(2,1)S(1)}, bf16[128,256]{1,0:T(8,128)(2,1)S(1)}) custom-call(bf16[272,256]{1,0:T(8,128)(2,1)S(1)} %collective-permute-done.off, bf16[1024,256]{1,0:T(8,128)(2,1)S(1)} %get-tuple-element.35.offered, bf16[272,256]{1,0:T(8,128)(2,1)S(1)} %collective-permute-done.4.on, bf16[1024,256]{1,0:T(8,128)(2,1)S(1)} %get-tuple-element.37.offered_on), custom_call_target="tpu_custom_call" | custom-call | tf_op jit(solution)/shard_map/answer/pallas_call | solution.py:300
  19.4 3.3 %collective-permute-start.5 = (bf16[128,256]{1,0:T(8,128)(2,1)S(1)}, bf16[128,256]{1,0:T(8,128)(2,1)S(1)}, u32[]{:S(2)}, u32[]{:S(2)}) collective-permute-start(bf16[128,256]{1,0:T(8,128)(2,1)S(1)} %get-tuple-element.38), channel_id=1, source_target_pairs={{0,30},{2,4},{4,2},{6,8},{8,6},{10,12},{12,10},{14,16},{16,14},{18... | collective-permute-start | bytes 196616 | tf_op jit(solution)/shard_map/ppermute | solution.py:405
  22.6 2.1 %collective-permute-start.6 = (bf16[128,256]{1,0:T(8,128)(2,1)S(1)}, bf16[128,256]{1,0:T(8,128)(2,1)S(1)}, u32[]{:S(2)}, u32[]{:S(2)}) collective-permute-start(bf16[128,256]{1,0:T(8,128)(2,1)S(1)} %get-tuple-element.39), channel_id=1, source_target_pairs={{0,2},{2,0},{4,6},{6,4},{8,10},{10,8},{12,14},{14,12},{16,18},{18,... | collective-permute-start | bytes 196616 | tf_op jit(solution)/shard_map/ppermute | solution.py:406
  24.7 0.0 collective-permute-done.7.rest_0_
  24.7 1.0 %rest.1 = (f32[128,256]{1,0:T(8,128)S(1)}, bf16[128,256]{1,0:T(8,128)(2,1)S(1)}, bf16[128,256]{1,0:T(8,128)(2,1)S(1)}) custom-call(s32[1,2,2]{2,1,0:T(2,128)S(1)} %copy-done.7, bf16[1536,256]{1,0:T(8,128)(2,1)S(1)} %get-tuple-element.40.second, bf16[1536,256]{1,0:T(8,128)(2,1)S(1)} %get-tuple-element.41.hop, bf16[128,1536]{1,0:T(8,128)(2,1)S(1)} %get-tuple-element.42.hot, ...), custom_call_target="tpu_custom_call" | custom-call | tf_op jit(solution)/shard_map/rest/pallas_call | solution.py:300
  25.7 0.1 collective-permute-done.5.off
  25.8 0.0 collective-permute-done.6.on
  25.9 1.5 %collective-permute-start.8 = (bf16[3,64,256]{2,1,0:T(8,128)(2,1)S(1)}, bf16[3,64,256]{2,1,0:T(8,128)(2,1)S(1)}, u32[]{:S(2)}, u32[]{:S(2)}) collective-permute-start(bf16[3,64,256]{2,1,0:T(8,128)(2,1)S(1)} %get-tuple-element.48), channel_id=1, source_target_pairs={{0,1},{1,0},{2,3},{3,2},{4,5},{5,4},{6,7},{7,6},{8,9},{9,8},{10,11... | collective-permute-start | bytes 294920 | tf_op jit(solution)/shard_map/ppermute | solution.py:324
  27.3 4.1 %collective-permute-done.8.refs_1_ = bf16[3,64,256]{2,1,0:T(8,128)(2,1)S(1)} collective-permute-done((bf16[3,64,256]{2,1,0:T(8,128)(2,1)S(1)}, bf16[3,64,256]{2,1,0:T(8,128)(2,1)S(1)}, u32[]{:S(2)}, u32[]{:S(2)}) %collective-permute-start.8) | collective-permute-done | bytes 98336 | tf_op jit(solution)/shard_map/ppermute | solution.py:324
  31.4 0.7 %gather.1 = bf16[128,512]{1,0:T(8,128)(2,1)} custom-call(bf16[3,64,256]{2,1,0:T(8,128)(2,1)S(1)} %get-tuple-element.47.refs_0_, bf16[3,64,256]{2,1,0:T(8,128)(2,1)S(1)} %collective-permute-done.8.refs_1_), custom_call_target="tpu_custom_call" | custom-call | tf_op jit(solution)/shard_map/gather/pallas_call | solution.py:300
  (1 shorter events, 0.0 us)
Async XLA Ops:
  0.0 2.2 %copy-start.1 = (bf16[1536,768]{1,0:T(8,128)(2,1)S(1)}, bf16[1536,768]{1,0:T(8,128)(2,1)}, u32[]{:S(2)}) copy-start(bf16[1536,768]{1,0:T(8,128)(2,1)} %features.1) | copy-start | bytes 7077892
  0.0 2.2 %copy-start.2 = (bf16[768,256]{1,0:T(8,128)(2,1)S(1)}, bf16[768,256]{1,0:T(8,128)(2,1)}, u32[]{:S(2)}) copy-start(bf16[768,256]{1,0:T(8,128)(2,1)} %projection.1) | copy-start | bytes 1179652
  0.0 2.2 %copy-start.3 = (s32[1536]{0:T(1024)S(1)}, s32[1536]{0:T(1024)}, u32[]{:S(2)}) copy-start(s32[1536]{0:T(1024)} %param.13) | copy-start | bytes 18436
  0.0 2.2 %copy-start.7 = (s32[1,2,2]{2,1,0:T(2,128)S(1)}, s32[1,2,2]{2,1,0:T(2,128)}, u32[]{:S(2)}) copy-start(s32[1,2,2]{2,1,0:T(2,128)} %send_ids.3) | copy-start | bytes 52
  0.0 2.2 %copy-start.6 = (s32[1,2,8]{2,1,0:T(2,128)S(1)}, s32[1,2,8]{2,1,0:T(2,128)}, u32[]{:S(2)}) copy-start(s32[1,2,8]{2,1,0:T(2,128)} %edge_ids.3) | copy-start | bytes 196
  2.1 8.5 %copy-start = (bf16[1536,512]{1,0:T(8,128)(2,1)S(1)}, bf16[1536,512]{1,0:T(8,128)(2,1)}, u32[]{:S(2)}) copy-start(bf16[1536,512]{1,0:T(8,128)(2,1)} %adjacency.5) | copy-start | bytes 4718596
  2.1 8.5 %copy-start.4 = (s32[12,4]{0,1:T(4,128)S(1)}, s32[12,4]{0,1:T(4,128)}, u32[]{:S(2)}) copy-start(s32[12,4]{0,1:T(4,128)} %param.14) | copy-start | bytes 580
  2.1 8.5 %copy-start.5 = (s32[1,2,64]{2,1,0:T(2,128)S(1)}, s32[1,2,64]{2,1,0:T(2,128)}, u32[]{:S(2)}) copy-start(s32[1,2,64]{2,1,0:T(2,128)} %train.3) | copy-start | bytes 1540
  2.9 11.2 %collective-permute-start.2 = (bf16[1024,256]{1,0:T(8,128)(2,1)S(1)}, bf16[1024,256]{1,0:T(8,128)(2,1)S(1)}, u32[]{:S(2)}, u32[]{:S(2)}) collective-permute-start(bf16[1024,256]{1,0:T(8,128)(2,1)S(1)} %get-tuple-element.30), channel_id=1, source_target_pairs={{0,2},{2,0},{4,6},{6,4},{8,10},{10,8},{12,14},{14,12},{16,18},{18,... | collective-permute-start | bytes 1572872 | tf_op jit(solution)/shard_map/ppermute | solution.py:348
  3.4 13.5 %collective-permute-start.1 = (bf16[1024,256]{1,0:T(8,128)(2,1)S(1)}, bf16[1024,256]{1,0:T(8,128)(2,1)S(1)}, u32[]{:S(2)}, u32[]{:S(2)}) collective-permute-start(bf16[1024,256]{1,0:T(8,128)(2,1)S(1)} %get-tuple-element.28), channel_id=1, source_target_pairs={{0,30},{2,4},{4,2},{6,8},{8,6},{10,12},{12,10},{14,16},{16,14},{18... | collective-permute-start | bytes 1572872 | tf_op jit(solution)/shard_map/ppermute | solution.py:346
  9.1 5.0 %collective-permute-start.3 = (bf16[256,256]{1,0:T(8,128)(2,1)S(1)}, bf16[256,256]{1,0:T(8,128)(2,1)S(1)}, u32[]{:S(2)}, u32[]{:S(2)}) collective-permute-start(bf16[256,256]{1,0:T(8,128)(2,1)S(1)} %get-tuple-element.31), channel_id=1, source_target_pairs={{0,1},{1,0},{2,3},{3,2},{4,5},{5,4},{6,7},{7,6},{8,9},{9,8},{10,11... | collective-permute-start | bytes 393224 | tf_op jit(solution)/shard_map/ppermute | solution.py:324
  11.5 7.4 %collective-permute-start = (bf16[272,256]{1,0:T(8,128)(2,1)S(1)}, bf16[272,256]{1,0:T(8,128)(2,1)S(1)}, u32[]{:S(2)}, u32[]{:S(2)}) collective-permute-start(bf16[272,256]{1,0:T(8,128)(2,1)S(1)} %ask.1.request), channel_id=1, source_target_pairs={{0,30},{2,4},{4,2},{6,8},{8,6},{10,12},{12,10},{14,16},{16,14},{18... | collective-permute-start | bytes 417800 | tf_op jit(solution)/shard_map/ppermute | solution.py:357
  15.3 3.6 %collective-permute-start.4 = (bf16[272,256]{1,0:T(8,128)(2,1)S(1)}, bf16[272,256]{1,0:T(8,128)(2,1)S(1)}, u32[]{:S(2)}, u32[]{:S(2)}) collective-permute-start(bf16[272,256]{1,0:T(8,128)(2,1)S(1)} %get-tuple-element.36), channel_id=1, source_target_pairs={{0,2},{2,0},{4,6},{6,4},{8,10},{10,8},{12,14},{14,12},{16,18},{18,... | collective-permute-start | bytes 417800 | tf_op jit(solution)/shard_map/ppermute | solution.py:380
  15.3 9.3 %collective-permute-start.7 = (bf16[272,256]{1,0:T(8,128)(2,1)S(1)}, bf16[272,256]{1,0:T(8,128)(2,1)S(1)}, u32[]{:S(2)}, u32[]{:S(2)}) collective-permute-start(bf16[272,256]{1,0:T(8,128)(2,1)S(1)} %get-tuple-element.36), channel_id=1, source_target_pairs={{0,1},{1,0},{2,3},{3,2},{4,5},{5,4},{6,7},{7,6},{8,9},{9,8},{10,11... | collective-permute-start | bytes 417800 | tf_op jit(solution)/shard_map/ppermute | solution.py:324
  19.4 6.5 %collective-permute-start.5 = (bf16[128,256]{1,0:T(8,128)(2,1)S(1)}, bf16[128,256]{1,0:T(8,128)(2,1)S(1)}, u32[]{:S(2)}, u32[]{:S(2)}) collective-permute-start(bf16[128,256]{1,0:T(8,128)(2,1)S(1)} %get-tuple-element.38), channel_id=1, source_target_pairs={{0,30},{2,4},{4,2},{6,8},{8,6},{10,12},{12,10},{14,16},{16,14},{18... | collective-permute-start | bytes 196616 | tf_op jit(solution)/shard_map/ppermute | solution.py:405
  22.6 3.2 %collective-permute-start.6 = (bf16[128,256]{1,0:T(8,128)(2,1)S(1)}, bf16[128,256]{1,0:T(8,128)(2,1)S(1)}, u32[]{:S(2)}, u32[]{:S(2)}) collective-permute-start(bf16[128,256]{1,0:T(8,128)(2,1)S(1)} %get-tuple-element.39), channel_id=1, source_target_pairs={{0,2},{2,0},{4,6},{6,4},{8,10},{10,8},{12,14},{14,12},{16,18},{18,... | collective-permute-start | bytes 196616 | tf_op jit(solution)/shard_map/ppermute | solution.py:406
  25.9 5.6 %collective-permute-start.8 = (bf16[3,64,256]{2,1,0:T(8,128)(2,1)S(1)}, bf16[3,64,256]{2,1,0:T(8,128)(2,1)S(1)}, u32[]{:S(2)}, u32[]{:S(2)}) collective-permute-start(bf16[3,64,256]{2,1,0:T(8,128)(2,1)S(1)} %get-tuple-element.48), channel_id=1, source_target_pairs={{0,1},{1,0},{2,3},{3,2},{4,5},{5,4},{6,7},{7,6},{8,9},{9,8},{10,11... | collective-permute-start | bytes 294920 | tf_op jit(solution)/shard_map/ppermute | solution.py:324

commit v6 on v5

--- a/solution.py
+++ b/solution.py
@@ -13,6 +13,8 @@
 CAPG = 8
 BF = jnp.bfloat16
 F32 = jnp.float32
+SHARE = 1.0 / TPB
+ON_PARTS = 2
 SPREAD_CHUNKS = 3
 
 
@@ -50,20 +52,20 @@
     return copies
 
 
-def fill_degrees(degrees, blocks):
-    degrees[pl.ds(blocks, 16 - blocks), :] = jnp.ones((16 - blocks, TILE), jnp.int32)
-
-
-def first_kernel(edge_ids, send_ids, degree, projection, features, head, first, off, on, *rest):
-    inner_out = rest[:-4]
+def fill_degrees(degree, degrees):
+    degrees[...] = jnp.ones_like(degrees)
+    degrees[pl.ds(0, degree.shape[0]), :] = degree[...]
+
+
+def first_kernel(edge_ids, send_ids, degree, projection, features, head, first, off, *rest):
+    on_parts, inner_out = rest[:ON_PARTS], rest[ON_PARTS:-4]
     edge_s, send_s, degrees, sems = rest[-4:]
     blocks = first.shape[0]
     owners = len(inner_out) + 1
     parity = lax.rem(lax.axis_index("group"), 2)
     mine = lax.axis_index("inner")
-    arriving = fetch([(edge_ids, edge_s), (send_ids, send_s), (degree, degrees.at[pl.ds(0, blocks)])], sems)
-    fill_degrees(degrees, blocks)
-    arriving[2].wait()
+    arriving = fetch([(edge_ids, edge_s), (send_ids, send_s)], sems)
+    fill_degrees(degree, degrees)
     roots = as_columns(lax.rsqrt(degrees[...].astype(F32)))
     done = head.shape[0] // TILE
     for b in range(done):
@@ -77,7 +79,8 @@
     arriving[1].wait()
     for s in range(CAPG):
         off[pl.ds(s * TILE, TILE), :] = first[edge_s[0, parity, s]]
-        on[pl.ds(s * TILE, TILE), :] = first[edge_s[0, 1 - parity, s]]
+        part, place = divmod(s, CAPG // ON_PARTS)
+        on_parts[part][pl.ds(place * TILE, TILE), :] = first[edge_s[0, 1 - parity, s]]
     for k in range(1, owners):
         peer = lax.rem(mine + k, owners)
         for s in range(CAP):
@@ -90,7 +93,7 @@
 
 
 def request_scale(request, count, width):
-    return lax.rsqrt(request_columns(request, count, width)[:, TPB : TPB + 1])
+    return TPB * TPB * lax.rsqrt(request_columns(request, count, width)[:, TPB : TPB + 1])
 
 
 def expanded(request, count, width, wanted):
@@ -99,7 +102,7 @@
     tiles = []
     for t in range(TPB):
         h, c = divmod(t * TILE, width)
-        tiles.append(request[pl.ds(h * count, count), c : c + TILE])
+        tiles.append(jnp.array(SHARE, BF) * request[pl.ds(h * count, count), c : c + TILE])
     nothing = jnp.zeros((), BF)
     parts = []
     for want in wanted:
@@ -108,22 +111,21 @@
     return parts
 
 
-def ask_kernel(tile_src, train, degree, after, adjacency, request, src_s, train_v, degrees, sems):
+def ask_kernel(tile_src, train, degree, after, adjacency, request, src_s, degrees, sem):
     blocks = degree.shape[0]
     owners = train.shape[1]
     count = owners * train.shape[2]
     width = request.shape[1]
-    arriving = fetch([(train, train_v), (tile_src, src_s), (degree, degrees.at[pl.ds(0, blocks)])], sems)
-    fill_degrees(degrees, blocks)
-    arriving[0].wait()
-    hot = jnp.concatenate(one_hot_parts(train_v, blocks), axis=1)
+    copy = pltpu.make_async_copy(tile_src, src_s, sem)
+    copy.start()
+    fill_degrees(degree, degrees)
+    hot = jnp.concatenate(one_hot_parts(train, blocks), axis=1)
     picked = jnp.dot(hot, adjacency[...], preferred_element_type=F32).astype(BF)
     strips = TPB * TILE // width
     for h in range(strips):
         request[pl.ds(h * count, count), :] = picked[:, h * width : (h + 1) * width]
-    arriving[1].wait()
-    arriving[2].wait()
-    row = ids_row(train_v)
+    copy.wait()
+    row = ids_row(train)
     block_of = lax.div(row, TILE)
     lane_hot = lax.broadcasted_iota(jnp.int32, (TILE, count), 0) == lax.rem(row, TILE)
     by_block = jnp.dot(
@@ -145,23 +147,24 @@
 
 
 def far_kernel(
-    tile_src, train, degree, adjacency, request, far, hot, roots, wide, ask, src_s, train_v, degrees, sems
+    tile_src, train, degree, adjacency, request, far, hot, roots, wide, ask, src_s, degrees, sem
 ):
     blocks = degree.shape[0]
     owners = train.shape[1]
     parity = lax.rem(lax.axis_index("group"), 2)
     off_base = blocks + owners * CAP + parity * CAPG
-    arriving = fetch([(train, train_v), (tile_src, src_s), (degree, degrees.at[pl.ds(0, blocks)])], sems)
-    fill_degrees(degrees, blocks)
+    copy = pltpu.make_async_copy(tile_src, src_s, sem)
+    copy.start()
+    fill_degrees(degree, degrees)
     far[...] = jnp.zeros_like(far)
+    share = jnp.array(SHARE, BF)
     count, width = hot.shape[0], request.shape[1]
     ask[...] = request[...]
     for b, part in enumerate(expanded(request, count, width, [float(b) for b in range(blocks)])):
         wide[:, b * TILE : (b + 1) * TILE] = part
-    for copy in arriving:
-        copy.wait()
+    copy.wait()
     roots[...] = as_columns(lax.rsqrt(degrees[...].astype(F32)))
-    for b, part in enumerate(one_hot_parts(train_v, blocks)):
+    for b, part in enumerate(one_hot_parts(train, blocks)):
         hot[:, b * TILE : (b + 1) * TILE] = part
     for b in range(blocks):
         for t in range(TPB):
@@ -170,10 +173,11 @@
             @pl.when(jnp.logical_and(slot >= 0, slot < CAPG))
             def _():
                 place = (pl.ds(b * TILE, TILE), pl.ds(pl.multiple_of(slot * TILE, TILE), TILE))
-                far[place] += adjacency[pl.ds(b * TILE, TILE), t * TILE : (t + 1) * TILE]
-
-
-def near_kernel(tile_src, first, adjacency, request, on, *rest):
+                far[place] += share * adjacency[pl.ds(b * TILE, TILE), t * TILE : (t + 1) * TILE]
+
+
+def near_kernel(tile_src, first, adjacency, request, *rest):
+    on, rest = rest[:ON_PARTS], rest[ON_PARTS:]
     owners = len(rest) - 4
     inner_in = rest[: owners - 1]
     sums, ask, src_s, table, sems = rest[owners - 1 :]
@@ -185,7 +189,7 @@
     ask[...] = request[...]
     for s in range(CAPG):
         table[group_base + parity * CAPG + s] = jnp.zeros((TILE, width), BF)
-        table[group_base + (1 - parity) * CAPG + s] = on[pl.ds(s * TILE, TILE), :]
+        table[group_base + (1 - parity) * CAPG + s] = on[s // (CAPG // ON_PARTS)][pl.ds(s % (CAPG // ON_PARTS) * TILE, TILE), :]
     for s in range(CAP):
         table[blocks + mine * CAP + s] = jnp.zeros((TILE, width), BF)
         for k in range(1, owners):
@@ -195,9 +199,8 @@
         copy.wait()
     for b in range(blocks):
         fetched = jnp.concatenate([table[src_s[t, b]] for t in range(TPB)], axis=0)
-        sums[pl.ds(b * TILE, TILE), :] = jnp.dot(
-            adjacency[pl.ds(b * TILE, TILE), :], fetched, preferred_element_type=F32
-        )
+        total = jnp.dot(adjacency[pl.ds(b * TILE, TILE), :], fetched, preferred_element_type=F32)
+        sums[pl.ds(b * TILE, TILE), :] = SHARE * total
 
 
 def spread_kernel(edge_ids, off, sums, far, roots, second, hop, offered, offered_on, edge_s, sem):
@@ -236,7 +239,7 @@
     copy.start()
     total = jnp.dot(wide[...], second[...], preferred_element_type=F32)
     own[...] = request_scale(request, count, width) * total
-    picked[...] = jnp.dot(hot[...], hop[...], preferred_element_type=F32).astype(BF)
+    picked[...] = (TPB * jnp.dot(hot[...], hop[...], preferred_element_type=F32)).astype(BF)
     copy.wait()
     for k in range(1, owners):
         peer = lax.rem(mine - k + owners, owners)
@@ -329,37 +332,38 @@
     def smem(like):
         return pltpu.SMEM(like.shape, jnp.int32)
 
-    train_scratch = pltpu.VMEM(train_ids.shape, jnp.int32)
     degree_scratch = pltpu.VMEM((16, TILE), jnp.int32)
     dma = pltpu.SemaphoreType.DMA
 
     head = jnp.dot(features[: blocks * 7 // 12 * TILE], projection, preferred_element_type=F32)
-    first, off, on, *inner_out = call(
+    first, off, *outgoing = call(
         first_kernel,
         "first",
         (edge_ids, send_ids, degree, projection, features, head),
-        [HBM] * 3 + [VMEM] * 3,
-        [array(blocks, TILE, width), array(CAPG * TILE, width), array(CAPG * TILE, width)]
+        [HBM] * 2 + [VMEM] * 4,
+        [array(blocks, TILE, width), array(CAPG * TILE, width)]
+        + [array(CAPG // ON_PARTS * TILE, width)] * ON_PARTS
         + [array(CAP * TILE, width)] * (owners - 1),
-        [smem(edge_ids), smem(send_ids), degree_scratch, dma((3,))],
-    )
+        [smem(edge_ids), smem(send_ids), degree_scratch, dma((2,))],
+    )
+    on, inner_out = outgoing[:ON_PARTS], outgoing[ON_PARTS:]
     off_in = lax.ppermute(off, "group", across)
     inner_in = [around(inner_out[k - 1], k) for k in range(1, owners)]
-    on_in = lax.ppermute(on, "group", beside)
+    on_in = [lax.ppermute(part, "group", beside) for part in on]
     (request,) = call(
         ask_kernel,
         "ask",
         (tile_src, train_ids, degree, first, adjacency),
-        [HBM] * 3 + [ANY, VMEM],
+        [HBM] + [VMEM] * 2 + [ANY, VMEM],
         [array(tail, width)],
-        [smem(tile_src), train_scratch, degree_scratch, dma((3,))],
+        [smem(tile_src), degree_scratch, dma],
     )
     asked_off = lax.ppermute(request, "group", across)
     far, hot, roots, wide, ask = call(
         far_kernel,
         "far",
         (tile_src, train_ids, degree, adjacency, request),
-        [HBM] * 3 + [VMEM] * 2,
+        [HBM] + [VMEM] * 4,
         [
             array(row_count, CAPG * TILE),
             array(count, row_count),
@@ -367,13 +371,13 @@
             array(count, row_count),
             array(tail, width),
         ],
-        [smem(tile_src), train_scratch, degree_scratch, dma((3,))],
+        [smem(tile_src), degree_scratch, dma],
     )
     sums, ask = call(
         near_kernel,
         "near",
-        (tile_src, first, adjacency, ask, on_in, *inner_in),
-        [HBM] * 2 + [VMEM] * (2 + owners),
+        (tile_src, first, adjacency, ask, *on_in, *inner_in),
+        [HBM] * 2 + [VMEM] * (1 + ON_PARTS + owners),
         [array(row_count, width, kind=F32), array(tail, width)],
         [smem(tile_src), pltpu.VMEM((blocks + owners * CAP + 2 * CAPG, TILE, width), BF), dma((2,))],
     )

time: 32.2 us -> 32.3 us (level)
    ppermute x1, starting transfers between devices: 2.05 us -> 2.65 us  [on_device(): on_part = lax.ppermute(to_on, 'group', beside)]
    ppermute x1, starting transfers between devices: 3.26 us -> 2.78 us  [on_device(): off_part = lax.ppermute(to_off, 'group', across)]
    ppermute x1, waiting for transfers between devices: 0.81 us -> 0.34 us  [on_device(): asked_off = lax.ppermute(request, 'group', across)]
    ppermute x3, waiting for transfers between devices: 5.22 us -> 5.58 us  [around(): lax.ppermute(value, 'inner', [(i, (i + k) % owners) for i in range(owners)])]
  transfers between devices with their start and end apart: 9 -> 10, of which waited for: 4 -> 3; matrix products, arithmetic and copies ran while one was open for 0% -> 0% of each run, Pallas kernels for 19% -> 19%
where the time goes in v6:
time: 32.3 us; the launch traced here: 32.1 us
  starting transfers between devices  16.3 us (50%)
  Pallas kernels  7.53 us (23%)
  waiting for transfers between devices  5.94 us (18%)
  matrix products  2.08 us (6%)
    pallas_call x9, Pallas kernels, call(): pl.pallas_call(kernel, out_shape=outputs, in_specs=specs, out_specs=[VMEM...  7.53 us
    ppermute x3, waiting for transfers between devices, around(): lax.ppermute(value, 'inner', [(i, (i + k) % owners) for i in range(owners)])  5.58 us
    ppermute x1, starting transfers between devices, on_device(): off_in = lax.ppermute(off, 'group', across)  5.51 us
    ppermute x3, starting transfers between devices, around(): lax.ppermute(value, 'inner', [(i, (i + k) % owners) for i in range(owners)])  4.6 us
    ppermute x1, starting transfers between devices, on_device(): off_part = lax.ppermute(to_off, 'group', across)  2.78 us
    ppermute x1, starting transfers between devices, on_device(): on_part = lax.ppermute(to_on, 'group', beside)  2.65 us
    dot_general x1, matrix products, on_device(): jnp.dot(features[:blocks * 7 // 12 * TILE], projection, preferred_element...  2.08 us
  transfers between devices with their start and end apart: 10, of which 3 were waited for; matrix products, arithmetic and copies ran while one was open for 0% of the time, Pallas kernels for 19%

profile of v6, /device:TPU:0, one launch (start us, length us, event | category | flops | bytes accessed | tf_op | source)
XLA Modules:
  0.0 32.1 jit_solution(1706410882901048470)
XLA Ops:
  0.0 0.0 copy-start.1
  0.0 0.0 copy-start.2
  0.0 0.0 copy-start.3
  0.0 0.0 copy-start.7
  0.0 0.0 copy-start.6
  0.0 2.1 %fusion.head = f32[896,256]{1,0:T(8,128)S(1)} fusion(bf16[768,256]{1,0:T(8,128)(2,1)} %projection.1, bf16[1536,768]{1,0:T(8,128)(2,1)} %features.1), kind=kOutput, calls=%fused_computation | convolution fusion | flops 352321536 | bytes 2686976 | tf_op jit(solution)/shard_map/dot_general | solution.py:338
  2.1 0.0 copy-start
  2.1 0.0 copy-start.4
  2.1 0.0 copy-start.5
  2.1 0.1 copy-done.1
  2.2 0.0 copy-done.2
  2.2 0.0 copy-done.3
  2.2 0.0 copy-done.7
  2.2 0.0 copy-done.6
  2.2 0.8 %first.1 = (bf16[12,128,256]{2,1,0:T(8,128)(2,1)S(1)}, bf16[1024,256]{1,0:T(8,128)(2,1)S(1)}, bf16[512,256]{1,0:T(8,128)(2,1)S(1)}, bf16[512,256]{1,0:T(8,128)(2,1)S(1)}, bf16[256,256]{1,0:T(8,128)(2,1)S(1)}) custom-call(s32[1,2,8]{2,1,0:T(2,128)S(1)} %copy-done.6, s32[1,2,2]{2,1,0:T(2,128)S(1)} %copy-done.7, s32[12,128]{1,0:T(8,128)S(1)} %bitcast.3, ...), custom_call_target="tpu_custom_call" | custom-call | tf_op jit(solution)/shard_map/first/pallas_call | solution.py:303
  3.0 5.5 %collective-permute-start.1 = (bf16[1024,256]{1,0:T(8,128)(2,1)S(1)}, bf16[1024,256]{1,0:T(8,128)(2,1)S(1)}, u32[]{:S(2)}, u32[]{:S(2)}) collective-permute-start(bf16[1024,256]{1,0:T(8,128)(2,1)S(1)} %get-tuple-element.29), channel_id=1, source_target_pairs={{0,30},{2,4},{4,2},{6,8},{8,6},{10,12},{12,10},{14,16},{16,14},{18... | collective-permute-start | bytes 1572872 | tf_op jit(solution)/shard_map/ppermute | solution.py:350
  8.5 0.0 collective-permute-start.2
  8.5 0.5 %collective-permute-start.3 = (bf16[512,256]{1,0:T(8,128)(2,1)S(1)}, bf16[512,256]{1,0:T(8,128)(2,1)S(1)}, u32[]{:S(2)}, u32[]{:S(2)}) collective-permute-start(bf16[512,256]{1,0:T(8,128)(2,1)S(1)} %get-tuple-element.32), channel_id=1, source_target_pairs={{0,2},{2,0},{4,6},{6,4},{8,10},{10,8},{12,14},{14,12},{16,18},{18,... | collective-permute-start | bytes 786440 | tf_op jit(solution)/shard_map/ppermute | solution.py:352
  9.0 1.5 %collective-permute-start.4 = (bf16[256,256]{1,0:T(8,128)(2,1)S(1)}, bf16[256,256]{1,0:T(8,128)(2,1)S(1)}, u32[]{:S(2)}, u32[]{:S(2)}) collective-permute-start(bf16[256,256]{1,0:T(8,128)(2,1)S(1)} %get-tuple-element.33), channel_id=1, source_target_pairs={{0,1},{1,0},{2,3},{3,2},{4,5},{5,4},{6,7},{7,6},{8,9},{9,8},{10,11... | collective-permute-start | bytes 393224 | tf_op jit(solution)/shard_map/ppermute | solution.py:327
  10.5 0.0 copy-done
  10.5 0.0 copy-done.4
  10.5 0.0 copy-done.5
  10.5 0.8 %ask.1.request = bf16[272,256]{1,0:T(8,128)(2,1)S(1)} custom-call(s32[4,12]{1,0:T(4,128)S(1)} %bitcast.6, s32[1,2,64]{2,1,0:T(2,128)S(1)} %copy-done.5, s32[12,128]{1,0:T(8,128)S(1)} %bitcast.4, bf16[12,128,256]{2,1,0:T(8,128)(2,1)S(1)} %get-tuple-element.28.after.first, bf16[1536,512]{1,0:T(8,128)(2,1)S(1)} %copy-done), custom_call_target="tpu_custom_call" | custom-call | tf_op jit(solution)/shard_map/ask/pallas_call | solution.py:303
  11.4 0.2 collective-permute-start
  11.6 1.4 %far.1 = (bf16[1536,1024]{1,0:T(8,128)(2,1)S(1)}, bf16[128,1536]{1,0:T(8,128)(2,1)S(1)}, f32[128,16]{1,0:T(8,128)S(1)}, bf16[128,1536]{1,0:T(8,128)(2,1)S(1)}, bf16[272,256]{1,0:T(8,128)(2,1)S(1)}) custom-call(s32[4,12]{1,0:T(4,128)S(1)} %bitcast.7, s32[1,2,64]{2,1,0:T(2,128)S(1)} %copy-done.5, s32[12,128]{1,0:T(8,128)S(1)} %bitcast.5, ...), custom_call_target="tpu_custom_call" | custom-call | tf_op jit(solution)/shard_map/far/pallas_call | solution.py:303
  13.0 1.5 %collective-permute-done.4.rest_2_ = bf16[256,256]{1,0:T(8,128)(2,1)S(1)} collective-permute-done((bf16[256,256]{1,0:T(8,128)(2,1)S(1)}, bf16[256,256]{1,0:T(8,128)(2,1)S(1)}, u32[]{:S(2)}, u32[]{:S(2)}) %collective-permute-start.4) | collective-permute-done | bytes 131104 | tf_op jit(solution)/shard_map/ppermute | solution.py:327
  14.4 0.0 collective-permute-done.2.rest_0_
  14.5 0.0 collective-permute-done.3.rest_1_
  14.5 1.2 %near.1 = (f32[1536,256]{1,0:T(8,128)S(1)}, bf16[272,256]{1,0:T(8,128)(2,1)S(1)}) custom-call(s32[4,12]{1,0:T(4,128)S(1)} %bitcast.8, bf16[12,128,256]{2,1,0:T(8,128)(2,1)S(1)} %get-tuple-element.28.after.first, bf16[1536,512]{1,0:T(8,128)(2,1)S(1)} %copy-done, bf16[272,256]{1,0:T(8,128)(2,1)S(1)} %get-tuple-element.30.request, ...), custom_call_target="tpu_custom_call" | custom-call | tf_op jit(solution)/shard_map/near/pallas_call | solution.py:303
  15.6 0.1 collective-permute-start.5
  15.7 1.6 %collective-permute-start.8 = (bf16[272,256]{1,0:T(8,128)(2,1)S(1)}, bf16[272,256]{1,0:T(8,128)(2,1)S(1)}, u32[]{:S(2)}, u32[]{:S(2)}) collective-permute-start(bf16[272,256]{1,0:T(8,128)(2,1)S(1)} %get-tuple-element.38), channel_id=1, source_target_pairs={{0,1},{1,0},{2,3},{3,2},{4,5},{5,4},{6,7},{7,6},{8,9},{9,8},{10,11... | collective-permute-start | bytes 417800 | tf_op jit(solution)/shard_map/ppermute | solution.py:327
  17.3 0.0 collective-permute-done.1.off
  17.3 1.1 %spread.1 = (bf16[1536,256]{1,0:T(8,128)(2,1)S(1)}, bf16[1536,256]{1,0:T(8,128)(2,1)S(1)}, bf16[1024,256]{1,0:T(8,128)(2,1)S(1)}, bf16[1024,256]{1,0:T(8,128)(2,1)S(1)}) custom-call(s32[1,2,8]{2,1,0:T(2,128)S(1)} %copy-done.6, bf16[1024,256]{1,0:T(8,128)(2,1)S(1)} %collective-permute-done.1.off, f32[1536,256]{1,0:T(8,128)S(1)} %get-tuple-element.34.sums, ...), custom_call_target="tpu_custom_call" | custom-call | tf_op jit(solution)/shard_map/spread/pallas_call | solution.py:303
  18.4 0.3 %collective-permute-done.off = bf16[272,256]{1,0:T(8,128)(2,1)S(1)} collective-permute-done((bf16[272,256]{1,0:T(8,128)(2,1)S(1)}, bf16[272,256]{1,0:T(8,128)(2,1)S(1)}, u32[]{:S(2)}, u32[]{:S(2)}) %collective-permute-start) | collective-permute-done | bytes 139296 | tf_op jit(solution)/shard_map/ppermute | solution.py:361
  18.7 0.0 collective-permute-done.5.on
  18.7 0.6 %answer.1 = (bf16[128,256]{1,0:T(8,128)(2,1)S(1)}, bf16[128,256]{1,0:T(8,128)(2,1)S(1)}) custom-call(bf16[272,256]{1,0:T(8,128)(2,1)S(1)} %collective-permute-done.off, bf16[1024,256]{1,0:T(8,128)(2,1)S(1)} %get-tuple-element.37.offered, bf16[272,256]{1,0:T(8,128)(2,1)S(1)} %collective-permute-done.5.on, bf16[1024,256]{1,0:T(8,128)(2,1)S(1)} %get-tuple-element.39.offered_on), custom_call_target="tpu_custom_call" | custom-call | tf_op jit(solution)/shard_map/answer/pallas_call | solution.py:303
  19.3 2.8 %collective-permute-start.6 = (bf16[128,256]{1,0:T(8,128)(2,1)S(1)}, bf16[128,256]{1,0:T(8,128)(2,1)S(1)}, u32[]{:S(2)}, u32[]{:S(2)}) collective-permute-start(bf16[128,256]{1,0:T(8,128)(2,1)S(1)} %get-tuple-element.40), channel_id=1, source_target_pairs={{0,30},{2,4},{4,2},{6,8},{8,6},{10,12},{12,10},{14,16},{16,14},{18... | collective-permute-start | bytes 196616 | tf_op jit(solution)/shard_map/ppermute | solution.py:409
  22.1 2.6 %collective-permute-start.7 = (bf16[128,256]{1,0:T(8,128)(2,1)S(1)}, bf16[128,256]{1,0:T(8,128)(2,1)S(1)}, u32[]{:S(2)}, u32[]{:S(2)}) collective-permute-start(bf16[128,256]{1,0:T(8,128)(2,1)S(1)} %get-tuple-element.41), channel_id=1, source_target_pairs={{0,2},{2,0},{4,6},{6,4},{8,10},{10,8},{12,14},{14,12},{16,18},{18,... | collective-permute-start | bytes 196616 | tf_op jit(solution)/shard_map/ppermute | solution.py:410
  24.7 0.0 collective-permute-done.8.rest_0_
  24.7 1.0 %rest.1 = (f32[128,256]{1,0:T(8,128)S(1)}, bf16[128,256]{1,0:T(8,128)(2,1)S(1)}, bf16[128,256]{1,0:T(8,128)(2,1)S(1)}) custom-call(s32[1,2,2]{2,1,0:T(2,128)S(1)} %copy-done.7, bf16[1536,256]{1,0:T(8,128)(2,1)S(1)} %get-tuple-element.42.second, bf16[1536,256]{1,0:T(8,128)(2,1)S(1)} %get-tuple-element.43.hop, bf16[128,1536]{1,0:T(8,128)(2,1)S(1)} %get-tuple-element.44.hot, ...), custom_call_target="tpu_custom_call" | custom-call | tf_op jit(solution)/shard_map/rest/pallas_call | solution.py:303
  25.8 0.0 collective-permute-done.6.off
  25.8 0.0 collective-permute-done.7.on
  25.8 1.6 %collective-permute-start.9 = (bf16[3,64,256]{2,1,0:T(8,128)(2,1)S(1)}, bf16[3,64,256]{2,1,0:T(8,128)(2,1)S(1)}, u32[]{:S(2)}, u32[]{:S(2)}) collective-permute-start(bf16[3,64,256]{2,1,0:T(8,128)(2,1)S(1)} %get-tuple-element.50), channel_id=1, source_target_pairs={{0,1},{1,0},{2,3},{3,2},{4,5},{5,4},{6,7},{7,6},{8,9},{9,8},{10,11... | collective-permute-start | bytes 294920 | tf_op jit(solution)/shard_map/ppermute | solution.py:327
  27.4 4.1 %collective-permute-done.9.refs_1_ = bf16[3,64,256]{2,1,0:T(8,128)(2,1)S(1)} collective-permute-done((bf16[3,64,256]{2,1,0:T(8,128)(2,1)S(1)}, bf16[3,64,256]{2,1,0:T(8,128)(2,1)S(1)}, u32[]{:S(2)}, u32[]{:S(2)}) %collective-permute-start.9) | collective-permute-done | bytes 98336 | tf_op jit(solution)/shard_map/ppermute | solution.py:327
  31.5 0.7 %gather.1 = bf16[128,512]{1,0:T(8,128)(2,1)} custom-call(bf16[3,64,256]{2,1,0:T(8,128)(2,1)S(1)} %get-tuple-element.49.refs_0_, bf16[3,64,256]{2,1,0:T(8,128)(2,1)S(1)} %collective-permute-done.9.refs_1_), custom_call_target="tpu_custom_call" | custom-call | tf_op jit(solution)/shard_map/gather/pallas_call | solution.py:303
  (1 shorter events, 0.0 us)
Async XLA Ops:
  0.0 2.2 %copy-start.1 = (bf16[1536,768]{1,0:T(8,128)(2,1)S(1)}, bf16[1536,768]{1,0:T(8,128)(2,1)}, u32[]{:S(2)}) copy-start(bf16[1536,768]{1,0:T(8,128)(2,1)} %features.1) | copy-start | bytes 7077892
  0.0 2.2 %copy-start.2 = (bf16[768,256]{1,0:T(8,128)(2,1)S(1)}, bf16[768,256]{1,0:T(8,128)(2,1)}, u32[]{:S(2)}) copy-start(bf16[768,256]{1,0:T(8,128)(2,1)} %projection.1) | copy-start | bytes 1179652
  0.0 2.2 %copy-start.3 = (s32[1536]{0:T(1024)S(1)}, s32[1536]{0:T(1024)}, u32[]{:S(2)}) copy-start(s32[1536]{0:T(1024)} %param.13) | copy-start | bytes 18436
  0.0 2.2 %copy-start.7 = (s32[1,2,2]{2,1,0:T(2,128)S(1)}, s32[1,2,2]{2,1,0:T(2,128)}, u32[]{:S(2)}) copy-start(s32[1,2,2]{2,1,0:T(2,128)} %send_ids.3) | copy-start | bytes 52
  0.0 2.2 %copy-start.6 = (s32[1,2,8]{2,1,0:T(2,128)S(1)}, s32[1,2,8]{2,1,0:T(2,128)}, u32[]{:S(2)}) copy-start(s32[1,2,8]{2,1,0:T(2,128)} %edge_ids.3) | copy-start | bytes 196
  2.1 8.4 %copy-start = (bf16[1536,512]{1,0:T(8,128)(2,1)S(1)}, bf16[1536,512]{1,0:T(8,128)(2,1)}, u32[]{:S(2)}) copy-start(bf16[1536,512]{1,0:T(8,128)(2,1)} %adjacency.5) | copy-start | bytes 4718596
  2.1 8.4 %copy-start.4 = (s32[12,4]{0,1:T(4,128)S(1)}, s32[12,4]{0,1:T(4,128)}, u32[]{:S(2)}) copy-start(s32[12,4]{0,1:T(4,128)} %param.14) | copy-start | bytes 580
  2.1 8.4 %copy-start.5 = (s32[1,2,64]{2,1,0:T(2,128)S(1)}, s32[1,2,64]{2,1,0:T(2,128)}, u32[]{:S(2)}) copy-start(s32[1,2,64]{2,1,0:T(2,128)} %train.3) | copy-start | bytes 1540
  3.0 14.2 %collective-permute-start.1 = (bf16[1024,256]{1,0:T(8,128)(2,1)S(1)}, bf16[1024,256]{1,0:T(8,128)(2,1)S(1)}, u32[]{:S(2)}, u32[]{:S(2)}) collective-permute-start(bf16[1024,256]{1,0:T(8,128)(2,1)S(1)} %get-tuple-element.29), channel_id=1, source_target_pairs={{0,30},{2,4},{4,2},{6,8},{8,6},{10,12},{12,10},{14,16},{16,14},{18... | collective-permute-start | bytes 1572872 | tf_op jit(solution)/shard_map/ppermute | solution.py:350
  8.5 5.9 %collective-permute-start.2 = (bf16[512,256]{1,0:T(8,128)(2,1)S(1)}, bf16[512,256]{1,0:T(8,128)(2,1)S(1)}, u32[]{:S(2)}, u32[]{:S(2)}) collective-permute-start(bf16[512,256]{1,0:T(8,128)(2,1)S(1)} %get-tuple-element.31), channel_id=1, source_target_pairs={{0,2},{2,0},{4,6},{6,4},{8,10},{10,8},{12,14},{14,12},{16,18},{18,... | collective-permute-start | bytes 786440 | tf_op jit(solution)/shard_map/ppermute | solution.py:352
  8.5 5.9 %collective-permute-start.3 = (bf16[512,256]{1,0:T(8,128)(2,1)S(1)}, bf16[512,256]{1,0:T(8,128)(2,1)S(1)}, u32[]{:S(2)}, u32[]{:S(2)}) collective-permute-start(bf16[512,256]{1,0:T(8,128)(2,1)S(1)} %get-tuple-element.32), channel_id=1, source_target_pairs={{0,2},{2,0},{4,6},{6,4},{8,10},{10,8},{12,14},{14,12},{16,18},{18,... | collective-permute-start | bytes 786440 | tf_op jit(solution)/shard_map/ppermute | solution.py:352
  9.0 5.4 %collective-permute-start.4 = (bf16[256,256]{1,0:T(8,128)(2,1)S(1)}, bf16[256,256]{1,0:T(8,128)(2,1)S(1)}, u32[]{:S(2)}, u32[]{:S(2)}) collective-permute-start(bf16[256,256]{1,0:T(8,128)(2,1)S(1)} %get-tuple-element.33), channel_id=1, source_target_pairs={{0,1},{1,0},{2,3},{3,2},{4,5},{5,4},{6,7},{7,6},{8,9},{9,8},{10,11... | collective-permute-start | bytes 393224 | tf_op jit(solution)/shard_map/ppermute | solution.py:327
  11.4 7.3 %collective-permute-start = (bf16[272,256]{1,0:T(8,128)(2,1)S(1)}, bf16[272,256]{1,0:T(8,128)(2,1)S(1)}, u32[]{:S(2)}, u32[]{:S(2)}) collective-permute-start(bf16[272,256]{1,0:T(8,128)(2,1)S(1)} %ask.1.request), channel_id=1, source_target_pairs={{0,30},{2,4},{4,2},{6,8},{8,6},{10,12},{12,10},{14,16},{16,14},{18... | collective-permute-start | bytes 417800 | tf_op jit(solution)/shard_map/ppermute | solution.py:361
  15.6 3.1 %collective-permute-start.5 = (bf16[272,256]{1,0:T(8,128)(2,1)S(1)}, bf16[272,256]{1,0:T(8,128)(2,1)S(1)}, u32[]{:S(2)}, u32[]{:S(2)}) collective-permute-start(bf16[272,256]{1,0:T(8,128)(2,1)S(1)} %get-tuple-element.38), channel_id=1, source_target_pairs={{0,2},{2,0},{4,6},{6,4},{8,10},{10,8},{12,14},{14,12},{16,18},{18,... | collective-permute-start | bytes 417800 | tf_op jit(solution)/shard_map/ppermute | solution.py:384
  15.7 9.0 %collective-permute-start.8 = (bf16[272,256]{1,0:T(8,128)(2,1)S(1)}, bf16[272,256]{1,0:T(8,128)(2,1)S(1)}, u32[]{:S(2)}, u32[]{:S(2)}) collective-permute-start(bf16[272,256]{1,0:T(8,128)(2,1)S(1)} %get-tuple-element.38), channel_id=1, source_target_pairs={{0,1},{1,0},{2,3},{3,2},{4,5},{5,4},{6,7},{7,6},{8,9},{9,8},{10,11... | collective-permute-start | bytes 417800 | tf_op jit(solution)/shard_map/ppermute | solution.py:327
  19.3 6.5 %collective-permute-start.6 = (bf16[128,256]{1,0:T(8,128)(2,1)S(1)}, bf16[128,256]{1,0:T(8,128)(2,1)S(1)}, u32[]{:S(2)}, u32[]{:S(2)}) collective-permute-start(bf16[128,256]{1,0:T(8,128)(2,1)S(1)} %get-tuple-element.40), channel_id=1, source_target_pairs={{0,30},{2,4},{4,2},{6,8},{8,6},{10,12},{12,10},{14,16},{16,14},{18... | collective-permute-start | bytes 196616 | tf_op jit(solution)/shard_map/ppermute | solution.py:409
  22.1 3.7 %collective-permute-start.7 = (bf16[128,256]{1,0:T(8,128)(2,1)S(1)}, bf16[128,256]{1,0:T(8,128)(2,1)S(1)}, u32[]{:S(2)}, u32[]{:S(2)}) collective-permute-start(bf16[128,256]{1,0:T(8,128)(2,1)S(1)} %get-tuple-element.41), channel_id=1, source_target_pairs={{0,2},{2,0},{4,6},{6,4},{8,10},{10,8},{12,14},{14,12},{16,18},{18,... | collective-permute-start | bytes 196616 | tf_op jit(solution)/shard_map/ppermute | solution.py:410
  25.8 5.6 %collective-permute-start.9 = (bf16[3,64,256]{2,1,0:T(8,128)(2,1)S(1)}, bf16[3,64,256]{2,1,0:T(8,128)(2,1)S(1)}, u32[]{:S(2)}, u32[]{:S(2)}) collective-permute-start(bf16[3,64,256]{2,1,0:T(8,128)(2,1)S(1)} %get-tuple-element.50), channel_id=1, source_target_pairs={{0,1},{1,0},{2,3},{3,2},{4,5},{5,4},{6,7},{7,6},{8,9},{9,8},{10,11... | collective-permute-start | bytes 294920 | tf_op jit(solution)/shard_map/ppermute | solution.py:327

commit v7 on v6

--- a/solution.py
+++ b/solution.py
@@ -14,7 +14,7 @@
 BF = jnp.bfloat16
 F32 = jnp.float32
 SHARE = 1.0 / TPB
-ON_PARTS = 2
+ON_PARTS = 1
 SPREAD_CHUNKS = 3
 
 

time: 32.3 us -> 32.3 us (level)
    ppermute x1, starting transfers between devices: 2.65 us -> 2.05 us  [on_device(): on_part = lax.ppermute(to_on, 'group', beside)]
    ppermute x1, starting transfers between devices: 2.78 us -> 3.29 us  [on_device(): off_part = lax.ppermute(to_off, 'group', across)]
    ppermute x1, waiting for transfers between devices: 0.34 us -> 0.78 us  [on_device(): asked_off = lax.ppermute(request, 'group', across)]
  transfers between devices with their start and end apart: 10 -> 9, of which waited for: 3 -> 4; matrix products, arithmetic and copies ran while one was open for 0% -> 0% of each run, Pallas kernels for 19% -> 19%
where the time goes in v7:
time: 32.3 us; the launch traced here: 32.1 us
  starting transfers between devices  16.2 us (50%)
  Pallas kernels  7.42 us (23%)
  waiting for transfers between devices  6.16 us (19%)
  matrix products  2.08 us (6%)
    pallas_call x9, Pallas kernels, call(): pl.pallas_call(kernel, out_shape=outputs, in_specs=specs, out_specs=[VMEM...  7.42 us
    ppermute x1, starting transfers between devices, on_device(): off_in = lax.ppermute(off, 'group', across)  5.67 us
    ppermute x3, waiting for transfers between devices, around(): lax.ppermute(value, 'inner', [(i, (i + k) % owners) for i in range(owners)])  5.29 us
    ppermute x3, starting transfers between devices, around(): lax.ppermute(value, 'inner', [(i, (i + k) % owners) for i in range(owners)])  4.56 us
    ppermute x1, starting transfers between devices, on_device(): off_part = lax.ppermute(to_off, 'group', across)  3.29 us
    dot_general x1, matrix products, on_device(): jnp.dot(features[:blocks * 7 // 12 * TILE], projection, preferred_element...  2.08 us
    ppermute x1, starting transfers between devices, on_device(): on_part = lax.ppermute(to_on, 'group', beside)  2.05 us
    ppermute x1, waiting for transfers between devices, on_device(): asked_off = lax.ppermute(request, 'group', across)  0.78 us
  transfers between devices with their start and end apart: 9, of which 4 were waited for; matrix products, arithmetic and copies ran while one was open for 0% of the time, Pallas kernels for 19%

profile of v7, /device:TPU:0, one launch (start us, length us, event | category | flops | bytes accessed | tf_op | source)
XLA Modules:
  0.0 32.1 jit_solution(12203326830899140210)
XLA Ops:
  0.0 0.0 copy-start.1
  0.0 0.0 copy-start.2
  0.0 0.0 copy-start.3
  0.0 0.0 copy-start.7
  0.0 0.0 copy-start.6
  0.0 2.1 %fusion.head = f32[896,256]{1,0:T(8,128)S(1)} fusion(bf16[768,256]{1,0:T(8,128)(2,1)} %projection.1, bf16[1536,768]{1,0:T(8,128)(2,1)} %features.1), kind=kOutput, calls=%fused_computation | convolution fusion | flops 352321536 | bytes 2686976 | tf_op jit(solution)/shard_map/dot_general | solution.py:338
  2.1 0.0 copy-start
  2.1 0.0 copy-start.4
  2.1 0.0 copy-start.5
  2.1 0.1 copy-done.1
  2.2 0.0 copy-done.2
  2.2 0.0 copy-done.3
  2.2 0.0 copy-done.7
  2.2 0.0 copy-done.6
  2.2 0.7 %first.1 = (bf16[12,128,256]{2,1,0:T(8,128)(2,1)S(1)}, bf16[1024,256]{1,0:T(8,128)(2,1)S(1)}, bf16[1024,256]{1,0:T(8,128)(2,1)S(1)}, bf16[256,256]{1,0:T(8,128)(2,1)S(1)}) custom-call(s32[1,2,8]{2,1,0:T(2,128)S(1)} %copy-done.6, s32[1,2,2]{2,1,0:T(2,128)S(1)} %copy-done.7, s32[12,128]{1,0:T(8,128)S(1)} %bitcast.3, bf16[768,256]{1,0:T(8,128)(2,1)S(1)} %copy-done.2, ...), custom_call_target="tpu_custom_call" | custom-call | tf_op jit(solution)/shard_map/first/pallas_call | solution.py:303
  2.9 0.5 %collective-permute-start.2 = (bf16[1024,256]{1,0:T(8,128)(2,1)S(1)}, bf16[1024,256]{1,0:T(8,128)(2,1)S(1)}, u32[]{:S(2)}, u32[]{:S(2)}) collective-permute-start(bf16[1024,256]{1,0:T(8,128)(2,1)S(1)} %get-tuple-element.30), channel_id=1, source_target_pairs={{0,2},{2,0},{4,6},{6,4},{8,10},{10,8},{12,14},{14,12},{16,18},{18,... | collective-permute-start | bytes 1572872 | tf_op jit(solution)/shard_map/ppermute | solution.py:352
  3.4 5.7 %collective-permute-start.1 = (bf16[1024,256]{1,0:T(8,128)(2,1)S(1)}, bf16[1024,256]{1,0:T(8,128)(2,1)S(1)}, u32[]{:S(2)}, u32[]{:S(2)}) collective-permute-start(bf16[1024,256]{1,0:T(8,128)(2,1)S(1)} %get-tuple-element.28), channel_id=1, source_target_pairs={{0,30},{2,4},{4,2},{6,8},{8,6},{10,12},{12,10},{14,16},{16,14},{18... | collective-permute-start | bytes 1572872 | tf_op jit(solution)/shard_map/ppermute | solution.py:350
  9.1 1.5 %collective-permute-start.3 = (bf16[256,256]{1,0:T(8,128)(2,1)S(1)}, bf16[256,256]{1,0:T(8,128)(2,1)S(1)}, u32[]{:S(2)}, u32[]{:S(2)}) collective-permute-start(bf16[256,256]{1,0:T(8,128)(2,1)S(1)} %get-tuple-element.31), channel_id=1, source_target_pairs={{0,1},{1,0},{2,3},{3,2},{4,5},{5,4},{6,7},{7,6},{8,9},{9,8},{10,11... | collective-permute-start | bytes 393224 | tf_op jit(solution)/shard_map/ppermute | solution.py:327
  10.6 0.0 copy-done
  10.6 0.0 copy-done.4
  10.6 0.0 copy-done.5
  10.6 0.8 %ask.1.request = bf16[272,256]{1,0:T(8,128)(2,1)S(1)} custom-call(s32[4,12]{1,0:T(4,128)S(1)} %bitcast.6, s32[1,2,64]{2,1,0:T(2,128)S(1)} %copy-done.5, s32[12,128]{1,0:T(8,128)S(1)} %bitcast.4, bf16[12,128,256]{2,1,0:T(8,128)(2,1)S(1)} %get-tuple-element.27.after.first, bf16[1536,512]{1,0:T(8,128)(2,1)S(1)} %copy-done), custom_call_target="tpu_custom_call" | custom-call | tf_op jit(solution)/shard_map/ask/pallas_call | solution.py:303
  11.4 0.1 collective-permute-start
  11.5 1.4 %far.1 = (bf16[1536,1024]{1,0:T(8,128)(2,1)S(1)}, bf16[128,1536]{1,0:T(8,128)(2,1)S(1)}, f32[128,16]{1,0:T(8,128)S(1)}, bf16[128,1536]{1,0:T(8,128)(2,1)S(1)}, bf16[272,256]{1,0:T(8,128)(2,1)S(1)}) custom-call(s32[4,12]{1,0:T(4,128)S(1)} %bitcast.7, s32[1,2,64]{2,1,0:T(2,128)S(1)} %copy-done.5, s32[12,128]{1,0:T(8,128)S(1)} %bitcast.5, ...), custom_call_target="tpu_custom_call" | custom-call | tf_op jit(solution)/shard_map/far/pallas_call | solution.py:303
  12.9 1.2 %collective-permute-done.3.rest_1_ = bf16[256,256]{1,0:T(8,128)(2,1)S(1)} collective-permute-done((bf16[256,256]{1,0:T(8,128)(2,1)S(1)}, bf16[256,256]{1,0:T(8,128)(2,1)S(1)}, u32[]{:S(2)}, u32[]{:S(2)}) %collective-permute-start.3) | collective-permute-done | bytes 131104 | tf_op jit(solution)/shard_map/ppermute | solution.py:327
  14.1 0.0 collective-permute-done.2.rest_0_
  14.1 1.2 %near.1 = (f32[1536,256]{1,0:T(8,128)S(1)}, bf16[272,256]{1,0:T(8,128)(2,1)S(1)}) custom-call(s32[4,12]{1,0:T(4,128)S(1)} %bitcast.8, bf16[12,128,256]{2,1,0:T(8,128)(2,1)S(1)} %get-tuple-element.27.after.first, bf16[1536,512]{1,0:T(8,128)(2,1)S(1)} %copy-done, bf16[272,256]{1,0:T(8,128)(2,1)S(1)} %get-tuple-element.29.request, ...), custom_call_target="tpu_custom_call" | custom-call | tf_op jit(solution)/shard_map/near/pallas_call | solution.py:303
  15.3 0.1 collective-permute-start.4
  15.3 1.6 %collective-permute-start.7 = (bf16[272,256]{1,0:T(8,128)(2,1)S(1)}, bf16[272,256]{1,0:T(8,128)(2,1)S(1)}, u32[]{:S(2)}, u32[]{:S(2)}) collective-permute-start(bf16[272,256]{1,0:T(8,128)(2,1)S(1)} %get-tuple-element.36), channel_id=1, source_target_pairs={{0,1},{1,0},{2,3},{3,2},{4,5},{5,4},{6,7},{7,6},{8,9},{9,8},{10,11... | collective-permute-start | bytes 417800 | tf_op jit(solution)/shard_map/ppermute | solution.py:327
  16.9 0.0 collective-permute-done.1.off
  16.9 1.1 %spread.1 = (bf16[1536,256]{1,0:T(8,128)(2,1)S(1)}, bf16[1536,256]{1,0:T(8,128)(2,1)S(1)}, bf16[1024,256]{1,0:T(8,128)(2,1)S(1)}, bf16[1024,256]{1,0:T(8,128)(2,1)S(1)}) custom-call(s32[1,2,8]{2,1,0:T(2,128)S(1)} %copy-done.6, bf16[1024,256]{1,0:T(8,128)(2,1)S(1)} %collective-permute-done.1.off, f32[1536,256]{1,0:T(8,128)S(1)} %get-tuple-element.32.sums, ...), custom_call_target="tpu_custom_call" | custom-call | tf_op jit(solution)/shard_map/spread/pallas_call | solution.py:303
  18.0 0.8 %collective-permute-done.off = bf16[272,256]{1,0:T(8,128)(2,1)S(1)} collective-permute-done((bf16[272,256]{1,0:T(8,128)(2,1)S(1)}, bf16[272,256]{1,0:T(8,128)(2,1)S(1)}, u32[]{:S(2)}, u32[]{:S(2)}) %collective-permute-start) | collective-permute-done | bytes 139296 | tf_op jit(solution)/shard_map/ppermute | solution.py:361
  18.8 0.0 collective-permute-done.4.on
  18.8 0.6 %answer.1 = (bf16[128,256]{1,0:T(8,128)(2,1)S(1)}, bf16[128,256]{1,0:T(8,128)(2,1)S(1)}) custom-call(bf16[272,256]{1,0:T(8,128)(2,1)S(1)} %collective-permute-done.off, bf16[1024,256]{1,0:T(8,128)(2,1)S(1)} %get-tuple-element.35.offered, bf16[272,256]{1,0:T(8,128)(2,1)S(1)} %collective-permute-done.4.on, bf16[1024,256]{1,0:T(8,128)(2,1)S(1)} %get-tuple-element.37.offered_on), custom_call_target="tpu_custom_call" | custom-call | tf_op jit(solution)/shard_map/answer/pallas_call | solution.py:303
  19.4 3.3 %collective-permute-start.5 = (bf16[128,256]{1,0:T(8,128)(2,1)S(1)}, bf16[128,256]{1,0:T(8,128)(2,1)S(1)}, u32[]{:S(2)}, u32[]{:S(2)}) collective-permute-start(bf16[128,256]{1,0:T(8,128)(2,1)S(1)} %get-tuple-element.38), channel_id=1, source_target_pairs={{0,30},{2,4},{4,2},{6,8},{8,6},{10,12},{12,10},{14,16},{16,14},{18... | collective-permute-start | bytes 196616 | tf_op jit(solution)/shard_map/ppermute | solution.py:409
  22.7 2.1 %collective-permute-start.6 = (bf16[128,256]{1,0:T(8,128)(2,1)S(1)}, bf16[128,256]{1,0:T(8,128)(2,1)S(1)}, u32[]{:S(2)}, u32[]{:S(2)}) collective-permute-start(bf16[128,256]{1,0:T(8,128)(2,1)S(1)} %get-tuple-element.39), channel_id=1, source_target_pairs={{0,2},{2,0},{4,6},{6,4},{8,10},{10,8},{12,14},{14,12},{16,18},{18,... | collective-permute-start | bytes 196616 | tf_op jit(solution)/shard_map/ppermute | solution.py:410
  24.7 0.0 collective-permute-done.7.rest_0_
  24.7 1.0 %rest.1 = (f32[128,256]{1,0:T(8,128)S(1)}, bf16[128,256]{1,0:T(8,128)(2,1)S(1)}, bf16[128,256]{1,0:T(8,128)(2,1)S(1)}) custom-call(s32[1,2,2]{2,1,0:T(2,128)S(1)} %copy-done.7, bf16[1536,256]{1,0:T(8,128)(2,1)S(1)} %get-tuple-element.40.second, bf16[1536,256]{1,0:T(8,128)(2,1)S(1)} %get-tuple-element.41.hop, bf16[128,1536]{1,0:T(8,128)(2,1)S(1)} %get-tuple-element.42.hot, ...), custom_call_target="tpu_custom_call" | custom-call | tf_op jit(solution)/shard_map/rest/pallas_call | solution.py:303
  25.8 0.1 collective-permute-done.5.off
  25.8 0.0 collective-permute-done.6.on
  25.9 1.5 %collective-permute-start.8 = (bf16[3,64,256]{2,1,0:T(8,128)(2,1)S(1)}, bf16[3,64,256]{2,1,0:T(8,128)(2,1)S(1)}, u32[]{:S(2)}, u32[]{:S(2)}) collective-permute-start(bf16[3,64,256]{2,1,0:T(8,128)(2,1)S(1)} %get-tuple-element.48), channel_id=1, source_target_pairs={{0,1},{1,0},{2,3},{3,2},{4,5},{5,4},{6,7},{7,6},{8,9},{9,8},{10,11... | collective-permute-start | bytes 294920 | tf_op jit(solution)/shard_map/ppermute | solution.py:327
  27.4 4.1 %collective-permute-done.8.refs_1_ = bf16[3,64,256]{2,1,0:T(8,128)(2,1)S(1)} collective-permute-done((bf16[3,64,256]{2,1,0:T(8,128)(2,1)S(1)}, bf16[3,64,256]{2,1,0:T(8,128)(2,1)S(1)}, u32[]{:S(2)}, u32[]{:S(2)}) %collective-permute-start.8) | collective-permute-done | bytes 98336 | tf_op jit(solution)/shard_map/ppermute | solution.py:327
  31.5 0.7 %gather.1 = bf16[128,512]{1,0:T(8,128)(2,1)} custom-call(bf16[3,64,256]{2,1,0:T(8,128)(2,1)S(1)} %get-tuple-element.47.refs_0_, bf16[3,64,256]{2,1,0:T(8,128)(2,1)S(1)} %collective-permute-done.8.refs_1_), custom_call_target="tpu_custom_call" | custom-call | tf_op jit(solution)/shard_map/gather/pallas_call | solution.py:303
  (1 shorter events, 0.0 us)
Async XLA Ops:
  0.0 2.2 %copy-start.1 = (bf16[1536,768]{1,0:T(8,128)(2,1)S(1)}, bf16[1536,768]{1,0:T(8,128)(2,1)}, u32[]{:S(2)}) copy-start(bf16[1536,768]{1,0:T(8,128)(2,1)} %features.1) | copy-start | bytes 7077892
  0.0 2.2 %copy-start.2 = (bf16[768,256]{1,0:T(8,128)(2,1)S(1)}, bf16[768,256]{1,0:T(8,128)(2,1)}, u32[]{:S(2)}) copy-start(bf16[768,256]{1,0:T(8,128)(2,1)} %projection.1) | copy-start | bytes 1179652
  0.0 2.2 %copy-start.3 = (s32[1536]{0:T(1024)S(1)}, s32[1536]{0:T(1024)}, u32[]{:S(2)}) copy-start(s32[1536]{0:T(1024)} %param.13) | copy-start | bytes 18436
  0.0 2.2 %copy-start.7 = (s32[1,2,2]{2,1,0:T(2,128)S(1)}, s32[1,2,2]{2,1,0:T(2,128)}, u32[]{:S(2)}) copy-start(s32[1,2,2]{2,1,0:T(2,128)} %send_ids.3) | copy-start | bytes 52
  0.0 2.2 %copy-start.6 = (s32[1,2,8]{2,1,0:T(2,128)S(1)}, s32[1,2,8]{2,1,0:T(2,128)}, u32[]{:S(2)}) copy-start(s32[1,2,8]{2,1,0:T(2,128)} %edge_ids.3) | copy-start | bytes 196
  2.1 8.5 %copy-start = (bf16[1536,512]{1,0:T(8,128)(2,1)S(1)}, bf16[1536,512]{1,0:T(8,128)(2,1)}, u32[]{:S(2)}) copy-start(bf16[1536,512]{1,0:T(8,128)(2,1)} %adjacency.5) | copy-start | bytes 4718596
  2.1 8.5 %copy-start.4 = (s32[12,4]{0,1:T(4,128)S(1)}, s32[12,4]{0,1:T(4,128)}, u32[]{:S(2)}) copy-start(s32[12,4]{0,1:T(4,128)} %param.14) | copy-start | bytes 580
  2.1 8.5 %copy-start.5 = (s32[1,2,64]{2,1,0:T(2,128)S(1)}, s32[1,2,64]{2,1,0:T(2,128)}, u32[]{:S(2)}) copy-start(s32[1,2,64]{2,1,0:T(2,128)} %train.3) | copy-start | bytes 1540
  2.9 11.2 %collective-permute-start.2 = (bf16[1024,256]{1,0:T(8,128)(2,1)S(1)}, bf16[1024,256]{1,0:T(8,128)(2,1)S(1)}, u32[]{:S(2)}, u32[]{:S(2)}) collective-permute-start(bf16[1024,256]{1,0:T(8,128)(2,1)S(1)} %get-tuple-element.30), channel_id=1, source_target_pairs={{0,2},{2,0},{4,6},{6,4},{8,10},{10,8},{12,14},{14,12},{16,18},{18,... | collective-permute-start | bytes 1572872 | tf_op jit(solution)/shard_map/ppermute | solution.py:352
  3.4 13.5 %collective-permute-start.1 = (bf16[1024,256]{1,0:T(8,128)(2,1)S(1)}, bf16[1024,256]{1,0:T(8,128)(2,1)S(1)}, u32[]{:S(2)}, u32[]{:S(2)}) collective-permute-start(bf16[1024,256]{1,0:T(8,128)(2,1)S(1)} %get-tuple-element.28), channel_id=1, source_target_pairs={{0,30},{2,4},{4,2},{6,8},{8,6},{10,12},{12,10},{14,16},{16,14},{18... | collective-permute-start | bytes 1572872 | tf_op jit(solution)/shard_map/ppermute | solution.py:350
  9.1 5.0 %collective-permute-start.3 = (bf16[256,256]{1,0:T(8,128)(2,1)S(1)}, bf16[256,256]{1,0:T(8,128)(2,1)S(1)}, u32[]{:S(2)}, u32[]{:S(2)}) collective-permute-start(bf16[256,256]{1,0:T(8,128)(2,1)S(1)} %get-tuple-element.31), channel_id=1, source_target_pairs={{0,1},{1,0},{2,3},{3,2},{4,5},{5,4},{6,7},{7,6},{8,9},{9,8},{10,11... | collective-permute-start | bytes 393224 | tf_op jit(solution)/shard_map/ppermute | solution.py:327
  11.4 7.4 %collective-permute-start = (bf16[272,256]{1,0:T(8,128)(2,1)S(1)}, bf16[272,256]{1,0:T(8,128)(2,1)S(1)}, u32[]{:S(2)}, u32[]{:S(2)}) collective-permute-start(bf16[272,256]{1,0:T(8,128)(2,1)S(1)} %ask.1.request), channel_id=1, source_target_pairs={{0,30},{2,4},{4,2},{6,8},{8,6},{10,12},{12,10},{14,16},{16,14},{18... | collective-permute-start | bytes 417800 | tf_op jit(solution)/shard_map/ppermute | solution.py:361
  15.3 3.5 %collective-permute-start.4 = (bf16[272,256]{1,0:T(8,128)(2,1)S(1)}, bf16[272,256]{1,0:T(8,128)(2,1)S(1)}, u32[]{:S(2)}, u32[]{:S(2)}) collective-permute-start(bf16[272,256]{1,0:T(8,128)(2,1)S(1)} %get-tuple-element.36), channel_id=1, source_target_pairs={{0,2},{2,0},{4,6},{6,4},{8,10},{10,8},{12,14},{14,12},{16,18},{18,... | collective-permute-start | bytes 417800 | tf_op jit(solution)/shard_map/ppermute | solution.py:384
  15.3 9.4 %collective-permute-start.7 = (bf16[272,256]{1,0:T(8,128)(2,1)S(1)}, bf16[272,256]{1,0:T(8,128)(2,1)S(1)}, u32[]{:S(2)}, u32[]{:S(2)}) collective-permute-start(bf16[272,256]{1,0:T(8,128)(2,1)S(1)} %get-tuple-element.36), channel_id=1, source_target_pairs={{0,1},{1,0},{2,3},{3,2},{4,5},{5,4},{6,7},{7,6},{8,9},{9,8},{10,11... | collective-permute-start | bytes 417800 | tf_op jit(solution)/shard_map/ppermute | solution.py:327
  19.4 6.5 %collective-permute-start.5 = (bf16[128,256]{1,0:T(8,128)(2,1)S(1)}, bf16[128,256]{1,0:T(8,128)(2,1)S(1)}, u32[]{:S(2)}, u32[]{:S(2)}) collective-permute-start(bf16[128,256]{1,0:T(8,128)(2,1)S(1)} %get-tuple-element.38), channel_id=1, source_target_pairs={{0,30},{2,4},{4,2},{6,8},{8,6},{10,12},{12,10},{14,16},{16,14},{18... | collective-permute-start | bytes 196616 | tf_op jit(solution)/shard_map/ppermute | solution.py:409
  22.7 3.2 %collective-permute-start.6 = (bf16[128,256]{1,0:T(8,128)(2,1)S(1)}, bf16[128,256]{1,0:T(8,128)(2,1)S(1)}, u32[]{:S(2)}, u32[]{:S(2)}) collective-permute-start(bf16[128,256]{1,0:T(8,128)(2,1)S(1)} %get-tuple-element.39), channel_id=1, source_target_pairs={{0,2},{2,0},{4,6},{6,4},{8,10},{10,8},{12,14},{14,12},{16,18},{18,... | collective-permute-start | bytes 196616 | tf_op jit(solution)/shard_map/ppermute | solution.py:410
  25.9 5.6 %collective-permute-start.8 = (bf16[3,64,256]{2,1,0:T(8,128)(2,1)S(1)}, bf16[3,64,256]{2,1,0:T(8,128)(2,1)S(1)}, u32[]{:S(2)}, u32[]{:S(2)}) collective-permute-start(bf16[3,64,256]{2,1,0:T(8,128)(2,1)S(1)} %get-tuple-element.48), channel_id=1, source_target_pairs={{0,1},{1,0},{2,3},{3,2},{4,5},{5,4},{6,7},{7,6},{8,9},{9,8},{10,11... | collective-permute-start | bytes 294920 | tf_op jit(solution)/shard_map/ppermute | solution.py:327
